TPU v7x, 512 devices: a whole 4x8x8 slice. The times are simulated.
512 devices in a mesh: member: 16 (over z_hi, x), band: 32 (over z_lo, y, core).
Axes of the slice: x: 4, y: 8, z: 8 (z_hi: 4, z_lo: 2; z = z_hi * 2 + z_lo), core: 2. Of those that a mesh axis runs over, the one named last changes fastest.
Arguments:
- queries: bfloat16 [131072, 1024], P(('member', 'band')), parts along dimension 0, may hold values from -5 to 5
- keys: bfloat16 [131072, 1024], P(('member', 'band')), parts along dimension 0, may hold values from -5 to 5
- values: bfloat16 [131072, 1024], P(('member', 'band')), parts along dimension 0, may hold values from -5 to 5
- out_grad: bfloat16 [131072, 1024], P(('member', 'band')), parts along dimension 0, may hold values from -5 to 5
- band_counts: int32 [512], P(('member', 'band')), parts along dimension 0, may hold values from 192 to 256, as said below
- block_lists: int32 [4096, 14], P(('member', 'band')), parts along dimension 0, may hold values from 0 to 19, as said below
- slot_counts: int32 [4096], P(('member', 'band')), parts along dimension 0, may hold values from 7 to 14, as said below
Outputs:
- query_grad: bfloat16 [131072, 1024], P(('member', 'band')), parts along dimension 0
- key_grad: bfloat16 [131072, 1024], P(('member', 'band')), parts along dimension 0
- value_grad: bfloat16 [131072, 1024], P(('member', 'band')), parts along dimension 0
There are 16 independent parts, one for each index of `member`. A program takes and returns all parts, laid end to end along the dimension named above; each array names one. Nothing has to cross between parts.
Inputs may be any that keep to these rules, and one draw needn't show every extreme that they name: `band_counts`: a band's valid tokens are its first rows; every band has at least the 192 rows that neighbours read, the middle band all of its rows, the first band exactly 192. `block_lists`: entry (b * 8 + n, l) names a frame block of band b: 0 to 7 the band's own blocks, 8 + r block r of band b - 1, 14 + r block r of band b + 1; slot 0 names block n itself; the live slots are distinct and never name a band below the first or above the last; slots past the live ones may name any frame block. `slot_counts`: some block of every band other than the first and last has all 14 slots live.
All inputs are finite; a program needn't handle non-finite values.
Results may differ from a plain program's by a relative error of at most 0.0093.
Values may be sent and summed in bfloat16 or wider, within the bound.
No kernel may reach another device: no remote copies, remote signals or barrier semaphores. Data moves between devices by JAX's collectives and lax.ppermute only.
A program may use at most 64 MiB of HBM per device.

v0:
```python
import jax
import jax.numpy as jnp
from jax import lax
from jax.sharding import PartitionSpec as P

HEADS = 8
BLK = 32
RB = 6


def padded(cells, sides, width):
    for axis, dim in sides:
        count = lax.axis_size(axis)
        ends = count - 1
        head = lax.slice_in_dim(cells, 0, width, axis=dim)
        tail = lax.slice_in_dim(cells, cells.shape[dim] - width, cells.shape[dim], axis=dim)
        cells = jnp.concatenate(
            [
                lax.ppermute(tail, axis, [(i, (i + 1) % count) for i in range(ends)]),
                cells,
                lax.ppermute(head, axis, [((i + 1) % count, i) for i in range(ends)]),
            ],
            axis=dim,
        )
    return cells


def shifted(x, axis, by):
    length = lax.axis_size(axis)
    pairs = [(i, i + by) for i in range(length) if 0 <= i + by < length]
    return lax.ppermute(x, axis, pairs)


def head_grads(q_head, g_head, k_frame, v_frame, allowed, scale):
    score = jnp.dot(q_head, k_frame.T, preferred_element_type=jnp.float32) * scale
    masked = jnp.where(allowed, score, -1e30)
    top = jnp.max(masked, axis=-1, keepdims=True)
    total = jnp.sum(jnp.where(allowed, jnp.exp(masked - top), 0.0), axis=-1, keepdims=True)
    total = total + jnp.where(jnp.any(allowed, axis=-1, keepdims=True), 0.0, 1.0)
    lse = top + jnp.log(total)
    weight = jnp.where(allowed, jnp.exp(masked - lse), 0.0)
    weight_b = weight.astype(jnp.bfloat16)
    attended = jnp.dot(weight_b, v_frame, preferred_element_type=jnp.float32)
    delta = jnp.sum(g_head.astype(jnp.float32) * attended, axis=-1)
    product = jnp.dot(g_head, v_frame.T, preferred_element_type=jnp.float32)
    score_grad = (scale * weight * (product - delta[:, None])).astype(jnp.bfloat16)
    grad_q = jnp.dot(score_grad, k_frame, preferred_element_type=jnp.float32)
    grad_k = jnp.dot(score_grad.T, q_head, preferred_element_type=jnp.float32)
    grad_v = jnp.dot(weight_b.T, g_head, preferred_element_type=jnp.float32)
    return (grad_q, grad_k, grad_v, lse[:, 0], delta)


def on_device(queries, keys, values, out_grad, band_counts, block_lists, slot_counts):
    tok, width = queries.shape
    heads = HEADS
    depth = width // heads
    blk = BLK
    blocks = tok // blk
    rim = RB * blk
    frame_blocks = blocks + 2 * RB
    slots = block_lists.shape[1]
    scale = depth ** (-0.5)
    count = band_counts[0]

    def by_head(array):
        return array.reshape(array.shape[0], heads, depth).transpose(1, 0, 2)

    edges = jnp.stack([keys[:rim], values[:rim]])
    widened = padded(edges, (("band", 1),), rim)
    frame_k = jnp.concatenate([keys, widened[0, :rim], widened[0, 2 * rim :]], axis=0)
    frame_v = jnp.concatenate([values, widened[1, :rim], widened[1, 2 * rim :]], axis=0)
    rows = jnp.arange(frame_blocks * blk, dtype=jnp.int32)
    key_valid = ((rows < count) | (rows >= tok)).reshape(frame_blocks, blk)
    slot_live = jnp.arange(slots, dtype=jnp.int32)[None, :] < slot_counts[:, None]
    frame_ids = jnp.arange(frame_blocks, dtype=jnp.int32)
    block_hit = jnp.any((block_lists[:, :, None] == frame_ids) & slot_live[:, :, None], axis=1)
    key_mask = (block_hit[:, :, None] & key_valid[None]).reshape(blocks, frame_blocks * blk)
    query_mask = jnp.arange(tok, dtype=jnp.int32).reshape(blocks, blk) < count
    allowed = (query_mask[:, :, None] & key_mask[:, None, :]).reshape(tok, frame_blocks * blk)

    def head_step(carry, inputs):
        q_head, g_head, k_head, v_head = inputs
        return (carry, head_grads(q_head, g_head, k_head, v_head, allowed, scale))

    inputs = (by_head(queries), by_head(out_grad), by_head(frame_k), by_head(frame_v))
    _, (grad_q, frame_gk, frame_gv, lse, delta) = lax.scan(head_step, 0, inputs)
    grad_q = grad_q.transpose(1, 0, 2).reshape(tok, width)
    frame_gk = frame_gk.transpose(1, 0, 2).reshape(frame_blocks * blk, width)
    frame_gv = frame_gv.transpose(1, 0, 2).reshape(frame_blocks * blk, width)
    lower_part = jnp.stack([frame_gk[tok : tok + rim], frame_gv[tok : tok + rim]])
    upper_part = jnp.stack([frame_gk[tok + rim :], frame_gv[tok + rim :]])
    from_above = shifted(lower_part, "band", -1)
    from_below = shifted(upper_part, "band", 1)
    lead_k = from_above[0] + from_below[0]
    lead_v = from_above[1] + from_below[1]
    key_grad = jnp.concatenate([frame_gk[:rim] + lead_k, frame_gk[rim:tok]], axis=0)
    value_grad = jnp.concatenate([frame_gv[:rim] + lead_v, frame_gv[rim:tok]], axis=0)
    return (
        grad_q.astype(jnp.bfloat16),
        key_grad.astype(jnp.bfloat16),
        value_grad.astype(jnp.bfloat16),
    )


def solution(mesh):
    placed = (
        P(("member", "band"), None),
        P(("member", "band"), None),
        P(("member", "band"), None),
        P(("member", "band"), None),
        P(("member", "band")),
        P(("member", "band"), None),
        P(("member", "band")),
    )
    return jax.shard_map(
        on_device,
        mesh=mesh,
        in_specs=placed,
        out_specs=(
            P(("member", "band"), None),
            P(("member", "band"), None),
            P(("member", "band"), None),
        ),
        check_vma=False,
    )
```

profile of v0, /device:TPU:454, one launch (start us, length us, event | category | flops | bytes accessed | tf_op | source)
XLA Modules:
  0.0 118.2 jit_solution(10859515635989319510)
XLA Ops:
  0.7 1.3 %slice_bitcast_fusion.2 = (bf16[1,192,1024]{2,1,0:T(8,128)(2,1)S(1)}, bf16[1,192,1024]{2,1,0:T(8,128)(2,1)S(1)}) fusion(bf16[256,1024]{1,0:T(8,128)(2,1)} %param.11, bf16[256,1024]{1,0:T(8,128)(2,1)} %param.10), kind=kLoop, calls=%fused_computation.61 | loop fusion | bytes 1572864 | tf_op jit(solution)/shard_map/stack | solution.py:68
  2.1 4.9 %collective-permute-start.1 = (bf16[2,192,1024]{2,1,0:T(8,128)(2,1)S(1)}, bf16[2,192,1024]{2,1,0:T(8,128)(2,1)}, u32[]{:S(2)}, u32[]{:S(2)}) collective-permute-start(bf16[2,192,1024]{2,1,0:T(8,128)(2,1)S(1)} %pad_maximum_fusion.2), channel_id=1, source_target_pairs={{1,0},{2,1},{3,2},{4,3},{5,4},{6,5},{7,6},{8,7},{9,8},{10,9},{11,1... | collective-permute-start | bytes 2359304 | tf_op jit(solution)/shard_map/ppermute | solution.py:21
  7.0 1.9 %collective-permute-start = (bf16[2,192,1024]{2,1,0:T(8,128)(2,1)S(1)}, bf16[2,192,1024]{2,1,0:T(8,128)(2,1)}, u32[]{:S(2)}, u32[]{:S(2)}) collective-permute-start(bf16[2,192,1024]{2,1,0:T(8,128)(2,1)S(1)} %pad_maximum_fusion.2), channel_id=1, source_target_pairs={{0,1},{1,2},{2,3},{3,4},{4,5},{5,6},{6,7},{7,8},{8,9},{9,10},{10,1... | collective-permute-start | bytes 2359304 | tf_op jit(solution)/shard_map/ppermute | solution.py:19
  8.9 1.0 copy.41
  11.9 1.0 copy.40
  13.1 3.4 %collective-permute-done.1 = bf16[2,192,1024]{2,1,0:T(8,128)(2,1)} collective-permute-done((bf16[2,192,1024]{2,1,0:T(8,128)(2,1)S(1)}, bf16[2,192,1024]{2,1,0:T(8,128)(2,1)}, u32[]{:S(2)}, u32[]{:S(2)}) %collective-permute-start.1) | collective-permute-done | bytes 786464 | tf_op jit(solution)/shard_map/ppermute | solution.py:21
  16.5 1.2 fusion.46
  17.9 1.0 copy.62
  18.9 3.7 %collective-permute-done = bf16[2,192,1024]{2,1,0:T(8,128)(2,1)} collective-permute-done((bf16[2,192,1024]{2,1,0:T(8,128)(2,1)S(1)}, bf16[2,192,1024]{2,1,0:T(8,128)(2,1)}, u32[]{:S(2)}, u32[]{:S(2)}) %collective-permute-start) | collective-permute-done | bytes 786464 | tf_op jit(solution)/shard_map/ppermute | solution.py:19
  22.5 1.2 fusion.45
  23.9 1.0 copy.61
  25.3 0.7 copy-done.6
  26.0 1.5 %maximum_bitcast_fusion = bf16[8,640,128]{1,2,0:T(8,128)(2,1)S(1)} fusion(bf16[192,8,128]{0,2,1:T(8,128)(2,1)} %bitcast.160, bf16[192,8,128]{0,2,1:T(8,128)(2,1)S(1)} %bitcast.162, bf16[256,8,128]{0,2,1:T(8,128)(2,1)} %bitcast.164), kind=kLoop, calls=%fused_computation.43 | loop fusion | flops 3932160 | bytes 2621440 | tf_op jit(solution)/shard_map/transpose | solution.py:66
  27.5 50.7 %while.16 = (s32[]{:T(128)}, bf16[8,256,128]{2,1,0:T(8,128)(2,1)}, f32[8,640,128]{2,1,0:T(8,128)}, f32[8,640,128]{2,1,0:T(8,128)}, bf16[8,256,128]{1,2,0:T(8,128...) while((s32[]{:T(128)}, bf16[8,256,128]{2,1,0:T(8,128)(2,1)}, ...), condition=%wide.region_6.7_spmd.clone, body=%wide.region_2.6_spmd.clone.sunk | while | flops 254705664 | bytes 6881405 | solution.py:86
  27.7 1.2 %fusion.81 = (f32[256]{0:T(256)S(1)}, f32[256,640]{1,0:T(8,128)S(1)}) fusion(pred[256,640]{1,0:T(32,128)(4,1)S(1)} %bitcast_and_fusion.2, bf16[8,640,128]{1,2,0:T(8,128)(2,1)S(1)} %get-tuple-element.282, s32[]{:T(128)S(6)} %copy.85, bf16[8,256,128]{1,2,0:T(8,128)(2,1)} %get-tuple-element.281), kind=kOutput, calls=%fused_computation.79.clone.1 | convolution fusion | flops 42434304 | bytes 1050624 | tf_op jit(solution)/shard_map/while/body/eval_jaxpr/dot_general | solution.py:35
  30.1 0.9 fusion.85
  31.0 1.9 %fusion.86 = f32[8,640,128]{2,1,0:T(8,128)} fusion(f32[8,640,128]{2,1,0:T(8,128)} %get-tuple-element.267, s32[]{:T(128)S(6)} %copy.85, bf16[256,640]{1,0:T(8,128)(2,1)S(1)} %fusion.84, bf16[8,256,128]{1,2,0:T(8,128)(2,1)} %get-tuple-element.281), kind=kOutput, calls=%fused_computation.9.clone.1 | convolution fusion | flops 41943040 | bytes 721920 | tf_op jit(solution)/shard_map/while/body/eval_jaxpr/dot_general | solution.py:48
  32.8 1.0 fusion.87
  34.0 1.2 %fusion.81 = (f32[256]{0:T(256)S(1)}, f32[256,640]{1,0:T(8,128)S(1)}) fusion(pred[256,640]{1,0:T(32,128)(4,1)S(1)} %bitcast_and_fusion.2, bf16[8,640,128]{1,2,0:T(8,128)(2,1)S(1)} %get-tuple-element.282, s32[]{:T(128)S(6)} %copy.85, bf16[8,256,128]{1,2,0:T(8,128)(2,1)} %get-tuple-element.281), kind=kOutput, calls=%fused_computation.79.clone.1 | convolution fusion | flops 42434304 | bytes 1050624 | tf_op jit(solution)/shard_map/while/body/eval_jaxpr/dot_general | solution.py:35
  36.4 0.9 fusion.85
  37.3 1.9 %fusion.86 = f32[8,640,128]{2,1,0:T(8,128)} fusion(f32[8,640,128]{2,1,0:T(8,128)} %get-tuple-element.267, s32[]{:T(128)S(6)} %copy.85, bf16[256,640]{1,0:T(8,128)(2,1)S(1)} %fusion.84, bf16[8,256,128]{1,2,0:T(8,128)(2,1)} %get-tuple-element.281), kind=kOutput, calls=%fused_computation.9.clone.1 | convolution fusion | flops 41943040 | bytes 721920 | tf_op jit(solution)/shard_map/while/body/eval_jaxpr/dot_general | solution.py:48
  39.2 1.0 fusion.87
  40.4 1.2 %fusion.81 = (f32[256]{0:T(256)S(1)}, f32[256,640]{1,0:T(8,128)S(1)}) fusion(pred[256,640]{1,0:T(32,128)(4,1)S(1)} %bitcast_and_fusion.2, bf16[8,640,128]{1,2,0:T(8,128)(2,1)S(1)} %get-tuple-element.282, s32[]{:T(128)S(6)} %copy.85, bf16[8,256,128]{1,2,0:T(8,128)(2,1)} %get-tuple-element.281), kind=kOutput, calls=%fused_computation.79.clone.1 | convolution fusion | flops 42434304 | bytes 1050624 | tf_op jit(solution)/shard_map/while/body/eval_jaxpr/dot_general | solution.py:35
  42.8 0.9 fusion.85
  43.7 1.9 %fusion.86 = f32[8,640,128]{2,1,0:T(8,128)} fusion(f32[8,640,128]{2,1,0:T(8,128)} %get-tuple-element.267, s32[]{:T(128)S(6)} %copy.85, bf16[256,640]{1,0:T(8,128)(2,1)S(1)} %fusion.84, bf16[8,256,128]{1,2,0:T(8,128)(2,1)} %get-tuple-element.281), kind=kOutput, calls=%fused_computation.9.clone.1 | convolution fusion | flops 41943040 | bytes 721920 | tf_op jit(solution)/shard_map/while/body/eval_jaxpr/dot_general | solution.py:48
  45.5 1.0 fusion.87
  46.7 1.2 %fusion.81 = (f32[256]{0:T(256)S(1)}, f32[256,640]{1,0:T(8,128)S(1)}) fusion(pred[256,640]{1,0:T(32,128)(4,1)S(1)} %bitcast_and_fusion.2, bf16[8,640,128]{1,2,0:T(8,128)(2,1)S(1)} %get-tuple-element.282, s32[]{:T(128)S(6)} %copy.85, bf16[8,256,128]{1,2,0:T(8,128)(2,1)} %get-tuple-element.281), kind=kOutput, calls=%fused_computation.79.clone.1 | convolution fusion | flops 42434304 | bytes 1050624 | tf_op jit(solution)/shard_map/while/body/eval_jaxpr/dot_general | solution.py:35
  49.1 0.9 fusion.85
  50.0 1.9 %fusion.86 = f32[8,640,128]{2,1,0:T(8,128)} fusion(f32[8,640,128]{2,1,0:T(8,128)} %get-tuple-element.267, s32[]{:T(128)S(6)} %copy.85, bf16[256,640]{1,0:T(8,128)(2,1)S(1)} %fusion.84, bf16[8,256,128]{1,2,0:T(8,128)(2,1)} %get-tuple-element.281), kind=kOutput, calls=%fused_computation.9.clone.1 | convolution fusion | flops 41943040 | bytes 721920 | tf_op jit(solution)/shard_map/while/body/eval_jaxpr/dot_general | solution.py:48
  51.9 1.0 fusion.87
  53.0 1.2 %fusion.81 = (f32[256]{0:T(256)S(1)}, f32[256,640]{1,0:T(8,128)S(1)}) fusion(pred[256,640]{1,0:T(32,128)(4,1)S(1)} %bitcast_and_fusion.2, bf16[8,640,128]{1,2,0:T(8,128)(2,1)S(1)} %get-tuple-element.282, s32[]{:T(128)S(6)} %copy.85, bf16[8,256,128]{1,2,0:T(8,128)(2,1)} %get-tuple-element.281), kind=kOutput, calls=%fused_computation.79.clone.1 | convolution fusion | flops 42434304 | bytes 1050624 | tf_op jit(solution)/shard_map/while/body/eval_jaxpr/dot_general | solution.py:35
  55.4 0.9 fusion.85
  56.3 1.9 %fusion.86 = f32[8,640,128]{2,1,0:T(8,128)} fusion(f32[8,640,128]{2,1,0:T(8,128)} %get-tuple-element.267, s32[]{:T(128)S(6)} %copy.85, bf16[256,640]{1,0:T(8,128)(2,1)S(1)} %fusion.84, bf16[8,256,128]{1,2,0:T(8,128)(2,1)} %get-tuple-element.281), kind=kOutput, calls=%fused_computation.9.clone.1 | convolution fusion | flops 41943040 | bytes 721920 | tf_op jit(solution)/shard_map/while/body/eval_jaxpr/dot_general | solution.py:48
  58.2 1.0 fusion.87
  59.4 1.2 %fusion.81 = (f32[256]{0:T(256)S(1)}, f32[256,640]{1,0:T(8,128)S(1)}) fusion(pred[256,640]{1,0:T(32,128)(4,1)S(1)} %bitcast_and_fusion.2, bf16[8,640,128]{1,2,0:T(8,128)(2,1)S(1)} %get-tuple-element.282, s32[]{:T(128)S(6)} %copy.85, bf16[8,256,128]{1,2,0:T(8,128)(2,1)} %get-tuple-element.281), kind=kOutput, calls=%fused_computation.79.clone.1 | convolution fusion | flops 42434304 | bytes 1050624 | tf_op jit(solution)/shard_map/while/body/eval_jaxpr/dot_general | solution.py:35
  61.8 0.9 fusion.85
  62.7 1.9 %fusion.86 = f32[8,640,128]{2,1,0:T(8,128)} fusion(f32[8,640,128]{2,1,0:T(8,128)} %get-tuple-element.267, s32[]{:T(128)S(6)} %copy.85, bf16[256,640]{1,0:T(8,128)(2,1)S(1)} %fusion.84, bf16[8,256,128]{1,2,0:T(8,128)(2,1)} %get-tuple-element.281), kind=kOutput, calls=%fused_computation.9.clone.1 | convolution fusion | flops 41943040 | bytes 721920 | tf_op jit(solution)/shard_map/while/body/eval_jaxpr/dot_general | solution.py:48
  64.5 1.0 fusion.87
  65.7 1.2 %fusion.81 = (f32[256]{0:T(256)S(1)}, f32[256,640]{1,0:T(8,128)S(1)}) fusion(pred[256,640]{1,0:T(32,128)(4,1)S(1)} %bitcast_and_fusion.2, bf16[8,640,128]{1,2,0:T(8,128)(2,1)S(1)} %get-tuple-element.282, s32[]{:T(128)S(6)} %copy.85, bf16[8,256,128]{1,2,0:T(8,128)(2,1)} %get-tuple-element.281), kind=kOutput, calls=%fused_computation.79.clone.1 | convolution fusion | flops 42434304 | bytes 1050624 | tf_op jit(solution)/shard_map/while/body/eval_jaxpr/dot_general | solution.py:35
  68.1 0.9 fusion.85
  69.0 1.9 %fusion.86 = f32[8,640,128]{2,1,0:T(8,128)} fusion(f32[8,640,128]{2,1,0:T(8,128)} %get-tuple-element.267, s32[]{:T(128)S(6)} %copy.85, bf16[256,640]{1,0:T(8,128)(2,1)S(1)} %fusion.84, bf16[8,256,128]{1,2,0:T(8,128)(2,1)} %get-tuple-element.281), kind=kOutput, calls=%fused_computation.9.clone.1 | convolution fusion | flops 41943040 | bytes 721920 | tf_op jit(solution)/shard_map/while/body/eval_jaxpr/dot_general | solution.py:48
  70.9 1.0 fusion.87
  72.1 1.2 %fusion.81 = (f32[256]{0:T(256)S(1)}, f32[256,640]{1,0:T(8,128)S(1)}) fusion(pred[256,640]{1,0:T(32,128)(4,1)S(1)} %bitcast_and_fusion.2, bf16[8,640,128]{1,2,0:T(8,128)(2,1)S(1)} %get-tuple-element.282, s32[]{:T(128)S(6)} %copy.85, bf16[8,256,128]{1,2,0:T(8,128)(2,1)} %get-tuple-element.281), kind=kOutput, calls=%fused_computation.79.clone.1 | convolution fusion | flops 42434304 | bytes 1050624 | tf_op jit(solution)/shard_map/while/body/eval_jaxpr/dot_general | solution.py:35
  74.5 0.9 fusion.85
  75.4 1.9 %fusion.86 = f32[8,640,128]{2,1,0:T(8,128)} fusion(f32[8,640,128]{2,1,0:T(8,128)} %get-tuple-element.267, s32[]{:T(128)S(6)} %copy.85, bf16[256,640]{1,0:T(8,128)(2,1)S(1)} %fusion.84, bf16[8,256,128]{1,2,0:T(8,128)(2,1)} %get-tuple-element.281), kind=kOutput, calls=%fused_computation.9.clone.1 | convolution fusion | flops 41943040 | bytes 721920 | tf_op jit(solution)/shard_map/while/body/eval_jaxpr/dot_general | solution.py:48
  77.2 1.0 fusion.87
  78.2 2.9 %slice_bitcast_fusion = (f32[8,24,8,128]{3,2,1,0:T(8,128)}, f32[192,8,128]{2,0,1:T(8,128)S(1)}, f32[192,8,128]{2,0,1:T(8,128)S(1)}) fusion(f32[640,8,128]{2,0,1:T(8,128)} %bitcast.156), kind=kLoop, calls=%fused_computation.51 | loop fusion | bytes 4718592
  81.1 1.1 fusion.44
  82.2 0.5 copy.54
  82.7 1.1 stack.30
  83.7 0.5 copy.56
  84.2 1.1 stack.33
  85.7 1.0 stack.34
  87.2 1.0 stack.31
  88.2 1.3 %pad_maximum_fusion = f32[2,192,1024]{2,1,0:T(8,128)S(1)} fusion(f32[1,192,1024]{2,1,0:T(8,128)} %stack.31, f32[1,192,1024]{2,1,0:T(8,128)S(1)} %copy-done.1), kind=kLoop, calls=%fused_computation.41 | loop fusion | flops 393216 | bytes 3145728 | tf_op jit(solution)/shard_map/stack | solution.py:90
  89.5 2.5 %collective-permute-start.2 = (f32[2,192,1024]{2,1,0:T(8,128)S(1)}, f32[2,192,1024]{2,1,0:T(8,128)S(1)}, u32[]{:S(2)}, u32[]{:S(2)}) collective-permute-start(f32[2,192,1024]{2,1,0:T(8,128)S(1)} %pad_maximum_fusion), channel_id=1, source_target_pairs={{1,0},{2,1},{3,2},{4,3},{5,4},{6,5},{7,6},{8,7},{9,8},{10,9},{11,1... | collective-permute-start | bytes 4718600 | tf_op jit(solution)/shard_map/ppermute | solution.py:31
  92.2 2.0 %collective-permute-start.3 = (f32[2,192,1024]{2,1,0:T(8,128)S(1)}, f32[2,192,1024]{2,1,0:T(8,128)S(1)}, u32[]{:S(2)}, u32[]{:S(2)}) collective-permute-start(f32[2,192,1024]{2,1,0:T(8,128)S(1)} %pad_maximum_fusion.1), channel_id=1, source_target_pairs={{0,1},{1,2},{2,3},{3,4},{4,5},{5,6},{6,7},{7,8},{8,9},{9,10},{10,1... | collective-permute-start | bytes 4718600 | tf_op jit(solution)/shard_map/ppermute | solution.py:31
  94.2 1.0 copy_bitcast_fusion.1
  95.2 1.0 copy_bitcast_fusion.2
  96.2 0.9 copy_bitcast_fusion
  97.0 12.9 %collective-permute-done.2 = f32[2,192,1024]{2,1,0:T(8,128)S(1)} collective-permute-done((f32[2,192,1024]{2,1,0:T(8,128)S(1)}, f32[2,192,1024]{2,1,0:T(8,128)S(1)}, u32[]{:S(2)}, u32[]{:S(2)}) %collective-permute-start.2) | collective-permute-done | bytes 1572896 | tf_op jit(solution)/shard_map/ppermute | solution.py:31
  110.0 6.1 %collective-permute-done.3 = f32[2,192,1024]{2,1,0:T(8,128)S(1)} collective-permute-done((f32[2,192,1024]{2,1,0:T(8,128)S(1)}, f32[2,192,1024]{2,1,0:T(8,128)S(1)}, u32[]{:S(2)}, u32[]{:S(2)}) %collective-permute-start.3) | collective-permute-done | bytes 1572896 | tf_op jit(solution)/shard_map/ppermute | solution.py:31
  116.5 0.8 pad_maximum_fusion.4
  117.3 0.8 pad_maximum_fusion.3
  (100 shorter events, 14.1 us)
Async XLA Ops:
  0.6 9.3 %copy-start.8 = (bf16[256,1024]{1,0:T(8,128)(2,1)S(1)}, bf16[256,1024]{1,0:T(8,128)(2,1)}, u32[]{:S(2)}) copy-start(bf16[256,1024]{1,0:T(8,128)(2,1)} %param.11) | copy-start | bytes 1572868
  0.6 8.3 %copy-start.7 = (bf16[256,1024]{1,0:T(8,128)(2,1)S(1)}, bf16[256,1024]{1,0:T(8,128)(2,1)}, u32[]{:S(2)}) copy-start(bf16[256,1024]{1,0:T(8,128)(2,1)} %param.10) | copy-start | bytes 1572868
  0.7 10.3 %copy-start.13 = (s32[8]{0:T(128)S(1)}, s32[8]{0:T(128)}, u32[]{:S(2)}) copy-start(s32[8]{0:T(128)} %param.15) | copy-start | bytes 100
  0.7 10.4 %copy-start.12 = (s32[8,14]{1,0:T(8,128)S(1)}, s32[8,14]{1,0:T(8,128)}, u32[]{:S(2)}) copy-start(s32[8,14]{1,0:T(8,128)} %param.14) | copy-start | bytes 1348
  0.7 11.2 %copy-start.9 = (bf16[256,1024]{1,0:T(8,128)(2,1)S(1)}, bf16[256,1024]{1,0:T(8,128)(2,1)}, u32[]{:S(2)}) copy-start(bf16[256,1024]{1,0:T(8,128)(2,1)} %param.9) | copy-start | bytes 1572868
  2.0 10.9 %copy-start.10 = (bf16[256,1024]{1,0:T(8,128)(2,1)S(1)}, bf16[256,1024]{1,0:T(8,128)(2,1)}, u32[]{:S(2)}) copy-start(bf16[256,1024]{1,0:T(8,128)(2,1)} %param.12) | copy-start | bytes 1572868
  2.1 14.4 %collective-permute-start.1 = (bf16[2,192,1024]{2,1,0:T(8,128)(2,1)S(1)}, bf16[2,192,1024]{2,1,0:T(8,128)(2,1)}, u32[]{:S(2)}, u32[]{:S(2)}) collective-permute-start(bf16[2,192,1024]{2,1,0:T(8,128)(2,1)S(1)} %pad_maximum_fusion.2), channel_id=1, source_target_pairs={{1,0},{2,1},{3,2},{4,3},{5,4},{6,5},{7,6},{8,7},{9,8},{10,9},{11,1... | collective-permute-start | bytes 2359304 | tf_op jit(solution)/shard_map/ppermute | solution.py:21
  7.0 15.5 %collective-permute-start = (bf16[2,192,1024]{2,1,0:T(8,128)(2,1)S(1)}, bf16[2,192,1024]{2,1,0:T(8,128)(2,1)}, u32[]{:S(2)}, u32[]{:S(2)}) collective-permute-start(bf16[2,192,1024]{2,1,0:T(8,128)(2,1)S(1)} %pad_maximum_fusion.2), channel_id=1, source_target_pairs={{0,1},{1,2},{2,3},{3,4},{4,5},{5,6},{6,7},{7,8},{8,9},{9,10},{10,1... | collective-permute-start | bytes 2359304 | tf_op jit(solution)/shard_map/ppermute | solution.py:19
  24.9 1.0 copy-start.6
  78.2 2.9 %copy-start.5 = (f32[8,640,128]{2,1,0:T(8,128)S(1)}, f32[8,640,128]{2,1,0:T(8,128)}, u32[]{:S(2)}) copy-start(f32[8,640,128]{2,1,0:T(8,128)} %get-tuple-element.94) | copy-start | bytes 7864324
  85.7 2.5 %copy-start.1 = (f32[1,192,1024]{2,1,0:T(8,128)S(1)}, f32[1,192,1024]{2,1,0:T(8,128)}, u32[]{:S(2)}) copy-start(f32[1,192,1024]{2,1,0:T(8,128)} %stack.30) | copy-start | bytes 2359300
  87.2 4.8 %copy-start = (f32[1,192,1024]{2,1,0:T(8,128)S(1)}, f32[1,192,1024]{2,1,0:T(8,128)}, u32[]{:S(2)}) copy-start(f32[1,192,1024]{2,1,0:T(8,128)} %stack.33) | copy-start | bytes 2359300
  87.2 4.8 %copy-start.2 = (f32[1,192,1024]{2,1,0:T(8,128)S(1)}, f32[1,192,1024]{2,1,0:T(8,128)}, u32[]{:S(2)}) copy-start(f32[1,192,1024]{2,1,0:T(8,128)} %stack.34) | copy-start | bytes 2359300
  89.5 6.7 %copy-start.11 = (bf16[8,256,128]{2,1,0:T(8,128)(2,1)S(1)}, bf16[8,256,128]{2,1,0:T(8,128)(2,1)}, u32[]{:S(2)}) copy-start(bf16[8,256,128]{2,1,0:T(8,128)(2,1)} %get-tuple-element.93) | copy-start | bytes 1572868
  89.5 26.6 %copy-start.3 = (f32[8,24,8,128]{3,2,1,0:T(8,128)S(1)}, f32[8,24,8,128]{3,2,1,0:T(8,128)}, u32[]{:S(2)}) copy-start(f32[8,24,8,128]{3,2,1,0:T(8,128)} %get-tuple-element.170) | copy-start | bytes 2359300
  89.5 26.6 %copy-start.4 = (f32[8,24,8,128]{3,2,1,0:T(8,128)S(1)}, f32[8,24,8,128]{3,2,1,0:T(8,128)}, u32[]{:S(2)}) copy-start(f32[8,24,8,128]{3,2,1,0:T(8,128)} %get-tuple-element.175) | copy-start | bytes 2359300
  89.5 20.4 %collective-permute-start.2 = (f32[2,192,1024]{2,1,0:T(8,128)S(1)}, f32[2,192,1024]{2,1,0:T(8,128)S(1)}, u32[]{:S(2)}, u32[]{:S(2)}) collective-permute-start(f32[2,192,1024]{2,1,0:T(8,128)S(1)} %pad_maximum_fusion), channel_id=1, source_target_pairs={{1,0},{2,1},{3,2},{4,3},{5,4},{6,5},{7,6},{8,7},{9,8},{10,9},{11,1... | collective-permute-start | bytes 4718600 | tf_op jit(solution)/shard_map/ppermute | solution.py:31
  92.2 23.8 %collective-permute-start.3 = (f32[2,192,1024]{2,1,0:T(8,128)S(1)}, f32[2,192,1024]{2,1,0:T(8,128)S(1)}, u32[]{:S(2)}, u32[]{:S(2)}) collective-permute-start(f32[2,192,1024]{2,1,0:T(8,128)S(1)} %pad_maximum_fusion.1), channel_id=1, source_target_pairs={{0,1},{1,2},{2,3},{3,4},{4,5},{5,6},{6,7},{7,8},{8,9},{9,10},{10,1... | collective-permute-start | bytes 4718600 | tf_op jit(solution)/shard_map/ppermute | solution.py:31
where the time goes:
time: 119 us; the launch traced here: 118 us
  matrix products  44.9 us (38%)
  waiting for transfers between devices  26.1 us (22%)
  local copies, waits for them, and re-layouts  22.6 us (19%)
  other arithmetic  11.3 us (9%)
  starting transfers between devices  11.3 us (9%)
  between operations  1.6 us (1%)
    ppermute x2, waiting for transfers between devices, shifted(): return lax.ppermute(x, axis, pairs)  19 us
    dot_general x8, matrix products, head_grads(): grad_k = jnp.dot(score_grad.T, q_head, preferred_element_type=jnp.float32)  14.9 us
    dot_general x8, matrix products, head_grads(): jnp.dot(q_head, k_frame.T, preferred_element_type=jnp.float32) * scale  9.79 us
    dot_general x8, matrix products, head_grads(): grad_v = jnp.dot(weight_b.T, g_head, preferred_element_type=jnp.float32)  8.22 us
    dot_general x8, matrix products, head_grads(): grad_q = jnp.dot(score_grad, k_frame, preferred_element_type=jnp.float32)  7.11 us
    unnamed x34, local copies, waits for them, and re-layouts  6.15 us
    ppermute x1, starting transfers between devices, padded(): lax.ppermute(head, axis, [((i + 1) % count, i) for i in range(ends)])  4.94 us
    ppermute x2, starting transfers between devices, shifted(): return lax.ppermute(x, axis, pairs)  4.46 us
  transfers between devices with their start and end apart: 4, of which 4 were waited for; matrix products, arithmetic and copies ran while one was open for 7% of the time, Pallas kernels for 0%

commit v1 on v0

v1 whole, which is shorter than its diff:
```python
import functools
import jax
import jax.numpy as jnp
from jax import lax
from jax.experimental import pallas as pl
from jax.experimental.pallas import tpu as pltpu
from jax.sharding import PartitionSpec as P

HEADS = 8
DEPTH = 128
BLK = 32
RB = 6
RIM = RB * BLK
TABLE = 32
LOG2E = 1.4426950408889634
NEG = -1e30
FLOOR = -1e20
MIB = 1024 * 1024
LOAD_LIMIT = 51.2
GATHER = True
SPLIT = 4


def nt(a, b):
    return lax.dot_general(a, b, (((1,), (1,)), ((), ())), preferred_element_type=jnp.float32)


def tn(a, b):
    return lax.dot_general(a, b, (((0,), (0,)), ((), ())), preferred_element_type=jnp.float32)


def nn(a, b):
    return jnp.dot(a, b, preferred_element_type=jnp.float32)


def cols(h):
    return slice(h * DEPTH, (h + 1) * DEPTH)


def biased(score, bias, first):
    scaled = score * (DEPTH ** -0.5 * LOG2E)
    parts = [
        scaled[at * BLK : (at + 1) * BLK] + bias[first + at : first + at + 1, :]
        for at in range(score.shape[0] // BLK)
    ]
    return jnp.concatenate(parts, axis=0)


def table_of(lists, live, ids, count, tok):
    blocks, slots = lists.shape
    hit = jnp.zeros((blocks, ids.shape[1]), jnp.float32)
    for l in range(slots):
        hit = jnp.where((lists[:, l : l + 1] == ids) & (live > l), 1.0, hit)
    lane = lax.broadcasted_iota(jnp.int32, (blocks, tok), 1)
    row = lax.broadcasted_iota(jnp.int32, (blocks, tok), 0)
    spread = jnp.where((lane // BLK == row) & (lane < count), 1.0, 0.0)
    return jnp.where(tn(hit, spread) > 0.5, 0.0, NEG)


def own_score(k, q, bias):
    x = nt(k, q) * (DEPTH ** -0.5 * LOG2E)
    parts = [x[at * BLK : (at + 1) * BLK] + bias[at : at + 1, :] for at in range(RB)]
    return jnp.concatenate(parts + [x[RIM:] + bias[TABLE:, :]], axis=0)


def stats_of(x, prod):
    top = jnp.maximum(jnp.max(x, axis=0, keepdims=True), FLOOR)
    p = jnp.exp2(x - top)
    return top, jnp.sum(p, axis=0, keepdims=True), jnp.sum(p * prod, axis=0, keepdims=True)


def merged(a, b):
    top = jnp.maximum(a[0], b[0])
    fa, fb = jnp.exp2(a[0] - top), jnp.exp2(b[0] - top)
    return top, a[1] * fa + b[1] * fb, a[2] * fa + b[2] * fb


def grads_of(x, prod, top, inv, delta):
    p = jnp.exp2(x - top)
    w = (p * inv).astype(jnp.bfloat16)
    ds = (p * (inv * (DEPTH ** -0.5)) * (prod - delta)).astype(jnp.bfloat16)
    return w, ds


def swap_across(x):
    count = lax.axis_size("band")
    pairs = [(at, at + 1) for at in range(1, count - 1, 2)]
    return lax.ppermute(x, "band", pairs + [(b, a) for a, b in pairs])


def swap_inside(x):
    if not GATHER:
        return lax.ppermute(x, "band", [(at, at ^ 1) for at in range(lax.axis_size("band"))])
    pairs = [[at, at + 1] for at in range(0, lax.axis_size("band"), 2)]
    return lax.all_gather(x, "band", axis_index_groups=pairs)


def load_kernel(
    k_ref, v_ref, q_ref, g_ref, lead_ref, k_out, v_out, q_out, g_out, sems
):
    tok = k_ref.shape[0]
    lead = lead_ref.shape[2]
    moves = [(src.at[pl.ds(0, RIM), pl.ds(0, lead)], lead_ref.at[at]) for at, src in enumerate((k_ref, v_ref))]
    moves += [(k_ref, k_out), (v_ref, v_out), (q_ref, q_out), (g_ref, g_out)]
    copies = [pltpu.make_async_copy(src, dst, sems.at[at]) for at, (src, dst) in enumerate(moves)]
    for copy in copies:
        copy.start()
    for copy in copies:
        copy.wait()


def own_kernel(
    count_ref, live_ref, lists_ref, q_ref, k_ref, v_ref, g_ref, table_ref, stats_ref, lead_b_ref, lead_i_ref
):
    tok = q_ref.shape[0]
    blocks = lists_ref.shape[0]
    count = count_ref[0]
    row = lax.broadcasted_iota(jnp.int32, (blocks, 1), 0)
    live = jnp.zeros_like(row)
    for n in range(blocks):
        live = jnp.where(row == n, live_ref[n], live)
    odd = lax.axis_index("band") % 2
    slot = lax.broadcasted_iota(jnp.int32, (blocks, TABLE), 1)
    x_first = 8 + RB * odd
    i_first = 8 + RB * (1 - odd)
    ids = jnp.where(slot < 8, slot, jnp.where(slot < 8 + RB, slot - 8 + x_first, slot - 8 - RB + i_first))
    ids = jnp.where(slot < 8 + 2 * RB, ids, -1)
    table = table_of(lists_ref[...], live, ids, count, tok)
    table_ref[:TABLE] = table
    past = lax.broadcasted_iota(jnp.int32, (tok - RIM, tok), 0) + RIM >= count
    tail = [jnp.broadcast_to(table[at : at + 1], (BLK, tok)) for at in range(RB, tok // BLK)]
    table_ref[TABLE:] = jnp.where(past, NEG, jnp.concatenate(tail, axis=0))
    for h in range(HEADS):
        q, k, v, g = (ref[:, cols(h)] for ref in (q_ref, k_ref, v_ref, g_ref))
        for at, lead in enumerate((k, v)):
            lead_i_ref[at, :, cols(h)] = lead[:RIM]
            if h >= SPLIT:
                lead_b_ref[at, :, cols(h - SPLIT)] = lead[:RIM]
        x = own_score(k, q, table_ref)
        top, total, raw = stats_of(x, nt(v, g))
        stats_ref[h] = jnp.concatenate([top, total, raw, jnp.zeros((5, tok), jnp.float32)], axis=0)


def rim_kernel(first, q_ref, g_ref, x_ref, i_ref, table_ref, stats_ref, *refs):
    gx_ref, gi_ref, final_ref, dq_ref = refs[-4:]
    if GATHER:
        i_ref = i_ref.at[1 - lax.axis_index("band") % 2]
    tok = q_ref.shape[0]
    if first:
        gi_ref[0] = refs[0][...]
        gi_ref = gi_ref.at[1]
    for at in range(x_ref.shape[2] // DEPTH):
        h = first + at
        q, g = q_ref[:, cols(h)], g_ref[:, cols(h)]
        score_x = biased(nt(x_ref[0, :, cols(at)], q), table_ref, 8)
        prod_x = nt(x_ref[1, :, cols(at)], g)
        score_i = biased(nt(i_ref[0, :, cols(h)], q), table_ref, 8 + RB)
        prod_i = nt(i_ref[1, :, cols(h)], g)
        own = (stats_ref[h, 0:1], stats_ref[h, 1:2], stats_ref[h, 2:3])
        top, total, raw = merged(own, merged(stats_of(score_x, prod_x), stats_of(score_i, prod_i)))
        inv = jnp.where(total > 0.0, 1.0 / jnp.where(total > 0.0, total, 1.0), 0.0)
        delta = raw * inv
        w, ds = grads_of(score_x, prod_x, top, inv, delta)
        gx_ref[0, :, cols(at)] = nn(ds, q).astype(jnp.bfloat16)
        gx_ref[1, :, cols(at)] = nn(w, g).astype(jnp.bfloat16)
        dq = tn(x_ref[0, :, cols(at)], ds)
        w, ds = grads_of(score_i, prod_i, top, inv, delta)
        gi_ref[0, :, cols(at)] = nn(ds, q).astype(jnp.bfloat16)
        gi_ref[1, :, cols(at)] = nn(w, g).astype(jnp.bfloat16)
        dq_ref[at] = dq + tn(i_ref[0, :, cols(h)], ds)
        final_ref[at] = jnp.concatenate([top, inv, delta, jnp.zeros((5, tok), jnp.float32)], axis=0)


def rest_of(first, at, q_ref, k_ref, v_ref, g_ref, table_ref, final_ref, rim_dq_ref):
    h = first + at
    q, k, v, g = (ref[:, cols(h)] for ref in (q_ref, k_ref, v_ref, g_ref))
    top, inv, delta = final_ref[at, 0:1], final_ref[at, 1:2], final_ref[at, 2:3]
    x = own_score(k, q, table_ref)
    w, ds = grads_of(x, nt(v, g), top, inv, delta)
    dq = rim_dq_ref[at] + tn(k, ds)
    return dq.T.astype(jnp.bfloat16), nn(ds, q), nn(w, g)


def held_kernel(first, *refs):
    _, dq_ref, pk_ref, pv_ref, dq_buf, sems = refs[7:]
    copies = []
    for at in range(pk_ref.shape[1] // DEPTH):
        dq, pk_ref[:, cols(at)], pv_ref[:, cols(at)] = rest_of(first, at, *refs[:7])
        dq_buf[:, cols(at)] = dq
        copies.append(pltpu.make_async_copy(dq_buf.at[:, cols(at)], dq_ref.at[:, cols(first + at)], sems.at[at]))
        copies[-1].start()
    for copy in copies:
        copy.wait()


def done_kernel(first, *refs):
    gx_ref, gi_ref, _, dq_ref, dk_ref, dv_ref, dq_buf, dk_buf, dv_buf, sems = refs[7:]
    if GATHER:
        gi_ref = gi_ref.at[1 - lax.axis_index("band") % 2]
    copies = []
    for at in range(dq_buf.shape[1] // DEPTH):
        dq, dk, dv = rest_of(first, at, *refs[:7])
        dq_buf[:, cols(at)] = dq
        for slot, buf, part in ((0, dk_buf, dk), (1, dv_buf, dv)):
            lead = gx_ref[slot, :, cols(at)].astype(jnp.float32) + gi_ref[0, slot, :, cols(at)].astype(jnp.float32)
            buf[:RIM, cols(at)] = (part[:RIM] + lead).astype(jnp.bfloat16)
            buf[RIM:, cols(at)] = part[RIM:].astype(jnp.bfloat16)
        for n, (buf, out) in enumerate(((dq_buf, dq_ref), (dk_buf, dk_ref), (dv_buf, dv_ref))):
            copies.append(pltpu.make_async_copy(buf.at[:, cols(at)], out.at[:, cols(first + at)], sems.at[n, at]))
            copies[-1].start()
    for copy in copies:
        copy.wait()


def add_kernel(first, pk_ref, pv_ref, gx_ref, gi_ref, _k, _v, dk_ref, dv_ref, dk_buf, dv_buf, sems):
    width = pk_ref.shape[1]
    if GATHER:
        gi_ref = gi_ref.at[1 - lax.axis_index("band") % 2]
    copies = []
    for slot, (own, buf, out) in enumerate(((pk_ref, dk_buf, dk_ref), (pv_ref, dv_buf, dv_ref))):
        lead = gx_ref[slot].astype(jnp.float32) + gi_ref[1, slot].astype(jnp.float32)
        buf[:RIM] = (own[:RIM] + lead).astype(jnp.bfloat16)
        buf[RIM:] = own[RIM:].astype(jnp.bfloat16)
        copies.append(pltpu.make_async_copy(buf, out.at[:, pl.ds(first * DEPTH, width)], sems.at[slot]))
        copies[-1].start()
    for copy in copies:
        copy.wait()


VMEM = pl.BlockSpec(memory_space=pltpu.VMEM)
SMEM = pl.BlockSpec(memory_space=pltpu.SMEM)
HBM = pl.BlockSpec(memory_space=pltpu.HBM)
ANY = pl.BlockSpec(memory_space=pl.ANY)


def call(body, name, ins, outs, out_specs, args, scratch=(), alias=None, limit=24):
    return pl.pallas_call(
        body,
        in_specs=ins,
        out_specs=out_specs,
        out_shape=outs,
        scratch_shapes=scratch,
        input_output_aliases=alias or {},
        compiler_params=pltpu.CompilerParams(vmem_limit_bytes=int(limit * MIB)),
        cost_estimate=pl.CostEstimate(flops=1000, bytes_accessed=1000, transcendentals=0),
        name=name,
    )(*args)


def shape(*dims, dtype=jnp.bfloat16):
    return jax.ShapeDtypeStruct(dims, dtype)


def on_device(queries, keys, values, out_grad, band_counts, block_lists, slot_counts):
    tok, width = queries.shape
    f32 = functools.partial(shape, dtype=jnp.float32)
    cuts = ((0, SPLIT), (SPLIT, HEADS))
    part = HEADS - SPLIT
    lead_a, k, v, q, g = call(
        load_kernel,
        "load_bands",
        [HBM] * 4,
        [shape(2, RIM, SPLIT * DEPTH)] + [shape(tok, width)] * 4,
        [VMEM] * 5,
        (keys, values, queries, out_grad),
        [pltpu.SemaphoreType.DMA((6,))],
        limit=LOAD_LIMIT,
    )
    x_a = swap_across(lead_a)
    table, stats, lead_b, lead_i = call(
        own_kernel,
        "own_stats",
        [SMEM] * 2 + [VMEM] * 5,
        [f32(TABLE + tok - RIM, tok), f32(HEADS, 8, tok), shape(2, RIM, part * DEPTH), shape(2, RIM, width)],
        [VMEM] * 4,
        (band_counts, slot_counts, block_lists, q, k, v, g),
    )
    x_b = swap_across(lead_b)
    i = swap_inside(lead_i)

    def rim(first, x, *more):
        heads = x.shape[2] // DEPTH
        gi = (2, 2, RIM, x.shape[2]) if more else x.shape
        return call(
            functools.partial(rim_kernel, first),
            "rim_grads",
            [VMEM] * (6 + len(more)),
            [shape(*x.shape), shape(*gi), f32(heads, 8, tok), f32(heads, DEPTH, tok)],
            [VMEM] * 4,
            (q, g, x, i, table, stats) + more,
        )

    gx_a, gi_a, final_a, dq_a = rim(0, x_a)
    gx_a = swap_across(gx_a)
    gx_b, gi, final_b, dq_b = rim(SPLIT, x_b, gi_a)
    gx_b = swap_across(gx_b)
    gi = swap_inside(gi)

    dq, pk, pv = call(
        functools.partial(held_kernel, SPLIT),
        "held_grads",
        [VMEM] * 7 + [ANY],
        [shape(tok, width), f32(tok, part * DEPTH), f32(tok, part * DEPTH)],
        [ANY, VMEM, VMEM],
        (q, k, v, g, table, final_b, dq_b, gx_a),
        [pltpu.VMEM((tok, part * DEPTH), jnp.bfloat16), pltpu.SemaphoreType.DMA((part,))],
    )
    dq, dk, dv = call(
        functools.partial(done_kernel, 0),
        "done_grads",
        [VMEM] * 9 + [ANY],
        [shape(tok, width)] * 3,
        [ANY] * 3,
        (q, k, v, g, table, final_a, dq_a, gx_a, gi, dq),
        [pltpu.VMEM((tok, SPLIT * DEPTH), jnp.bfloat16)] * 3 + [pltpu.SemaphoreType.DMA((3, SPLIT))],
        {9: 0},
    )
    dk, dv = call(
        functools.partial(add_kernel, SPLIT),
        "add_rims",
        [VMEM] * 4 + [ANY] * 2,
        [shape(tok, width)] * 2,
        [ANY] * 2,
        (pk, pv, gx_b, gi, dk, dv),
        [pltpu.VMEM((tok, part * DEPTH), jnp.bfloat16)] * 2 + [pltpu.SemaphoreType.DMA((2,))],
        {4: 0, 5: 1},
    )
    return dq, dk, dv


def solution(mesh):
    placed = P(("member", "band"), None)
    flat = P(("member", "band"))
    return jax.shard_map(
        on_device,
        mesh=mesh,
        in_specs=(placed, placed, placed, placed, flat, placed, flat),
        out_specs=(placed, placed, placed),
        check_vma=False,
    )
```

time: 119 us -> 79.4 us (0.67)
  the two profiles are of different devices: /device:TPU:454 before, /device:TPU:1 now
where the time goes in v1:
time: 79.4 us; the launch traced here: 79 us
  waiting for transfers between devices  26.9 us (34%)
  between operations  14.9 us (19%)
  Pallas kernels  14.5 us (18%)
  starting transfers between devices  12.2 us (15%)
  local copies, waits for them, and re-layouts  10.6 us (13%)
    all_gather x2, waiting for transfers between devices, swap_inside(): return lax.all_gather(x, 'band', axis_index_groups=pairs)  19.6 us
    pallas_call x7, Pallas kernels, call(): pl.pallas_call(body, in_specs=ins, out_specs=out_specs, out_shape=outs, s...  14.5 us
    ppermute x4, starting transfers between devices, swap_across(): return lax.ppermute(x, 'band', pairs + [(b, a) for a, b in pairs])  12.1 us
    unnamed x36, local copies, waits for them, and re-layouts  10.6 us
    ppermute x4, waiting for transfers between devices, swap_across(): return lax.ppermute(x, 'band', pairs + [(b, a) for a, b in pairs])  7.25 us
  transfers between devices with their start and end apart: 6, of which 4 were waited for; matrix products, arithmetic and copies ran while one was open for 0% of the time, Pallas kernels for 8%

profile of v1, /device:TPU:1, one launch (start us, length us, event | category | flops | bytes accessed | tf_op | source)
XLA Modules:
  0.0 79.0 jit_solution(7623394156794959576)
XLA Ops:
  7.2 0.0 copy-start.15
  7.2 0.0 copy-start.14
  7.2 0.0 all-gather.5.cloned.1.call-start
  7.9 1.8 %load_bands.1 = (bf16[2,192,512]{2,1,0:T(8,128)(2,1)S(1)}, bf16[256,1024]{1,0:T(8,128)(2,1)S(1)}, bf16[256,1024]{1,0:T(8,128)(2,1)S(1)}, bf16[256,1024]{1,0:T(8,128)(2,1)S(1)}, bf16[256,1024]{1,0:T(8,128)(2,1)S(1)}) custom-call(bf16[256,1024]{1,0:T(8,128)(2,1)} %k_ref.1, bf16[256,1024]{1,0:T(8,128)(2,1)} %v_ref.1, bf16[256,1024]{1,0:T(8,128)(2,1)} %q_ref.1, ...), custom_call_target="tpu_custom_call" | custom-call | flops 1000 | bytes 1000 | tf_op jit(solution)/shard_map/load_bands/pallas_call | solution.py:237
  9.7 0.0 copy-done.15
  9.7 0.0 copy-done.14
  9.7 2.5 %own_stats.1 = (f32[96,256]{1,0:T(8,128)S(1)}, f32[8,8,256]{2,1,0:T(8,128)S(1)}, bf16[2,192,512]{2,1,0:T(8,128)(2,1)}, bf16[2,192,1024]{2,1,0:T(8,128)(2,1)}) custom-call(s32[1]{0:T(128)S(6)} %copy.16.count_ref, s32[8]{0:T(128)S(1)} %copy-done.15, s32[8,14]{1,0:T(8,128)S(1)} %copy-done.14, bf16[256,1024]{1,0:T(8,128)(2,1)S(1)} %get-tuple-element.28.q_ref.refs_0_, ...), custom_call_target="tpu_custom_call" | custom-call | flops 1000 | bytes 1000 | tf_op jit(solution)/shard_map/own_stats/pallas_call | solution.py:237
  12.2 0.0 copy-start.9
  12.2 0.6 copy-done.9
  12.8 0.0 all-gather.5.cloned.1.call-update
  12.9 0.0 all-gather.7.cloned.1.call-start
  12.9 4.6 %collective-permute-start = (bf16[2,192,512]{2,1,0:T(8,128)(2,1)S(1)}, bf16[2,192,512]{2,1,0:T(8,128)(2,1)S(1)}, u32[]{:S(2)}, u32[]{:S(2)}) collective-permute-start(bf16[2,192,512]{2,1,0:T(8,128)(2,1)S(1)} %get-tuple-element.33), channel_id=1, source_target_pairs={{1,2},{3,4},{5,6},{7,8},{9,10},{11,12},{13,14},{15,16},{17,18},{19... | collective-permute-start | bytes 1179656 | tf_op jit(solution)/shard_map/ppermute | solution.py:88
  17.5 1.9 %collective-permute-start.2 = (bf16[2,192,512]{2,1,0:T(8,128)(2,1)}, bf16[2,192,512]{2,1,0:T(8,128)(2,1)S(1)}, u32[]{:S(2)}, u32[]{:S(2)}) collective-permute-start(bf16[2,192,512]{2,1,0:T(8,128)(2,1)} %get-tuple-element.39), channel_id=1, source_target_pairs={{1,2},{3,4},{5,6},{7,8},{9,10},{11,12},{13,14},{15,16},{17,18},{19... | collective-permute-start | bytes 1179656 | tf_op jit(solution)/shard_map/ppermute | solution.py:88
  19.4 3.5 %collective-permute-done.x_ref = bf16[2,192,512]{2,1,0:T(8,128)(2,1)S(1)} collective-permute-done((bf16[2,192,512]{2,1,0:T(8,128)(2,1)S(1)}, bf16[2,192,512]{2,1,0:T(8,128)(2,1)S(1)}, u32[]{:S(2)}, u32[]{:S(2)}) %collective-permute-start) | collective-permute-done | bytes 393248 | tf_op jit(solution)/shard_map/ppermute | solution.py:88
  23.0 14.9 %all-gather.5.cloned.1.call-done = bf16[4,192,1024]{2,1,0:T(8,128)(2,1)} async-done(((bf16[2,192,1024]{2,1,0:T(8,128)(2,1)}), bf16[4,192,1024]{2,1,0:T(8,128)(2,1)}) %all-gather.5.cloned.1.call-update) | async-done | bytes 1572880 | tf_op jit(solution)/shard_map/all_gather | solution.py:95
  37.9 0.0 copy-start
  37.9 1.4 %copy-done = bf16[4,192,1024]{2,1,0:T(8,128)(2,1)S(1)} copy-done((bf16[4,192,1024]{2,1,0:T(8,128)(2,1)S(1)}, bf16[4,192,1024]{2,1,0:T(8,128)(2,1)}, u32[]{:S(2)}) %copy-start) | copy-done | bytes 1572888
  39.3 0.0 copy-start.10
  39.3 0.8 %copy-done.10 = f32[8,8,256]{2,1,0:T(8,128)S(1)} copy-done((f32[8,8,256]{2,1,0:T(8,128)S(1)}, f32[8,8,256]{2,1,0:T(8,128)}, u32[]{:S(2)}) %copy-start.10) | copy-done | bytes 65560
  40.2 0.0 copy-start.1
  40.2 0.0 copy-start.11
  40.2 2.1 %rim_grads.2 = (bf16[2,192,512]{2,1,0:T(8,128)(2,1)S(1)}, bf16[2,192,512]{2,1,0:T(8,128)(2,1)S(1)}, f32[4,8,256]{2,1,0:T(8,128)S(1)}, f32[4,128,256]{2,1,0:T(8,128)S(1)}) custom-call(bf16[256,1024]{1,0:T(8,128)(2,1)S(1)} %get-tuple-element.28.q_ref.refs_0_, bf16[256,1024]{1,0:T(8,128)(2,1)S(1)} %get-tuple-element.31.g_ref.refs_3_, ...), custom_call_target="tpu_custom_call" | custom-call | flops 1000 | bytes 1000 | tf_op jit(solution)/shard_map/rim_grads/pallas_call | solution.py:237
  42.3 0.0 copy-start.17
  42.3 0.7 copy-done.17
  43.1 0.0 collective-permute-done.2.x_ref
  43.1 0.0 copy-done.1
  43.1 0.0 copy-done.11
  43.1 3.0 %rim_grads.3 = (bf16[2,192,512]{2,1,0:T(8,128)(2,1)S(1)}, bf16[2,2,192,512]{3,2,1,0:T(8,128)(2,1)}, f32[4,8,256]{2,1,0:T(8,128)S(1)}, f32[4,128,256]{2,1,0:T(8,128)S(1)}) custom-call(bf16[256,1024]{1,0:T(8,128)(2,1)S(1)} %get-tuple-element.28.q_ref.refs_0_, bf16[256,1024]{1,0:T(8,128)(2,1)S(1)} %get-tuple-element.31.g_ref.refs_3_, ...), custom_call_target="tpu_custom_call" | custom-call | flops 1000 | bytes 1000 | tf_op jit(solution)/shard_map/rim_grads/pallas_call | solution.py:237
  46.1 0.0 copy-start.3
  46.1 0.8 %copy-done.3 = f32[4,128,256]{2,1,0:T(8,128)} copy-done((f32[4,128,256]{2,1,0:T(8,128)}, f32[4,128,256]{2,1,0:T(8,128)S(1)}, u32[]{:S(2)}) %copy-start.3) | copy-done | bytes 524312
  46.8 0.0 copy-start.12
  46.9 0.6 copy-done.12
  47.5 0.0 copy-start.16
  47.5 0.7 copy-done.16
  48.2 0.0 all-gather.7.cloned.1.call-update
  48.2 2.2 %collective-permute-start.1 = (bf16[2,192,512]{2,1,0:T(8,128)(2,1)}, bf16[2,192,512]{2,1,0:T(8,128)(2,1)S(1)}, u32[]{:S(2)}, u32[]{:S(2)}) collective-permute-start(bf16[2,192,512]{2,1,0:T(8,128)(2,1)} %copy-done.17), channel_id=1, source_target_pairs={{1,2},{3,4},{5,6},{7,8},{9,10},{11,12},{13,14},{15,16},{17,18},{19... | collective-permute-start | bytes 1179656 | tf_op jit(solution)/shard_map/ppermute | solution.py:88
  50.4 3.4 %collective-permute-start.3 = (bf16[2,192,512]{2,1,0:T(8,128)(2,1)}, bf16[2,192,512]{2,1,0:T(8,128)(2,1)S(1)}, u32[]{:S(2)}, u32[]{:S(2)}) collective-permute-start(bf16[2,192,512]{2,1,0:T(8,128)(2,1)} %copy-done.16), channel_id=1, source_target_pairs={{1,2},{3,4},{5,6},{7,8},{9,10},{11,12},{13,14},{15,16},{17,18},{19... | collective-permute-start | bytes 1179656 | tf_op jit(solution)/shard_map/ppermute | solution.py:88
  53.8 3.7 %collective-permute-done.1.refs_7_ = bf16[2,192,512]{2,1,0:T(8,128)(2,1)S(1)} collective-permute-done((bf16[2,192,512]{2,1,0:T(8,128)(2,1)}, bf16[2,192,512]{2,1,0:T(8,128)(2,1)S(1)}, u32[]{:S(2)}, u32[]{:S(2)}) %collective-permute-start.1) | collective-permute-done | bytes 393248 | tf_op jit(solution)/shard_map/ppermute | solution.py:88
  57.5 0.0 copy-start.4
  57.5 1.0 %copy-done.4 = f32[4,128,256]{2,1,0:T(8,128)S(1)} copy-done((f32[4,128,256]{2,1,0:T(8,128)S(1)}, f32[4,128,256]{2,1,0:T(8,128)}, u32[]{:S(2)}) %copy-start.4) | copy-done | bytes 524312
  58.6 0.0 copy-start.13
  58.6 0.8 copy-done.13
  59.3 2.0 %held_grads.1 = (bf16[256,1024]{1,0:T(8,128)(2,1)}, f32[256,512]{1,0:T(8,128)S(1)}, f32[256,512]{1,0:T(8,128)S(1)}) custom-call(bf16[256,1024]{1,0:T(8,128)(2,1)S(1)} %get-tuple-element.28.q_ref.refs_0_, bf16[256,1024]{1,0:T(8,128)(2,1)S(1)} %get-tuple-element.29.k_ref.refs_1_, bf16[256,1024]{1,0:T(8,128)(2,1)S(1)} %get-tuple-element.30.v_ref.refs_2_, ...), custom_call_target="tpu_custom_call" | custom-call | flops 1000 | bytes 1000 | tf_op jit(solution)/shard_map/held_grads/pallas_call | solution.py:237
  61.4 0.0 copy-start.5
  61.4 0.8 %copy-done.5 = f32[256,512]{1,0:T(8,128)} copy-done((f32[256,512]{1,0:T(8,128)}, f32[256,512]{1,0:T(8,128)S(1)}, u32[]{:S(2)}) %copy-start.5) | copy-done | bytes 524312
  62.2 0.0 copy-start.7
  62.2 0.8 %copy-done.7 = f32[256,512]{1,0:T(8,128)} copy-done((f32[256,512]{1,0:T(8,128)}, f32[256,512]{1,0:T(8,128)S(1)}, u32[]{:S(2)}) %copy-start.7) | copy-done | bytes 524312
  63.0 4.7 %all-gather.7.cloned.1.call-done = bf16[4,2,192,512]{3,2,1,0:T(8,128)(2,1)} async-done(((bf16[2,2,192,512]{3,2,1,0:T(8,128)(2,1)}), bf16[4,2,192,512]{3,2,1,0:T(8,128)(2,1)}) %all-gather.7.cloned.1.call-update) | async-done | bytes 1572880 | tf_op jit(solution)/shard_map/all_gather | solution.py:95
  67.6 0.0 copy-start.2
  67.6 1.4 %copy-done.2 = bf16[4,2,192,512]{3,2,1,0:T(8,128)(2,1)S(1)} copy-done((bf16[4,2,192,512]{3,2,1,0:T(8,128)(2,1)S(1)}, bf16[4,2,192,512]{3,2,1,0:T(8,128)(2,1)}, u32[]{:S(2)}) %copy-start.2) | copy-done | bytes 1572888
  69.0 0.0 copy-start.6
  69.0 0.0 copy-start.8
  69.0 2.1 %done_grads.1 = (bf16[256,1024]{1,0:T(8,128)(2,1)}, bf16[256,1024]{1,0:T(8,128)(2,1)}, bf16[256,1024]{1,0:T(8,128)(2,1)}) custom-call(bf16[256,1024]{1,0:T(8,128)(2,1)S(1)} %get-tuple-element.28.q_ref.refs_0_, bf16[256,1024]{1,0:T(8,128)(2,1)S(1)} %get-tuple-element.29.k_ref.refs_1_, ...), custom_call_target="tpu_custom_call", output_to_operand_aliasing={{0}: (9, {})} | custom-call | flops 1000 | bytes 1000 | tf_op jit(solution)/shard_map/done_grads/pallas_call | solution.py:237
  71.2 0.0 collective-permute-done.3.gx_ref
  71.2 0.0 copy-done.6
  71.2 0.0 copy-done.8
  71.2 0.9 %add_rims.1 = (bf16[256,1024]{1,0:T(8,128)(2,1)}, bf16[256,1024]{1,0:T(8,128)(2,1)}) custom-call(f32[256,512]{1,0:T(8,128)S(1)} %copy-done.6, f32[256,512]{1,0:T(8,128)S(1)} %copy-done.8, bf16[2,192,512]{2,1,0:T(8,128)(2,1)S(1)} %collective-permute-done.3.gx_ref, ...), custom_call_target="tpu_custom_call", output_to_operand_aliasing={{0}: (4, {}), {1}: (5, {})} | custom-call | flops 1000 | bytes 1000 | tf_op jit(solution)/shard_map/add_rims/pallas_call | solution.py:237
Async XLA Ops:
  7.2 2.5 %copy-start.15 = (s32[8]{0:T(128)S(1)}, s32[8]{0:T(128)}, u32[]{:S(2)}) copy-start(s32[8]{0:T(128)} %live_ref.1) | copy-start | bytes 100
  7.2 2.5 %copy-start.14 = (s32[8,14]{1,0:T(8,128)S(1)}, s32[8,14]{1,0:T(8,128)}, u32[]{:S(2)}) copy-start(s32[8,14]{1,0:T(8,128)} %lists_ref.1) | copy-start | bytes 1348
  7.2 30.7 %all-gather.5.cloned.1.call-start = ((), (), s32[]{:S(2)}) async-start(), calls=%async_computation | async-start | bytes 2359296 | tf_op jit(solution)/shard_map/all_gather | solution.py:95
  12.2 0.6 copy-start.9
  12.9 54.8 %all-gather.7.cloned.1.call-start = ((), (), s32[]{:S(2)}) async-start(), calls=%async_computation.1 | async-start | bytes 2359296 | tf_op jit(solution)/shard_map/all_gather | solution.py:95
  12.9 10.0 %collective-permute-start = (bf16[2,192,512]{2,1,0:T(8,128)(2,1)S(1)}, bf16[2,192,512]{2,1,0:T(8,128)(2,1)S(1)}, u32[]{:S(2)}, u32[]{:S(2)}) collective-permute-start(bf16[2,192,512]{2,1,0:T(8,128)(2,1)S(1)} %get-tuple-element.33), channel_id=1, source_target_pairs={{1,2},{3,4},{5,6},{7,8},{9,10},{11,12},{13,14},{15,16},{17,18},{19... | collective-permute-start | bytes 1179656 | tf_op jit(solution)/shard_map/ppermute | solution.py:88
  17.5 25.5 %collective-permute-start.2 = (bf16[2,192,512]{2,1,0:T(8,128)(2,1)}, bf16[2,192,512]{2,1,0:T(8,128)(2,1)S(1)}, u32[]{:S(2)}, u32[]{:S(2)}) collective-permute-start(bf16[2,192,512]{2,1,0:T(8,128)(2,1)} %get-tuple-element.39), channel_id=1, source_target_pairs={{1,2},{3,4},{5,6},{7,8},{9,10},{11,12},{13,14},{15,16},{17,18},{19... | collective-permute-start | bytes 1179656 | tf_op jit(solution)/shard_map/ppermute | solution.py:88
  37.9 1.4 %copy-start = (bf16[4,192,1024]{2,1,0:T(8,128)(2,1)S(1)}, bf16[4,192,1024]{2,1,0:T(8,128)(2,1)}, u32[]{:S(2)}) copy-start(bf16[4,192,1024]{2,1,0:T(8,128)(2,1)} %all-gather.5.cloned.1.call-done) | copy-start | bytes 4718596
  39.3 0.8 %copy-start.10 = (f32[8,8,256]{2,1,0:T(8,128)S(1)}, f32[8,8,256]{2,1,0:T(8,128)}, u32[]{:S(2)}) copy-start(f32[8,8,256]{2,1,0:T(8,128)} %copy-done.9) | copy-start | bytes 196612
  40.2 2.9 %copy-start.1 = (bf16[4,192,1024]{2,1,0:T(8,128)(2,1)S(1)}, bf16[4,192,1024]{2,1,0:T(8,128)(2,1)}, u32[]{:S(2)}) copy-start(bf16[4,192,1024]{2,1,0:T(8,128)(2,1)} %all-gather.5.cloned.1.call-done) | copy-start | bytes 4718596
  40.2 2.9 %copy-start.11 = (f32[8,8,256]{2,1,0:T(8,128)S(1)}, f32[8,8,256]{2,1,0:T(8,128)}, u32[]{:S(2)}) copy-start(f32[8,8,256]{2,1,0:T(8,128)} %copy-done.9) | copy-start | bytes 196612
  42.3 0.7 copy-start.17
  46.1 0.8 %copy-start.3 = (f32[4,128,256]{2,1,0:T(8,128)}, f32[4,128,256]{2,1,0:T(8,128)S(1)}, u32[]{:S(2)}) copy-start(f32[4,128,256]{2,1,0:T(8,128)S(1)} %get-tuple-element.43.refs_6_) | copy-start | bytes 1572868
  46.8 0.6 copy-start.12
  47.5 0.7 copy-start.16
  48.2 9.3 %collective-permute-start.1 = (bf16[2,192,512]{2,1,0:T(8,128)(2,1)}, bf16[2,192,512]{2,1,0:T(8,128)(2,1)S(1)}, u32[]{:S(2)}, u32[]{:S(2)}) collective-permute-start(bf16[2,192,512]{2,1,0:T(8,128)(2,1)} %copy-done.17), channel_id=1, source_target_pairs={{1,2},{3,4},{5,6},{7,8},{9,10},{11,12},{13,14},{15,16},{17,18},{19... | collective-permute-start | bytes 1179656 | tf_op jit(solution)/shard_map/ppermute | solution.py:88
  50.4 20.7 %collective-permute-start.3 = (bf16[2,192,512]{2,1,0:T(8,128)(2,1)}, bf16[2,192,512]{2,1,0:T(8,128)(2,1)S(1)}, u32[]{:S(2)}, u32[]{:S(2)}) collective-permute-start(bf16[2,192,512]{2,1,0:T(8,128)(2,1)} %copy-done.16), channel_id=1, source_target_pairs={{1,2},{3,4},{5,6},{7,8},{9,10},{11,12},{13,14},{15,16},{17,18},{19... | collective-permute-start | bytes 1179656 | tf_op jit(solution)/shard_map/ppermute | solution.py:88
  57.5 1.0 %copy-start.4 = (f32[4,128,256]{2,1,0:T(8,128)S(1)}, f32[4,128,256]{2,1,0:T(8,128)}, u32[]{:S(2)}) copy-start(f32[4,128,256]{2,1,0:T(8,128)} %copy-done.3) | copy-start | bytes 1572868
  58.6 0.8 copy-start.13
  61.4 0.8 %copy-start.5 = (f32[256,512]{1,0:T(8,128)}, f32[256,512]{1,0:T(8,128)S(1)}, u32[]{:S(2)}) copy-start(f32[256,512]{1,0:T(8,128)S(1)} %get-tuple-element.46.pk_ref) | copy-start | bytes 1572868
  62.2 0.8 %copy-start.7 = (f32[256,512]{1,0:T(8,128)}, f32[256,512]{1,0:T(8,128)S(1)}, u32[]{:S(2)}) copy-start(f32[256,512]{1,0:T(8,128)S(1)} %get-tuple-element.47.pv_ref) | copy-start | bytes 1572868
  67.6 1.4 %copy-start.2 = (bf16[4,2,192,512]{3,2,1,0:T(8,128)(2,1)S(1)}, bf16[4,2,192,512]{3,2,1,0:T(8,128)(2,1)}, u32[]{:S(2)}) copy-start(bf16[4,2,192,512]{3,2,1,0:T(8,128)(2,1)} %all-gather.7.cloned.1.call-done) | copy-start | bytes 4718596
  69.0 2.2 %copy-start.6 = (f32[256,512]{1,0:T(8,128)S(1)}, f32[256,512]{1,0:T(8,128)}, u32[]{:S(2)}) copy-start(f32[256,512]{1,0:T(8,128)} %copy-done.5) | copy-start | bytes 1572868
  69.0 2.2 %copy-start.8 = (f32[256,512]{1,0:T(8,128)S(1)}, f32[256,512]{1,0:T(8,128)}, u32[]{:S(2)}) copy-start(f32[256,512]{1,0:T(8,128)} %copy-done.7) | copy-start | bytes 1572868
Sparse Core Ops, SparseCore 0:
  13.0 24.8 all-gather.4
  48.4 19.2 all-gather.6

commit v2 on v1

--- a/solution.py
+++ b/solution.py
@@ -16,9 +16,18 @@
 NEG = -1e30
 FLOOR = -1e20
 MIB = 1024 * 1024
-LOAD_LIMIT = 51.2
-GATHER = True
+LOAD_LIMIT = 51.1
 SPLIT = 4
+MEGA = 10**6
+WEIGHT = {
+    "load_bands": 1,
+    "pack_leads": 1,
+    "first_stats": 11000,
+    "rim_grads": 1,
+    "held_grads": 11000,
+    "done_grads": 11000,
+    "add_rims": 1,
+}
 
 
 def nt(a, b):
@@ -89,18 +98,14 @@
 
 
 def swap_inside(x):
-    if not GATHER:
-        return lax.ppermute(x, "band", [(at, at ^ 1) for at in range(lax.axis_size("band"))])
-    pairs = [[at, at + 1] for at in range(0, lax.axis_size("band"), 2)]
-    return lax.all_gather(x, "band", axis_index_groups=pairs)
-
-
-def load_kernel(
-    k_ref, v_ref, q_ref, g_ref, lead_ref, k_out, v_out, q_out, g_out, sems
-):
-    tok = k_ref.shape[0]
-    lead = lead_ref.shape[2]
-    moves = [(src.at[pl.ds(0, RIM), pl.ds(0, lead)], lead_ref.at[at]) for at, src in enumerate((k_ref, v_ref))]
+    return lax.ppermute(x, "band", [(at, at ^ 1) for at in range(lax.axis_size("band"))])
+
+
+def load_kernel(k_ref, v_ref, q_ref, g_ref, lead_a_ref, lead_b_ref, k_out, v_out, q_out, g_out, sems):
+    moves = []
+    for lead, first in ((lead_a_ref, 0), (lead_b_ref, k_ref.shape[1] - lead_b_ref.shape[2])):
+        for at, src in enumerate((k_ref, v_ref)):
+            moves.append((src.at[pl.ds(0, RIM), pl.ds(first, lead.shape[2])], lead.at[at]))
     moves += [(k_ref, k_out), (v_ref, v_out), (q_ref, q_out), (g_ref, g_out)]
     copies = [pltpu.make_async_copy(src, dst, sems.at[at]) for at, (src, dst) in enumerate(moves)]
     for copy in copies:
@@ -109,16 +114,15 @@
         copy.wait()
 
 
-def own_kernel(
-    count_ref, live_ref, lists_ref, q_ref, k_ref, v_ref, g_ref, table_ref, stats_ref, lead_b_ref, lead_i_ref
-):
-    tok = q_ref.shape[0]
+def pack_kernel(count_ref, live_ref, lists_ref, k_ref, v_ref, table_ref, lead_ref):
+    tok = k_ref.shape[0]
+    for at, ref in enumerate((k_ref, v_ref)):
+        lead_ref[at] = ref[:RIM, :]
     blocks = lists_ref.shape[0]
-    count = count_ref[0]
-    row = lax.broadcasted_iota(jnp.int32, (blocks, 1), 0)
-    live = jnp.zeros_like(row)
-    for n in range(blocks):
-        live = jnp.where(row == n, live_ref[n], live)
+    count = count_ref[...]
+    row = lax.broadcasted_iota(jnp.int32, (blocks, blocks), 0)
+    lane = lax.broadcasted_iota(jnp.int32, (blocks, blocks), 1)
+    live = jnp.sum(jnp.where(row == lane, live_ref[...], 0), axis=1, keepdims=True)
     odd = lax.axis_index("band") % 2
     slot = lax.broadcasted_iota(jnp.int32, (blocks, TABLE), 1)
     x_first = 8 + RB * odd
@@ -130,25 +134,26 @@
     past = lax.broadcasted_iota(jnp.int32, (tok - RIM, tok), 0) + RIM >= count
     tail = [jnp.broadcast_to(table[at : at + 1], (BLK, tok)) for at in range(RB, tok // BLK)]
     table_ref[TABLE:] = jnp.where(past, NEG, jnp.concatenate(tail, axis=0))
-    for h in range(HEADS):
+
+
+def first_kernel(q_ref, k_ref, v_ref, g_ref, x_ref, table_ref, stats_ref):
+    tok = q_ref.shape[0]
+    for h in range(stats_ref.shape[0]):
         q, k, v, g = (ref[:, cols(h)] for ref in (q_ref, k_ref, v_ref, g_ref))
-        for at, lead in enumerate((k, v)):
-            lead_i_ref[at, :, cols(h)] = lead[:RIM]
-            if h >= SPLIT:
-                lead_b_ref[at, :, cols(h - SPLIT)] = lead[:RIM]
-        x = own_score(k, q, table_ref)
-        top, total, raw = stats_of(x, nt(v, g))
-        stats_ref[h] = jnp.concatenate([top, total, raw, jnp.zeros((5, tok), jnp.float32)], axis=0)
-
-
-def rim_kernel(first, q_ref, g_ref, x_ref, i_ref, table_ref, stats_ref, *refs):
+        own = stats_of(own_score(k, q, table_ref), nt(v, g))
+        rim = stats_of(biased(nt(x_ref[0, :, cols(h)], q), table_ref, 8), nt(x_ref[1, :, cols(h)], g))
+        stats_ref[h] = jnp.concatenate(merged(own, rim) + (jnp.zeros((5, tok), jnp.float32),), axis=0)
+
+
+def rim_kernel(first, q_ref, g_ref, x_ref, i_ref, table_ref, *refs):
     gx_ref, gi_ref, final_ref, dq_ref = refs[-4:]
-    if GATHER:
-        i_ref = i_ref.at[1 - lax.axis_index("band") % 2]
     tok = q_ref.shape[0]
     if first:
-        gi_ref[0] = refs[0][...]
+        k_ref, v_ref, before = refs[:3]
+        gi_ref[0] = before[...]
         gi_ref = gi_ref.at[1]
+    else:
+        stats_ref = refs[0]
     for at in range(x_ref.shape[2] // DEPTH):
         h = first + at
         q, g = q_ref[:, cols(h)], g_ref[:, cols(h)]
@@ -156,8 +161,12 @@
         prod_x = nt(x_ref[1, :, cols(at)], g)
         score_i = biased(nt(i_ref[0, :, cols(h)], q), table_ref, 8 + RB)
         prod_i = nt(i_ref[1, :, cols(h)], g)
-        own = (stats_ref[h, 0:1], stats_ref[h, 1:2], stats_ref[h, 2:3])
-        top, total, raw = merged(own, merged(stats_of(score_x, prod_x), stats_of(score_i, prod_i)))
+        if first:
+            own = stats_of(own_score(k_ref[:, cols(h)], q, table_ref), nt(v_ref[:, cols(h)], g))
+            known = merged(own, stats_of(score_x, prod_x))
+        else:
+            known = (stats_ref[h, 0:1], stats_ref[h, 1:2], stats_ref[h, 2:3])
+        top, total, raw = merged(known, stats_of(score_i, prod_i))
         inv = jnp.where(total > 0.0, 1.0 / jnp.where(total > 0.0, total, 1.0), 0.0)
         delta = raw * inv
         w, ds = grads_of(score_x, prod_x, top, inv, delta)
@@ -195,8 +204,6 @@
 
 def done_kernel(first, *refs):
     gx_ref, gi_ref, _, dq_ref, dk_ref, dv_ref, dq_buf, dk_buf, dv_buf, sems = refs[7:]
-    if GATHER:
-        gi_ref = gi_ref.at[1 - lax.axis_index("band") % 2]
     copies = []
     for at in range(dq_buf.shape[1] // DEPTH):
         dq, dk, dv = rest_of(first, at, *refs[:7])
@@ -214,8 +221,6 @@
 
 def add_kernel(first, pk_ref, pv_ref, gx_ref, gi_ref, _k, _v, dk_ref, dv_ref, dk_buf, dv_buf, sems):
     width = pk_ref.shape[1]
-    if GATHER:
-        gi_ref = gi_ref.at[1 - lax.axis_index("band") % 2]
     copies = []
     for slot, (own, buf, out) in enumerate(((pk_ref, dk_buf, dk_ref), (pv_ref, dv_buf, dv_ref))):
         lead = gx_ref[slot].astype(jnp.float32) + gi_ref[1, slot].astype(jnp.float32)
@@ -228,7 +233,6 @@
 
 
 VMEM = pl.BlockSpec(memory_space=pltpu.VMEM)
-SMEM = pl.BlockSpec(memory_space=pltpu.SMEM)
 HBM = pl.BlockSpec(memory_space=pltpu.HBM)
 ANY = pl.BlockSpec(memory_space=pl.ANY)
 
@@ -242,7 +246,7 @@
         scratch_shapes=scratch,
         input_output_aliases=alias or {},
         compiler_params=pltpu.CompilerParams(vmem_limit_bytes=int(limit * MIB)),
-        cost_estimate=pl.CostEstimate(flops=1000, bytes_accessed=1000, transcendentals=0),
+        cost_estimate=pl.CostEstimate(flops=WEIGHT[name] * MEGA, bytes_accessed=1000, transcendentals=0),
         name=name,
     )(*args)
 
@@ -256,43 +260,45 @@
     f32 = functools.partial(shape, dtype=jnp.float32)
     cuts = ((0, SPLIT), (SPLIT, HEADS))
     part = HEADS - SPLIT
-    lead_a, k, v, q, g = call(
+    lead_a, lead_b, k, v, q, g = call(
         load_kernel,
         "load_bands",
         [HBM] * 4,
-        [shape(2, RIM, SPLIT * DEPTH)] + [shape(tok, width)] * 4,
+        [shape(2, RIM, SPLIT * DEPTH), shape(2, RIM, part * DEPTH)] + [shape(tok, width)] * 4,
+        [VMEM] * 6,
+        (keys, values, queries, out_grad),
+        [pltpu.SemaphoreType.DMA((8,))],
+        limit=LOAD_LIMIT,
+    )
+    x_a, x_b = swap_across(lead_a), swap_across(lead_b)
+    table, lead_i = call(
+        pack_kernel,
+        "pack_leads",
         [VMEM] * 5,
-        (keys, values, queries, out_grad),
-        [pltpu.SemaphoreType.DMA((6,))],
-        limit=LOAD_LIMIT,
-    )
-    x_a = swap_across(lead_a)
-    table, stats, lead_b, lead_i = call(
-        own_kernel,
-        "own_stats",
-        [SMEM] * 2 + [VMEM] * 5,
-        [f32(TABLE + tok - RIM, tok), f32(HEADS, 8, tok), shape(2, RIM, part * DEPTH), shape(2, RIM, width)],
-        [VMEM] * 4,
-        (band_counts, slot_counts, block_lists, q, k, v, g),
-    )
-    x_b = swap_across(lead_b)
+        [f32(TABLE + tok - RIM, tok), shape(2, RIM, width)],
+        [VMEM] * 2,
+        (band_counts[:, None], slot_counts[None], block_lists, k, v),
+    )
     i = swap_inside(lead_i)
+    stats_a = call(
+        first_kernel, "first_stats", [VMEM] * 6, f32(SPLIT, 8, tok), VMEM, (q, k, v, g, x_a, table)
+    )
 
     def rim(first, x, *more):
         heads = x.shape[2] // DEPTH
-        gi = (2, 2, RIM, x.shape[2]) if more else x.shape
+        gi = (2, 2, RIM, x.shape[2]) if first else x.shape
         return call(
             functools.partial(rim_kernel, first),
             "rim_grads",
-            [VMEM] * (6 + len(more)),
+            [VMEM] * (5 + len(more)),
             [shape(*x.shape), shape(*gi), f32(heads, 8, tok), f32(heads, DEPTH, tok)],
             [VMEM] * 4,
-            (q, g, x, i, table, stats) + more,
+            (q, g, x, i, table) + more,
         )
 
-    gx_a, gi_a, final_a, dq_a = rim(0, x_a)
+    gx_a, gi_a, final_a, dq_a = rim(0, x_a, stats_a)
     gx_a = swap_across(gx_a)
-    gx_b, gi, final_b, dq_b = rim(SPLIT, x_b, gi_a)
+    gx_b, gi, final_b, dq_b = rim(SPLIT, x_b, k, v, gi_a)
     gx_b = swap_across(gx_b)
     gi = swap_inside(gi)
 

time: 79.4 us -> 38.1 us (0.48)
  the two profiles are of different devices: /device:TPU:1 before, /device:TPU:454 now
where the time goes in v2:
time: 38.1 us; the launch traced here: 37.7 us
  starting transfers between devices  19.2 us (50%)
  Pallas kernels  13 us (34%)
  waiting for transfers between devices  3.52 us (9%)
  between operations  1.41 us (4%)
  local copies, waits for them, and re-layouts  0.68 us (2%)
    ppermute x4, starting transfers between devices, swap_across(): return lax.ppermute(x, 'band', pairs + [(b, a) for a, b in pairs])  15.3 us
    pallas_call x8, Pallas kernels, call(): pl.pallas_call(body, in_specs=ins, out_specs=out_specs, out_shape=outs, s...  13 us
    ppermute x2, starting transfers between devices, swap_inside(): lax.ppermute(x, 'band', [(at, at ^ 1) for at in range(lax.axis_size('band...  3.84 us
    ppermute x4, waiting for transfers between devices, swap_across(): return lax.ppermute(x, 'band', pairs + [(b, a) for a, b in pairs])  2.01 us
    ppermute x2, waiting for transfers between devices, swap_inside(): lax.ppermute(x, 'band', [(at, at ^ 1) for at in range(lax.axis_size('band...  1.51 us
  transfers between devices with their start and end apart: 6, of which 3 were waited for; matrix products, arithmetic and copies ran while one was open for 0% of the time, Pallas kernels for 27%

profile of v2, /device:TPU:454, one launch (start us, length us, event | category | flops | bytes accessed | tf_op | source)
XLA Modules:
  0.0 37.7 jit_solution(15723100335040403831)
XLA Ops:
  0.6 1.9 %load_bands.1 = (bf16[2,192,512]{2,1,0:T(8,128)(2,1)S(1)}, bf16[2,192,512]{2,1,0:T(8,128)(2,1)S(1)}, bf16[256,1024]{1,0:T(8,128)(2,1)S(1)}, bf16[256,1024]{1,0:T...) custom-call(bf16[256,1024]{1,0:T(8,128)(2,1)} %k_ref.1, bf16[256,1024]{1,0:T(8,128)(2,1)} %v_ref.1, ...), custom_call_target="tpu_custom_call" | custom-call | flops 1000000 | bytes 1000 | tf_op jit(solution)/shard_map/load_bands/pallas_call | solution.py:241
  2.6 4.8 %collective-permute-start = (bf16[2,192,512]{2,1,0:T(8,128)(2,1)S(1)}, bf16[2,192,512]{2,1,0:T(8,128)(2,1)S(1)}, u32[]{:S(2)}, u32[]{:S(2)}) collective-permute-start(bf16[2,192,512]{2,1,0:T(8,128)(2,1)S(1)} %get-tuple-element.32), channel_id=1, source_target_pairs={{1,2},{3,4},{5,6},{7,8},{9,10},{11,12},{13,14},{15,16},{17,18},{19... | collective-permute-start | bytes 1179656 | tf_op jit(solution)/shard_map/ppermute | solution.py:97
  7.4 2.9 %collective-permute-start.3 = (bf16[2,192,512]{2,1,0:T(8,128)(2,1)S(1)}, bf16[2,192,512]{2,1,0:T(8,128)(2,1)S(1)}, u32[]{:S(2)}, u32[]{:S(2)}) collective-permute-start(bf16[2,192,512]{2,1,0:T(8,128)(2,1)S(1)} %get-tuple-element.37), channel_id=1, source_target_pairs={{1,2},{3,4},{5,6},{7,8},{9,10},{11,12},{13,14},{15,16},{17,18},{19... | collective-permute-start | bytes 1179656 | tf_op jit(solution)/shard_map/ppermute | solution.py:97
  10.9 0.0 copy-start
  10.9 0.0 copy-start.1
  10.9 0.7 %copy-done = s32[8,14]{1,0:T(8,128)S(1)} copy-done((s32[8,14]{1,0:T(8,128)S(1)}, s32[8,14]{1,0:T(8,128)}, u32[]{:S(2)}) %copy-start) | copy-done | bytes 472
  11.6 0.0 copy-done.1
  11.6 0.3 pack_leads.1
  11.9 1.9 %collective-permute-start.1 = (bf16[2,192,1024]{2,1,0:T(8,128)(2,1)S(1)}, bf16[2,192,1024]{2,1,0:T(8,128)(2,1)S(1)}, u32[]{:S(2)}, u32[]{:S(2)}) collective-permute-start(bf16[2,192,1024]{2,1,0:T(8,128)(2,1)S(1)} %get-tuple-element.33), channel_id=1, source_target_pairs={{0,1},{1,0},{2,3},{3,2},{4,5},{5,4},{6,7},{7,6},{8,9},{9,8},{10,11... | collective-permute-start | bytes 2359304 | tf_op jit(solution)/shard_map/ppermute | solution.py:101
  13.8 0.0 collective-permute-done.x_ref
  13.9 0.9 %first_stats.1.refs_0_ = f32[4,8,256]{2,1,0:T(8,128)S(1)} custom-call(bf16[256,1024]{1,0:T(8,128)(2,1)S(1)} %get-tuple-element.27.q_ref.refs_0_, bf16[256,1024]{1,0:T(8,128)(2,1)S(1)} %get-tuple-element.28.k_ref.refs_0_.refs_1_, bf16[256,1024]{1,0:T(8,128)(2,1)S(1)} %get-tuple-element.29.v_ref.refs_1_.refs_2_, ...), custom_call_target="tpu_custom_call" | custom-call | flops 11000000512 | bytes 1000 | tf_op jit(solution)/shard_map/first_stats/pallas_call | solution.py:241
  14.8 1.3 %collective-permute-done.1.i_ref = bf16[2,192,1024]{2,1,0:T(8,128)(2,1)S(1)} collective-permute-done((bf16[2,192,1024]{2,1,0:T(8,128)(2,1)S(1)}, bf16[2,192,1024]{2,1,0:T(8,128)(2,1)S(1)}, u32[]{:S(2)}, u32[]{:S(2)}) %collective-permute-start.1) | collective-permute-done | bytes 786464 | tf_op jit(solution)/shard_map/ppermute | solution.py:101
  16.1 2.2 %rim_grads.2 = (bf16[2,192,512]{2,1,0:T(8,128)(2,1)S(1)}, bf16[2,192,512]{2,1,0:T(8,128)(2,1)S(1)}, f32[4,8,256]{2,1,0:T(8,128)S(1)}, f32[4,128,256]{2,1,0:T(8,128)S(1)}) custom-call(bf16[256,1024]{1,0:T(8,128)(2,1)S(1)} %get-tuple-element.27.q_ref.refs_0_, bf16[256,1024]{1,0:T(8,128)(2,1)S(1)} %get-tuple-element.30.g_ref.refs_3_, ...), custom_call_target="tpu_custom_call" | custom-call | flops 1000000 | bytes 1000 | tf_op jit(solution)/shard_map/rim_grads/pallas_call | solution.py:241
  18.3 4.8 %collective-permute-start.2 = (bf16[2,192,512]{2,1,0:T(8,128)(2,1)S(1)}, bf16[2,192,512]{2,1,0:T(8,128)(2,1)S(1)}, u32[]{:S(2)}, u32[]{:S(2)}) collective-permute-start(bf16[2,192,512]{2,1,0:T(8,128)(2,1)S(1)} %get-tuple-element.36), channel_id=1, source_target_pairs={{1,2},{3,4},{5,6},{7,8},{9,10},{11,12},{13,14},{15,16},{17,18},{19... | collective-permute-start | bytes 1179656 | tf_op jit(solution)/shard_map/ppermute | solution.py:97
  23.1 0.0 collective-permute-done.3.x_ref
  23.1 2.6 %rim_grads.3 = (bf16[2,192,512]{2,1,0:T(8,128)(2,1)S(1)}, bf16[2,2,192,512]{3,2,1,0:T(8,128)(2,1)S(1)}, f32[4,8,256]{2,1,0:T(8,128)S(1)}, f32[4,128,256]{2,1,0:T(8,128)S(1)}) custom-call(bf16[256,1024]{1,0:T(8,128)(2,1)S(1)} %get-tuple-element.27.q_ref.refs_0_, bf16[256,1024]{1,0:T(8,128)(2,1)S(1)} %get-tuple-element.30.g_ref.refs_3_, ...), custom_call_target="tpu_custom_call" | custom-call | flops 1000000 | bytes 1000 | tf_op jit(solution)/shard_map/rim_grads/pallas_call | solution.py:241
  25.7 2.9 %collective-permute-start.5 = (bf16[2,192,512]{2,1,0:T(8,128)(2,1)S(1)}, bf16[2,192,512]{2,1,0:T(8,128)(2,1)S(1)}, u32[]{:S(2)}, u32[]{:S(2)}) collective-permute-start(bf16[2,192,512]{2,1,0:T(8,128)(2,1)S(1)} %get-tuple-element.46), channel_id=1, source_target_pairs={{1,2},{3,4},{5,6},{7,8},{9,10},{11,12},{13,14},{15,16},{17,18},{19... | collective-permute-start | bytes 1179656 | tf_op jit(solution)/shard_map/ppermute | solution.py:97
  28.5 1.9 %collective-permute-start.4 = (bf16[2,2,192,512]{3,2,1,0:T(8,128)(2,1)S(1)}, bf16[2,2,192,512]{3,2,1,0:T(8,128)(2,1)S(1)}, u32[]{:S(2)}, u32[]{:S(2)}) collective-permute-start(bf16[2,2,192,512]{3,2,1,0:T(8,128)(2,1)S(1)} %get-tuple-element.39), channel_id=1, source_target_pairs={{0,1},{1,0},{2,3},{3,2},{4,5},{5,4},{6,7},{7,6},{8,9},{9,8},{10,11... | collective-permute-start | bytes 2359304 | tf_op jit(solution)/shard_map/ppermute | solution.py:101
  30.5 0.0 collective-permute-done.2.refs_7_
  30.5 2.0 %held_grads.1 = (bf16[256,1024]{1,0:T(8,128)(2,1)}, f32[256,512]{1,0:T(8,128)S(1)}, f32[256,512]{1,0:T(8,128)S(1)}) custom-call(bf16[256,1024]{1,0:T(8,128)(2,1)S(1)} %get-tuple-element.27.q_ref.refs_0_, bf16[256,1024]{1,0:T(8,128)(2,1)S(1)} %get-tuple-element.28.k_ref.refs_0_.refs_1_, bf16[256,1024]{1,0:T(8,128)(2,1)S(1)} %get-tuple-element.29.v_ref.refs_1_.refs_2_, ...), custom_call_target="tpu_custom_call" | custom-call | flops 11000000512 | bytes 1000 | tf_op jit(solution)/shard_map/held_grads/pallas_call | solution.py:241
  32.5 0.2 collective-permute-done.4.refs_8_.gi_ref
  32.7 2.1 %done_grads.1 = (bf16[256,1024]{1,0:T(8,128)(2,1)}, bf16[256,1024]{1,0:T(8,128)(2,1)}, bf16[256,1024]{1,0:T(8,128)(2,1)}) custom-call(bf16[256,1024]{1,0:T(8,128)(2,1)S(1)} %get-tuple-element.27.q_ref.refs_0_, bf16[256,1024]{1,0:T(8,128)(2,1)S(1)} %get-tuple-element.28.k_ref.refs_0_.refs_1_, ...), custom_call_target="tpu_custom_call", output_to_operand_aliasing={{0}: (9, {})} | custom-call | flops 11000000512 | bytes 1000 | tf_op jit(solution)/shard_map/done_grads/pallas_call | solution.py:241
  34.9 2.0 %collective-permute-done.5.gx_ref = bf16[2,192,512]{2,1,0:T(8,128)(2,1)S(1)} collective-permute-done((bf16[2,192,512]{2,1,0:T(8,128)(2,1)S(1)}, bf16[2,192,512]{2,1,0:T(8,128)(2,1)S(1)}, u32[]{:S(2)}, u32[]{:S(2)}) %collective-permute-start.5) | collective-permute-done | bytes 393248 | tf_op jit(solution)/shard_map/ppermute | solution.py:97
  36.9 0.9 %add_rims.1 = (bf16[256,1024]{1,0:T(8,128)(2,1)}, bf16[256,1024]{1,0:T(8,128)(2,1)}) custom-call(f32[256,512]{1,0:T(8,128)S(1)} %get-tuple-element.44.pk_ref, f32[256,512]{1,0:T(8,128)S(1)} %get-tuple-element.45.pv_ref, bf16[2,192,512]{2,1,0:T(8,128)(2,1)S(1)} %collective-permute-done.5.gx_ref, ...), custom_call_target="tpu_custom_call", output_to_operand_aliasing={{0}: (4, {}), {1}: (5, {})} | custom-call | flops 1000000 | bytes 1000 | tf_op jit(solution)/shard_map/add_rims/pallas_call | solution.py:241
Async XLA Ops:
  2.6 11.3 %collective-permute-start = (bf16[2,192,512]{2,1,0:T(8,128)(2,1)S(1)}, bf16[2,192,512]{2,1,0:T(8,128)(2,1)S(1)}, u32[]{:S(2)}, u32[]{:S(2)}) collective-permute-start(bf16[2,192,512]{2,1,0:T(8,128)(2,1)S(1)} %get-tuple-element.32), channel_id=1, source_target_pairs={{1,2},{3,4},{5,6},{7,8},{9,10},{11,12},{13,14},{15,16},{17,18},{19... | collective-permute-start | bytes 1179656 | tf_op jit(solution)/shard_map/ppermute | solution.py:97
  7.4 15.7 %collective-permute-start.3 = (bf16[2,192,512]{2,1,0:T(8,128)(2,1)S(1)}, bf16[2,192,512]{2,1,0:T(8,128)(2,1)S(1)}, u32[]{:S(2)}, u32[]{:S(2)}) collective-permute-start(bf16[2,192,512]{2,1,0:T(8,128)(2,1)S(1)} %get-tuple-element.37), channel_id=1, source_target_pairs={{1,2},{3,4},{5,6},{7,8},{9,10},{11,12},{13,14},{15,16},{17,18},{19... | collective-permute-start | bytes 1179656 | tf_op jit(solution)/shard_map/ppermute | solution.py:97
  10.9 0.7 %copy-start = (s32[8,14]{1,0:T(8,128)S(1)}, s32[8,14]{1,0:T(8,128)}, u32[]{:S(2)}) copy-start(s32[8,14]{1,0:T(8,128)} %lists_ref.1) | copy-start | bytes 1348
  10.9 0.7 %copy-start.1 = (s32[8]{0:T(128)S(1)}, s32[8]{0:T(128)}, u32[]{:S(2)}) copy-start(s32[8]{0:T(128)} %param.13) | copy-start | bytes 100
  11.9 4.2 %collective-permute-start.1 = (bf16[2,192,1024]{2,1,0:T(8,128)(2,1)S(1)}, bf16[2,192,1024]{2,1,0:T(8,128)(2,1)S(1)}, u32[]{:S(2)}, u32[]{:S(2)}) collective-permute-start(bf16[2,192,1024]{2,1,0:T(8,128)(2,1)S(1)} %get-tuple-element.33), channel_id=1, source_target_pairs={{0,1},{1,0},{2,3},{3,2},{4,5},{5,4},{6,7},{7,6},{8,9},{9,8},{10,11... | collective-permute-start | bytes 2359304 | tf_op jit(solution)/shard_map/ppermute | solution.py:101
  18.3 12.2 %collective-permute-start.2 = (bf16[2,192,512]{2,1,0:T(8,128)(2,1)S(1)}, bf16[2,192,512]{2,1,0:T(8,128)(2,1)S(1)}, u32[]{:S(2)}, u32[]{:S(2)}) collective-permute-start(bf16[2,192,512]{2,1,0:T(8,128)(2,1)S(1)} %get-tuple-element.36), channel_id=1, source_target_pairs={{1,2},{3,4},{5,6},{7,8},{9,10},{11,12},{13,14},{15,16},{17,18},{19... | collective-permute-start | bytes 1179656 | tf_op jit(solution)/shard_map/ppermute | solution.py:97
  25.7 11.2 %collective-permute-start.5 = (bf16[2,192,512]{2,1,0:T(8,128)(2,1)S(1)}, bf16[2,192,512]{2,1,0:T(8,128)(2,1)S(1)}, u32[]{:S(2)}, u32[]{:S(2)}) collective-permute-start(bf16[2,192,512]{2,1,0:T(8,128)(2,1)S(1)} %get-tuple-element.46), channel_id=1, source_target_pairs={{1,2},{3,4},{5,6},{7,8},{9,10},{11,12},{13,14},{15,16},{17,18},{19... | collective-permute-start | bytes 1179656 | tf_op jit(solution)/shard_map/ppermute | solution.py:97
  28.5 4.2 %collective-permute-start.4 = (bf16[2,2,192,512]{3,2,1,0:T(8,128)(2,1)S(1)}, bf16[2,2,192,512]{3,2,1,0:T(8,128)(2,1)S(1)}, u32[]{:S(2)}, u32[]{:S(2)}) collective-permute-start(bf16[2,2,192,512]{3,2,1,0:T(8,128)(2,1)S(1)} %get-tuple-element.39), channel_id=1, source_target_pairs={{0,1},{1,0},{2,3},{3,2},{4,5},{5,4},{6,7},{7,6},{8,9},{9,8},{10,11... | collective-permute-start | bytes 2359304 | tf_op jit(solution)/shard_map/ppermute | solution.py:101

commit v3 on v2

v3 whole, which is shorter than its diff:
```python
import functools
import jax
import jax.numpy as jnp
from jax import lax
from jax.experimental import pallas as pl
from jax.experimental.pallas import tpu as pltpu
from jax.sharding import PartitionSpec as P

HEADS = 8
DEPTH = 128
BLK = 32
RB = 6
RIM = RB * BLK
TABLE = 32
LOG2E = 1.4426950408889634
NEG = -1e30
FLOOR = -1e20
MIB = 1024 * 1024
LOAD_LIMIT = 53.14
SPLIT = 4
MEGA = 10**6
WEIGHT = {
    "load_bands": 5500,
    "pack_leads": 1,
    "own_stats": 1,
    "first_stats": 11000,
    "rim_grads": 1,
    "inside_grads": 1,
    "held_grads": 11000,
    "done_grads": 11000,
    "add_rims": 1,
}


def nt(a, b):
    return lax.dot_general(a, b, (((1,), (1,)), ((), ())), preferred_element_type=jnp.float32)


def tn(a, b):
    return lax.dot_general(a, b, (((0,), (0,)), ((), ())), preferred_element_type=jnp.float32)


def nn(a, b):
    return jnp.dot(a, b, preferred_element_type=jnp.float32)


def cols(h):
    return slice(h * DEPTH, (h + 1) * DEPTH)


def biased(score, bias, first):
    scaled = score * (DEPTH ** -0.5 * LOG2E)
    parts = [
        scaled[at * BLK : (at + 1) * BLK] + bias[first + at : first + at + 1, :]
        for at in range(score.shape[0] // BLK)
    ]
    return jnp.concatenate(parts, axis=0)


def table_of(lists, live, ids, count, tok):
    blocks, slots = lists.shape
    hit = jnp.zeros((blocks, ids.shape[1]), jnp.float32)
    for l in range(slots):
        hit = jnp.where((lists[:, l : l + 1] == ids) & (live > l), 1.0, hit)
    lane = lax.broadcasted_iota(jnp.int32, (blocks, tok), 1)
    row = lax.broadcasted_iota(jnp.int32, (blocks, tok), 0)
    spread = jnp.where((lane // BLK == row) & (lane < count), 1.0, 0.0)
    return jnp.where(tn(hit, spread) > 0.5, 0.0, NEG)


def own_score(k, q, bias):
    x = nt(k, q) * (DEPTH ** -0.5 * LOG2E)
    parts = [x[at * BLK : (at + 1) * BLK] + bias[at : at + 1, :] for at in range(RB)]
    return jnp.concatenate(parts + [x[RIM:] + bias[TABLE:, :]], axis=0)


def merged(a, b):
    top = jnp.maximum(a[0], b[0])
    fa, fb = jnp.exp2(a[0] - top), jnp.exp2(b[0] - top)
    return top, a[1] * fa + b[1] * fb, a[2] * fa + b[2] * fb


def held_of(x, prod, p_ref, prod_ref):
    top = jnp.maximum(jnp.max(x, axis=0, keepdims=True), FLOOR)
    p = jnp.exp2(x - top)
    p_ref[...] = p
    prod_ref[...] = prod
    return top, jnp.sum(p, axis=0, keepdims=True), jnp.sum(p * prod, axis=0, keepdims=True)


def rows_of(values):
    pad = jnp.zeros((8 - len(values), values[0].shape[1]), jnp.float32)
    return jnp.concatenate(tuple(values) + (pad,), axis=0)


def known(ref):
    return ref[0:1], ref[1:2], ref[2:3]


def grads_of(p, prod, factor, delta):
    w = (p * factor).astype(jnp.bfloat16)
    ds = (p * (factor * (DEPTH ** -0.5)) * (prod - delta)).astype(jnp.bfloat16)
    return w, ds


def swap_across(x):
    count = lax.axis_size("band")
    pairs = [(at, at + 1) for at in range(1, count - 1, 2)]
    return lax.ppermute(x, "band", pairs + [(b, a) for a, b in pairs])


def swap_inside(x):
    return lax.ppermute(x, "band", [(at, at ^ 1) for at in range(lax.axis_size("band"))])


def load_kernel(k_ref, v_ref, lead_a_ref, lead_b_ref, sems):
    moves = []
    for lead, first in ((lead_a_ref, 0), (lead_b_ref, k_ref.shape[1] - lead_b_ref.shape[2])):
        for at, src in enumerate((k_ref, v_ref)):
            moves.append((src.at[pl.ds(0, RIM), pl.ds(first, lead.shape[2])], lead.at[at]))
    copies = [pltpu.make_async_copy(src, dst, sems.at[at]) for at, (src, dst) in enumerate(moves)]
    for copy in copies:
        copy.start()
    for copy in copies:
        copy.wait()


def pack_kernel(k_ref, v_ref, lead_ref):
    for at, ref in enumerate((k_ref, v_ref)):
        lead_ref[at] = ref[:RIM, :]


def own_kernel(count_ref, live_ref, lists_ref, q_ref, k_ref, v_ref, g_ref, table_ref, stats_ref, p_ref, prod_ref):
    tok = q_ref.shape[0]
    blocks = lists_ref.shape[0]
    count = count_ref[...]
    row = lax.broadcasted_iota(jnp.int32, (blocks, blocks), 0)
    lane = lax.broadcasted_iota(jnp.int32, (blocks, blocks), 1)
    live = jnp.sum(jnp.where(row == lane, live_ref[...], 0), axis=1, keepdims=True)
    odd = lax.axis_index("band") % 2
    slot = lax.broadcasted_iota(jnp.int32, (blocks, TABLE), 1)
    x_first = 8 + RB * odd
    i_first = 8 + RB * (1 - odd)
    ids = jnp.where(slot < 8, slot, jnp.where(slot < 8 + RB, slot - 8 + x_first, slot - 8 - RB + i_first))
    ids = jnp.where(slot < 8 + 2 * RB, ids, -1)
    table = table_of(lists_ref[...], live, ids, count, tok)
    table_ref[:TABLE] = table
    past = lax.broadcasted_iota(jnp.int32, (tok - RIM, tok), 0) + RIM >= count
    tail = [jnp.broadcast_to(table[at : at + 1], (BLK, tok)) for at in range(RB, tok // BLK)]
    table_ref[TABLE:] = jnp.where(past, NEG, jnp.concatenate(tail, axis=0))
    for h in range(HEADS):
        q, k, v, g = (ref[:, cols(h)] for ref in (q_ref, k_ref, v_ref, g_ref))
        stats_ref[h] = rows_of(held_of(own_score(k, q, table_ref), nt(v, g), p_ref.at[h], prod_ref.at[h]))


def first_kernel(q_ref, g_ref, x_ref, table_ref, stats_ref, p_ref, prod_ref):
    for h in range(SPLIT):
        q, g = q_ref[:, cols(h)], g_ref[:, cols(h)]
        x = biased(nt(x_ref[0, :, cols(h)], q), table_ref, 8)
        stats_ref[h] = rows_of(held_of(x, nt(x_ref[1, :, cols(h)], g), p_ref.at[h], prod_ref.at[h]))


def rim_kernel(first, q_ref, g_ref, x_ref, i_ref, table_ref, stats_ref, *refs):
    gx_ref, final_ref, dq_ref, pi_ref, prodi_ref = refs[-5:]
    for at in range(x_ref.shape[2] // DEPTH):
        h = first + at
        q, g = q_ref[:, cols(h)], g_ref[:, cols(h)]
        x = biased(nt(i_ref[0, :, cols(h)], q), table_ref, 8 + RB)
        part_i = held_of(x, nt(i_ref[1, :, cols(h)], g), pi_ref.at[at], prodi_ref.at[at])
        if first:
            score, prod = biased(nt(x_ref[0, :, cols(at)], q), table_ref, 8), nt(x_ref[1, :, cols(at)], g)
            top = jnp.maximum(jnp.max(score, axis=0, keepdims=True), FLOOR)
            p = jnp.exp2(score - top)
            part_x = top, jnp.sum(p, axis=0, keepdims=True), jnp.sum(p * prod, axis=0, keepdims=True)
        else:
            stats_x_ref, px_ref, prodx_ref = refs[:3]
            part_x, p, prod = known(stats_x_ref.at[h]), px_ref[h], prodx_ref[h]
        own = known(stats_ref.at[h])
        top, total, raw = merged(merged(own, part_i), part_x)
        inv = jnp.where(total > 0.0, 1.0 / jnp.where(total > 0.0, total, 1.0), 0.0)
        delta = raw * inv
        w, ds = grads_of(p, prod, jnp.exp2(part_x[0] - top) * inv, delta)
        gx_ref[0, :, cols(at)] = nn(ds, q).astype(jnp.bfloat16)
        gx_ref[1, :, cols(at)] = nn(w, g).astype(jnp.bfloat16)
        dq_ref[at] = tn(x_ref[0, :, cols(at)], ds)
        final_ref[at] = rows_of((jnp.exp2(own[0] - top) * inv, jnp.exp2(part_i[0] - top) * inv, delta))


def inside_kernel(q_ref, g_ref, i_ref, *refs):
    gi_ref, dq_ref = refs[-2:]
    for h in range(HEADS):
        final_ref, rim_dq_ref, pi_ref, prodi_ref = refs[:4] if h < SPLIT else refs[4:8]
        at = h if h < SPLIT else h - SPLIT
        q, g = q_ref[:, cols(h)], g_ref[:, cols(h)]
        w, ds = grads_of(pi_ref[at], prodi_ref[at], final_ref[at, 1:2], final_ref[at, 2:3])
        gi_ref[0, :, cols(h)] = nn(ds, q).astype(jnp.bfloat16)
        gi_ref[1, :, cols(h)] = nn(w, g).astype(jnp.bfloat16)
        dq_ref[h] = rim_dq_ref[at] + tn(i_ref[0, :, cols(h)], ds)


def rest_of(first, at, q_ref, k_ref, g_ref, p_ref, prod_ref, final_ref, rim_dq_ref):
    h = first + at
    q, k, g = (ref[:, cols(h)] for ref in (q_ref, k_ref, g_ref))
    w, ds = grads_of(p_ref[h], prod_ref[h], final_ref[at, 0:1], final_ref[at, 2:3])
    dq = rim_dq_ref[h] + tn(k, ds)
    return dq.T.astype(jnp.bfloat16), nn(ds, q), nn(w, g)


def held_kernel(first, *refs):
    _, dq_ref, pk_ref, pv_ref, dq_buf, sems = refs[7:]
    copies = []
    for at in range(pk_ref.shape[1] // DEPTH):
        dq, pk_ref[:, cols(at)], pv_ref[:, cols(at)] = rest_of(first, at, *refs[:7])
        dq_buf[:, cols(at)] = dq
        copies.append(pltpu.make_async_copy(dq_buf.at[:, cols(at)], dq_ref.at[:, cols(first + at)], sems.at[at]))
        copies[-1].start()
    for copy in copies:
        copy.wait()


def done_kernel(first, *refs):
    gx_ref, gi_ref, _, dq_ref, dk_ref, dv_ref, dq_buf, dk_buf, dv_buf, sems = refs[7:]
    copies = []
    for at in range(dq_buf.shape[1] // DEPTH):
        dq, dk, dv = rest_of(first, at, *refs[:7])
        dq_buf[:, cols(at)] = dq
        for slot, buf, part in ((0, dk_buf, dk), (1, dv_buf, dv)):
            lead = gx_ref[slot, :, cols(at)].astype(jnp.float32) + gi_ref[slot, :, cols(first + at)].astype(jnp.float32)
            buf[:RIM, cols(at)] = (part[:RIM] + lead).astype(jnp.bfloat16)
            buf[RIM:, cols(at)] = part[RIM:].astype(jnp.bfloat16)
        for n, (buf, out) in enumerate(((dq_buf, dq_ref), (dk_buf, dk_ref), (dv_buf, dv_ref))):
            copies.append(pltpu.make_async_copy(buf.at[:, cols(at)], out.at[:, cols(first + at)], sems.at[n, at]))
            copies[-1].start()
    for copy in copies:
        copy.wait()


def add_kernel(first, pk_ref, pv_ref, gx_ref, gi_ref, _k, _v, dk_ref, dv_ref, dk_buf, dv_buf, sems):
    copies = []
    for at in range(pk_ref.shape[1] // DEPTH):
        for slot, (own, buf, out) in enumerate(((pk_ref, dk_buf, dk_ref), (pv_ref, dv_buf, dv_ref))):
            lead = gx_ref[slot, :, cols(at)].astype(jnp.float32) + gi_ref[slot, :, cols(first + at)].astype(jnp.float32)
            buf[:RIM, cols(at)] = (own[:RIM, cols(at)] + lead).astype(jnp.bfloat16)
            buf[RIM:, cols(at)] = own[RIM:, cols(at)].astype(jnp.bfloat16)
            copies.append(pltpu.make_async_copy(buf.at[:, cols(at)], out.at[:, cols(first + at)], sems.at[slot, at]))
            copies[-1].start()
    for copy in copies:
        copy.wait()


VMEM = pl.BlockSpec(memory_space=pltpu.VMEM)
HBM = pl.BlockSpec(memory_space=pltpu.HBM)
ANY = pl.BlockSpec(memory_space=pl.ANY)


def call(body, name, ins, outs, out_specs, args, scratch=(), alias=None, limit=24):
    return pl.pallas_call(
        body,
        in_specs=ins,
        out_specs=out_specs,
        out_shape=outs,
        scratch_shapes=scratch,
        input_output_aliases=alias or {},
        compiler_params=pltpu.CompilerParams(vmem_limit_bytes=int(limit * MIB)),
        cost_estimate=pl.CostEstimate(flops=WEIGHT[name] * MEGA, bytes_accessed=1000, transcendentals=0),
        name=name,
    )(*args)


def shape(*dims, dtype=jnp.bfloat16):
    return jax.ShapeDtypeStruct(dims, dtype)


def on_device(queries, keys, values, out_grad, band_counts, block_lists, slot_counts):
    tok, width = queries.shape
    f32 = functools.partial(shape, dtype=jnp.float32)
    cuts = ((0, SPLIT), (SPLIT, HEADS))
    part = HEADS - SPLIT
    q, k, v, g = queries, keys, values, out_grad
    lead_a, lead_b = call(
        load_kernel,
        "load_bands",
        [HBM] * 2,
        [shape(2, RIM, SPLIT * DEPTH), shape(2, RIM, part * DEPTH)],
        [VMEM] * 2,
        (keys, values),
        [pltpu.SemaphoreType.DMA((4,))],
        limit=LOAD_LIMIT,
    )
    x_a, x_b = swap_across(lead_a), swap_across(lead_b)
    lead_i = call(pack_kernel, "pack_leads", [VMEM] * 2, shape(2, RIM, width), VMEM, (k, v))
    i = swap_inside(lead_i)
    table, stats, p, prod = call(
        own_kernel,
        "own_stats",
        [VMEM] * 7,
        [f32(TABLE + tok - RIM, tok), f32(HEADS, 8, tok), f32(HEADS, tok, tok), f32(HEADS, tok, tok)],
        [VMEM] * 4,
        (band_counts[:, None], slot_counts[None], block_lists, q, k, v, g),
    )
    stats_x, px, prodx = call(
        first_kernel,
        "first_stats",
        [VMEM] * 4,
        [f32(SPLIT, 8, tok), f32(SPLIT, RIM, tok), f32(SPLIT, RIM, tok)],
        [VMEM] * 3,
        (q, g, x_a, table),
    )

    def rim(first, x, *more):
        heads = x.shape[2] // DEPTH
        return call(
            functools.partial(rim_kernel, first),
            "rim_grads",
            [VMEM] * (6 + len(more)),
            [shape(*x.shape), f32(heads, 8, tok), f32(heads, DEPTH, tok), f32(heads, RIM, tok), f32(heads, RIM, tok)],
            [VMEM] * 5,
            (q, g, x, i, table, stats) + more,
        )

    gx_a, *rest_a = rim(0, x_a, stats_x, px, prodx)
    gx_a = swap_across(gx_a)
    gx_b, *rest_b = rim(SPLIT, x_b)
    gx_b = swap_across(gx_b)
    gi, dq_rim = call(
        inside_kernel,
        "inside_grads",
        [VMEM] * 11,
        [shape(2, RIM, width), f32(HEADS, DEPTH, tok)],
        [VMEM] * 2,
        (q, g, i, *rest_a, *rest_b),
    )
    gi = swap_inside(gi)

    dq, pk, pv = call(
        functools.partial(held_kernel, SPLIT),
        "held_grads",
        [VMEM] * 7 + [ANY],
        [shape(tok, width), f32(tok, part * DEPTH), f32(tok, part * DEPTH)],
        [ANY, VMEM, VMEM],
        (q, k, g, p, prod, rest_b[0], dq_rim, gx_a),
        [pltpu.VMEM((tok, part * DEPTH), jnp.bfloat16), pltpu.SemaphoreType.DMA((part,))],
    )
    dq, dk, dv = call(
        functools.partial(done_kernel, 0),
        "done_grads",
        [VMEM] * 9 + [ANY],
        [shape(tok, width)] * 3,
        [ANY] * 3,
        (q, k, g, p, prod, rest_a[0], dq_rim, gx_a, gi, dq),
        [pltpu.VMEM((tok, SPLIT * DEPTH), jnp.bfloat16)] * 3 + [pltpu.SemaphoreType.DMA((3, SPLIT))],
        {9: 0},
    )
    dk, dv = call(
        functools.partial(add_kernel, SPLIT),
        "add_rims",
        [VMEM] * 4 + [ANY] * 2,
        [shape(tok, width)] * 2,
        [ANY] * 2,
        (pk, pv, gx_b, gi, dk, dv),
        [pltpu.VMEM((tok, part * DEPTH), jnp.bfloat16)] * 2 + [pltpu.SemaphoreType.DMA((2, part))],
        {4: 0, 5: 1},
    )
    return dq, dk, dv


def solution(mesh):
    placed = P(("member", "band"), None)
    flat = P(("member", "band"))
    return jax.shard_map(
        on_device,
        mesh=mesh,
        in_specs=(placed, placed, placed, placed, flat, placed, flat),
        out_specs=(placed, placed, placed),
        check_vma=False,
    )
```

time: 38.1 us -> 34.6 us (0.908)
  Pallas kernels: 13 us -> 10.4 us
  local copies, waits for them, and re-layouts: 0.68 us -> 0.03 us
  waiting for transfers between devices: 3.52 us -> 2.99 us
    pallas_call x8 -> x10, Pallas kernels: 13 us -> 10.4 us  [call(): pl.pallas_call(body, in_specs=ins, out_specs=out_specs, out_shape=outs, s...]
    unnamed x4 -> x12, local copies, waits for them, and re-layouts: 0.68 us -> 0.03 us
    ppermute x2, waiting for transfers between devices: 1.51 us -> 1.02 us  [swap_inside(): lax.ppermute(x, 'band', [(at, at ^ 1) for at in range(lax.axis_size('band...]
  transfers between devices with their start and end apart: 6 -> 6, of which waited for: 3 -> 2; matrix products, arithmetic and copies ran while one was open for 0% -> 0% of each run, Pallas kernels for 27% -> 24%
where the time goes in v3:
time: 34.6 us; the launch traced here: 34.3 us
  starting transfers between devices  19.3 us (56%)
  Pallas kernels  10.4 us (30%)
  waiting for transfers between devices  2.99 us (9%)
  between operations  1.51 us (4%)
    ppermute x4, starting transfers between devices, swap_across(): return lax.ppermute(x, 'band', pairs + [(b, a) for a, b in pairs])  15.5 us
    pallas_call x10, Pallas kernels, call(): pl.pallas_call(body, in_specs=ins, out_specs=out_specs, out_shape=outs, s...  10.4 us
    ppermute x2, starting transfers between devices, swap_inside(): lax.ppermute(x, 'band', [(at, at ^ 1) for at in range(lax.axis_size('band...  3.84 us
    ppermute x4, waiting for transfers between devices, swap_across(): return lax.ppermute(x, 'band', pairs + [(b, a) for a, b in pairs])  1.97 us
    ppermute x2, waiting for transfers between devices, swap_inside(): lax.ppermute(x, 'band', [(at, at ^ 1) for at in range(lax.axis_size('band...  1.02 us
  transfers between devices with their start and end apart: 6, of which 2 were waited for; matrix products, arithmetic and copies ran while one was open for 0% of the time, Pallas kernels for 24%

profile of v3, /device:TPU:454, one launch (start us, length us, event | category | flops | bytes accessed | tf_op | source)
XLA Modules:
  0.0 34.3 jit_solution(12968797875303120553)
XLA Ops:
  0.6 0.0 copy-start.3
  0.6 0.0 copy-start.2
  0.7 0.0 copy-start.5
  0.7 0.0 copy-start.4
  0.7 1.3 %load_bands.1 = (bf16[2,192,512]{2,1,0:T(8,128)(2,1)S(1)}, bf16[2,192,512]{2,1,0:T(8,128)(2,1)S(1)}) custom-call(bf16[256,1024]{1,0:T(8,128)(2,1)} %refs_1_.3, bf16[256,1024]{1,0:T(8,128)(2,1)} %v_ref.5), custom_call_target="tpu_custom_call" | custom-call | flops 5500000256 | bytes 1000 | tf_op jit(solution)/shard_map/load_bands/pallas_call | solution.py:257
  2.0 0.0 copy-start
  2.0 0.0 copy-start.1
  2.0 4.9 %collective-permute-start = (bf16[2,192,512]{2,1,0:T(8,128)(2,1)S(1)}, bf16[2,192,512]{2,1,0:T(8,128)(2,1)S(1)}, u32[]{:S(2)}, u32[]{:S(2)}) collective-permute-start(bf16[2,192,512]{2,1,0:T(8,128)(2,1)S(1)} %get-tuple-element.34), channel_id=1, source_target_pairs={{1,2},{3,4},{5,6},{7,8},{9,10},{11,12},{13,14},{15,16},{17,18},{19... | collective-permute-start | bytes 1179656 | tf_op jit(solution)/shard_map/ppermute | solution.py:109
  7.0 2.9 %collective-permute-start.2 = (bf16[2,192,512]{2,1,0:T(8,128)(2,1)S(1)}, bf16[2,192,512]{2,1,0:T(8,128)(2,1)S(1)}, u32[]{:S(2)}, u32[]{:S(2)}) collective-permute-start(bf16[2,192,512]{2,1,0:T(8,128)(2,1)S(1)} %get-tuple-element.44), channel_id=1, source_target_pairs={{1,2},{3,4},{5,6},{7,8},{9,10},{11,12},{13,14},{15,16},{17,18},{19... | collective-permute-start | bytes 1179656 | tf_op jit(solution)/shard_map/ppermute | solution.py:109
  9.8 0.0 copy-done.3
  9.9 0.0 copy-done.2
  9.9 0.1 pack_leads.1
  9.9 1.9 %collective-permute-start.1 = (bf16[2,192,1024]{2,1,0:T(8,128)(2,1)S(1)}, bf16[2,192,1024]{2,1,0:T(8,128)(2,1)S(1)}, u32[]{:S(2)}, u32[]{:S(2)}) collective-permute-start(bf16[2,192,1024]{2,1,0:T(8,128)(2,1)S(1)} %pack_leads.1), channel_id=1, source_target_pairs={{0,1},{1,0},{2,3},{3,2},{4,5},{5,4},{6,7},{7,6},{8,9},{9,8},{10,11... | collective-permute-start | bytes 2359304 | tf_op jit(solution)/shard_map/ppermute | solution.py:113
  12.5 0.0 copy-done.5
  12.5 0.0 copy-done.4
  12.5 0.0 copy-done
  12.5 0.0 copy-done.1
  12.5 1.1 %own_stats.1 = (f32[96,256]{1,0:T(8,128)S(1)}, f32[8,8,256]{2,1,0:T(8,128)S(1)}, f32[8,256,256]{2,1,0:T(8,128)S(1)}, f32[8,256,256]{2,1,0:T(8,128)S(1)}) custom-call(s32[1,1]{1,0:T(1,128)} %bitcast.2.count_ref, s32[1,8]{1,0:T(1,128)S(1)} %bitcast.3, s32[8,14]{1,0:T(8,128)S(1)} %copy-done.4, bf16[256,1024]{1,0:T(8,128)(2,1)S(1)} %copy-done, ...), custom_call_target="tpu_custom_call" | custom-call | flops 1000000 | bytes 1000 | tf_op jit(solution)/shard_map/own_stats/pallas_call | solution.py:257
  13.6 0.0 collective-permute-done.x_ref
  13.7 0.5 %first_stats.1 = (f32[4,8,256]{2,1,0:T(8,128)S(1)}, f32[4,192,256]{2,1,0:T(8,128)S(1)}, f32[4,192,256]{2,1,0:T(8,128)S(1)}) custom-call(bf16[256,1024]{1,0:T(8,128)(2,1)S(1)} %copy-done, bf16[256,1024]{1,0:T(8,128)(2,1)S(1)} %copy-done.1, bf16[2,192,512]{2,1,0:T(8,128)(2,1)S(1)} %collective-permute-done.x_ref, f32[96,256]{1,0:T(8,128)S(1)} %get-tuple-element.35.table_ref), custom_call_target="tpu_custom_call" | custom-call | flops 11000000512 | bytes 1000 | tf_op jit(solution)/shard_map/first_stats/pallas_call | solution.py:257
  14.1 0.0 collective-permute-done.1.i_ref
  14.1 1.5 %rim_grads.2 = (bf16[2,192,512]{2,1,0:T(8,128)(2,1)S(1)}, f32[4,8,256]{2,1,0:T(8,128)S(1)}, f32[4,128,256]{2,1,0:T(8,128)S(1)}, f32[4,192,256]{2,1,0:T(8,128)S(1)}, f32[4,192,256]{2,1,0:T(8,128)S(1)}) custom-call(bf16[256,1024]{1,0:T(8,128)(2,1)S(1)} %copy-done, bf16[256,1024]{1,0:T(8,128)(2,1)S(1)} %copy-done.1, ...), custom_call_target="tpu_custom_call" | custom-call | flops 1000000 | bytes 1000 | tf_op jit(solution)/shard_map/rim_grads/pallas_call | solution.py:257
  15.6 4.8 %collective-permute-start.3 = (bf16[2,192,512]{2,1,0:T(8,128)(2,1)S(1)}, bf16[2,192,512]{2,1,0:T(8,128)(2,1)S(1)}, u32[]{:S(2)}, u32[]{:S(2)}) collective-permute-start(bf16[2,192,512]{2,1,0:T(8,128)(2,1)S(1)} %get-tuple-element.50), channel_id=1, source_target_pairs={{1,2},{3,4},{5,6},{7,8},{9,10},{11,12},{13,14},{15,16},{17,18},{19... | collective-permute-start | bytes 1179656 | tf_op jit(solution)/shard_map/ppermute | solution.py:109
  20.4 0.0 collective-permute-done.2.x_ref
  20.4 1.7 %rim_grads.3 = (bf16[2,192,512]{2,1,0:T(8,128)(2,1)S(1)}, f32[4,8,256]{2,1,0:T(8,128)S(1)}, f32[4,128,256]{2,1,0:T(8,128)S(1)}, f32[4,192,256]{2,1,0:T(8,128)S(1)}, f32[4,192,256]{2,1,0:T(8,128)S(1)}) custom-call(bf16[256,1024]{1,0:T(8,128)(2,1)S(1)} %copy-done, bf16[256,1024]{1,0:T(8,128)(2,1)S(1)} %copy-done.1, ...), custom_call_target="tpu_custom_call" | custom-call | flops 1000000 | bytes 1000 | tf_op jit(solution)/shard_map/rim_grads/pallas_call | solution.py:257
  22.2 2.9 %collective-permute-start.5 = (bf16[2,192,512]{2,1,0:T(8,128)(2,1)S(1)}, bf16[2,192,512]{2,1,0:T(8,128)(2,1)S(1)}, u32[]{:S(2)}, u32[]{:S(2)}) collective-permute-start(bf16[2,192,512]{2,1,0:T(8,128)(2,1)S(1)} %get-tuple-element.56), channel_id=1, source_target_pairs={{1,2},{3,4},{5,6},{7,8},{9,10},{11,12},{13,14},{15,16},{17,18},{19... | collective-permute-start | bytes 1179656 | tf_op jit(solution)/shard_map/ppermute | solution.py:109
  25.1 0.8 %inside_grads.1 = (bf16[2,192,1024]{2,1,0:T(8,128)(2,1)S(1)}, f32[8,128,256]{2,1,0:T(8,128)S(1)}) custom-call(bf16[256,1024]{1,0:T(8,128)(2,1)S(1)} %copy-done, bf16[256,1024]{1,0:T(8,128)(2,1)S(1)} %copy-done.1, bf16[2,192,1024]{2,1,0:T(8,128)(2,1)S(1)} %collective-permute-done.1.i_ref, f32[4,8,256]{2,1,0:T(8,128)S(1)} %get-tuple-element.40.refs_0_.refs_5_, ...), custom_call_target="tpu_custom_call" | custom-call | flops 1000000 | bytes 1000 | tf_op jit(solution)/shard_map/inside_grads/pallas_call | solution.py:257
  25.9 1.9 %collective-permute-start.4 = (bf16[2,192,1024]{2,1,0:T(8,128)(2,1)S(1)}, bf16[2,192,1024]{2,1,0:T(8,128)(2,1)S(1)}, u32[]{:S(2)}, u32[]{:S(2)}) collective-permute-start(bf16[2,192,1024]{2,1,0:T(8,128)(2,1)S(1)} %get-tuple-element.51), channel_id=1, source_target_pairs={{0,1},{1,0},{2,3},{3,2},{4,5},{5,4},{6,7},{7,6},{8,9},{9,8},{10,11... | collective-permute-start | bytes 2359304 | tf_op jit(solution)/shard_map/ppermute | solution.py:113
  27.8 0.0 collective-permute-done.3.refs_7_
  27.8 1.2 %held_grads.1 = (bf16[256,1024]{1,0:T(8,128)(2,1)}, f32[256,512]{1,0:T(8,128)S(1)}, f32[256,512]{1,0:T(8,128)S(1)}) custom-call(bf16[256,1024]{1,0:T(8,128)(2,1)S(1)} %copy-done, bf16[256,1024]{1,0:T(8,128)(2,1)S(1)} %copy-done.3, bf16[256,1024]{1,0:T(8,128)(2,1)S(1)} %copy-done.1, f32[8,256,256]{2,1,0:T(8,128)S(1)} %get-tuple-element.32.refs_3_, ...), custom_call_target="tpu_custom_call" | custom-call | flops 11000000512 | bytes 1000 | tf_op jit(solution)/shard_map/held_grads/pallas_call | solution.py:257
  29.0 1.0 %collective-permute-done.4.refs_8_.gi_ref = bf16[2,192,1024]{2,1,0:T(8,128)(2,1)S(1)} collective-permute-done((bf16[2,192,1024]{2,1,0:T(8,128)(2,1)S(1)}, bf16[2,192,1024]{2,1,0:T(8,128)(2,1)S(1)}, u32[]{:S(2)}, u32[]{:S(2)}) %collective-permute-start.4) | collective-permute-done | bytes 786464 | tf_op jit(solution)/shard_map/ppermute | solution.py:113
  30.0 1.4 %done_grads.1 = (bf16[256,1024]{1,0:T(8,128)(2,1)}, bf16[256,1024]{1,0:T(8,128)(2,1)}, bf16[256,1024]{1,0:T(8,128)(2,1)}) custom-call(bf16[256,1024]{1,0:T(8,128)(2,1)S(1)} %copy-done, bf16[256,1024]{1,0:T(8,128)(2,1)S(1)} %copy-done.3, bf16[256,1024]{1,0:T(8,128)(2,1)S(1)} %copy-done.1, ...), custom_call_target="tpu_custom_call", output_to_operand_aliasing={{0}: (9, {})} | custom-call | flops 11000000512 | bytes 1000 | tf_op jit(solution)/shard_map/done_grads/pallas_call | solution.py:257
  31.4 2.0 %collective-permute-done.5.gx_ref = bf16[2,192,512]{2,1,0:T(8,128)(2,1)S(1)} collective-permute-done((bf16[2,192,512]{2,1,0:T(8,128)(2,1)S(1)}, bf16[2,192,512]{2,1,0:T(8,128)(2,1)S(1)}, u32[]{:S(2)}, u32[]{:S(2)}) %collective-permute-start.5) | collective-permute-done | bytes 393248 | tf_op jit(solution)/shard_map/ppermute | solution.py:109
  33.4 0.9 %add_rims.1 = (bf16[256,1024]{1,0:T(8,128)(2,1)}, bf16[256,1024]{1,0:T(8,128)(2,1)}) custom-call(f32[256,512]{1,0:T(8,128)S(1)} %get-tuple-element.54.pk_ref, f32[256,512]{1,0:T(8,128)S(1)} %get-tuple-element.55.pv_ref, bf16[2,192,512]{2,1,0:T(8,128)(2,1)S(1)} %collective-permute-done.5.gx_ref, ...), custom_call_target="tpu_custom_call", output_to_operand_aliasing={{0}: (4, {}), {1}: (5, {})} | custom-call | flops 1000000 | bytes 1000 | tf_op jit(solution)/shard_map/add_rims/pallas_call | solution.py:257
Async XLA Ops:
  0.6 9.2 %copy-start.3 = (bf16[256,1024]{1,0:T(8,128)(2,1)S(1)}, bf16[256,1024]{1,0:T(8,128)(2,1)}, u32[]{:S(2)}) copy-start(bf16[256,1024]{1,0:T(8,128)(2,1)} %refs_1_.3) | copy-start | bytes 1572868
  0.6 9.2 %copy-start.2 = (bf16[256,1024]{1,0:T(8,128)(2,1)S(1)}, bf16[256,1024]{1,0:T(8,128)(2,1)}, u32[]{:S(2)}) copy-start(bf16[256,1024]{1,0:T(8,128)(2,1)} %v_ref.5) | copy-start | bytes 1572868
  0.7 11.9 %copy-start.5 = (s32[8]{0:T(128)S(1)}, s32[8]{0:T(128)}, u32[]{:S(2)}) copy-start(s32[8]{0:T(128)} %param.13) | copy-start | bytes 100
  0.7 11.9 %copy-start.4 = (s32[8,14]{1,0:T(8,128)S(1)}, s32[8,14]{1,0:T(8,128)}, u32[]{:S(2)}) copy-start(s32[8,14]{1,0:T(8,128)} %lists_ref.1) | copy-start | bytes 1348
  2.0 10.5 %copy-start = (bf16[256,1024]{1,0:T(8,128)(2,1)S(1)}, bf16[256,1024]{1,0:T(8,128)(2,1)}, u32[]{:S(2)}) copy-start(bf16[256,1024]{1,0:T(8,128)(2,1)} %refs_0_.3) | copy-start | bytes 1572868
  2.0 10.5 %copy-start.1 = (bf16[256,1024]{1,0:T(8,128)(2,1)S(1)}, bf16[256,1024]{1,0:T(8,128)(2,1)}, u32[]{:S(2)}) copy-start(bf16[256,1024]{1,0:T(8,128)(2,1)} %refs_2_.3) | copy-start | bytes 1572868
  2.0 11.6 %collective-permute-start = (bf16[2,192,512]{2,1,0:T(8,128)(2,1)S(1)}, bf16[2,192,512]{2,1,0:T(8,128)(2,1)S(1)}, u32[]{:S(2)}, u32[]{:S(2)}) collective-permute-start(bf16[2,192,512]{2,1,0:T(8,128)(2,1)S(1)} %get-tuple-element.34), channel_id=1, source_target_pairs={{1,2},{3,4},{5,6},{7,8},{9,10},{11,12},{13,14},{15,16},{17,18},{19... | collective-permute-start | bytes 1179656 | tf_op jit(solution)/shard_map/ppermute | solution.py:109
  7.0 13.5 %collective-permute-start.2 = (bf16[2,192,512]{2,1,0:T(8,128)(2,1)S(1)}, bf16[2,192,512]{2,1,0:T(8,128)(2,1)S(1)}, u32[]{:S(2)}, u32[]{:S(2)}) collective-permute-start(bf16[2,192,512]{2,1,0:T(8,128)(2,1)S(1)} %get-tuple-element.44), channel_id=1, source_target_pairs={{1,2},{3,4},{5,6},{7,8},{9,10},{11,12},{13,14},{15,16},{17,18},{19... | collective-permute-start | bytes 1179656 | tf_op jit(solution)/shard_map/ppermute | solution.py:109
  9.9 4.2 %collective-permute-start.1 = (bf16[2,192,1024]{2,1,0:T(8,128)(2,1)S(1)}, bf16[2,192,1024]{2,1,0:T(8,128)(2,1)S(1)}, u32[]{:S(2)}, u32[]{:S(2)}) collective-permute-start(bf16[2,192,1024]{2,1,0:T(8,128)(2,1)S(1)} %pack_leads.1), channel_id=1, source_target_pairs={{0,1},{1,0},{2,3},{3,2},{4,5},{5,4},{6,7},{7,6},{8,9},{9,8},{10,11... | collective-permute-start | bytes 2359304 | tf_op jit(solution)/shard_map/ppermute | solution.py:113
  15.6 12.2 %collective-permute-start.3 = (bf16[2,192,512]{2,1,0:T(8,128)(2,1)S(1)}, bf16[2,192,512]{2,1,0:T(8,128)(2,1)S(1)}, u32[]{:S(2)}, u32[]{:S(2)}) collective-permute-start(bf16[2,192,512]{2,1,0:T(8,128)(2,1)S(1)} %get-tuple-element.50), channel_id=1, source_target_pairs={{1,2},{3,4},{5,6},{7,8},{9,10},{11,12},{13,14},{15,16},{17,18},{19... | collective-permute-start | bytes 1179656 | tf_op jit(solution)/shard_map/ppermute | solution.py:109
  22.2 11.2 %collective-permute-start.5 = (bf16[2,192,512]{2,1,0:T(8,128)(2,1)S(1)}, bf16[2,192,512]{2,1,0:T(8,128)(2,1)S(1)}, u32[]{:S(2)}, u32[]{:S(2)}) collective-permute-start(bf16[2,192,512]{2,1,0:T(8,128)(2,1)S(1)} %get-tuple-element.56), channel_id=1, source_target_pairs={{1,2},{3,4},{5,6},{7,8},{9,10},{11,12},{13,14},{15,16},{17,18},{19... | collective-permute-start | bytes 1179656 | tf_op jit(solution)/shard_map/ppermute | solution.py:109
  25.9 4.2 %collective-permute-start.4 = (bf16[2,192,1024]{2,1,0:T(8,128)(2,1)S(1)}, bf16[2,192,1024]{2,1,0:T(8,128)(2,1)S(1)}, u32[]{:S(2)}, u32[]{:S(2)}) collective-permute-start(bf16[2,192,1024]{2,1,0:T(8,128)(2,1)S(1)} %get-tuple-element.51), channel_id=1, source_target_pairs={{0,1},{1,0},{2,3},{3,2},{4,5},{5,4},{6,7},{7,6},{8,9},{9,8},{10,11... | collective-permute-start | bytes 2359304 | tf_op jit(solution)/shard_map/ppermute | solution.py:113

commit v4 on v3

--- a/solution.py
+++ b/solution.py
@@ -48,13 +48,25 @@
     return slice(h * DEPTH, (h + 1) * DEPTH)
 
 
-def biased(score, bias, first):
-    scaled = score * (DEPTH ** -0.5 * LOG2E)
-    parts = [
-        scaled[at * BLK : (at + 1) * BLK] + bias[first + at : first + at + 1, :]
-        for at in range(score.shape[0] // BLK)
-    ]
-    return jnp.concatenate(parts, axis=0)
+SCALE = DEPTH ** -0.5 * LOG2E
+
+
+def exps_of(score, bias, first):
+    parts = [score[at * BLK : (at + 1) * BLK] for at in range(score.shape[0] // BLK)]
+    rows = [bias[first + at : first + at + 1, :] for at in range(len(parts))]
+    tops = [jnp.max(part, axis=0, keepdims=True) * SCALE + row for part, row in zip(parts, rows)]
+    top = functools.reduce(jnp.maximum, tops, jnp.full_like(tops[0], FLOOR))
+    return top, jnp.concatenate([jnp.exp2(part * SCALE + (row - top)) for part, row in zip(parts, rows)], axis=0)
+
+
+def own_exps(score, bias):
+    lead, tail = score[:RIM], score[RIM:] * SCALE + bias[TABLE:, :]
+    parts = [lead[at * BLK : (at + 1) * BLK] for at in range(RB)]
+    rows = [bias[at : at + 1, :] for at in range(RB)]
+    tops = [jnp.max(part, axis=0, keepdims=True) * SCALE + row for part, row in zip(parts, rows)]
+    top = functools.reduce(jnp.maximum, tops, jnp.maximum(jnp.max(tail, axis=0, keepdims=True), FLOOR))
+    exps = [jnp.exp2(part * SCALE + (row - top)) for part, row in zip(parts, rows)]
+    return top, jnp.concatenate(exps + [jnp.exp2(tail - top)], axis=0)
 
 
 def table_of(lists, live, ids, count, tok):
@@ -68,23 +80,13 @@
     return jnp.where(tn(hit, spread) > 0.5, 0.0, NEG)
 
 
-def own_score(k, q, bias):
-    x = nt(k, q) * (DEPTH ** -0.5 * LOG2E)
-    parts = [x[at * BLK : (at + 1) * BLK] + bias[at : at + 1, :] for at in range(RB)]
-    return jnp.concatenate(parts + [x[RIM:] + bias[TABLE:, :]], axis=0)
-
-
 def merged(a, b):
     top = jnp.maximum(a[0], b[0])
     fa, fb = jnp.exp2(a[0] - top), jnp.exp2(b[0] - top)
     return top, a[1] * fa + b[1] * fb, a[2] * fa + b[2] * fb
 
 
-def held_of(x, prod, p_ref, prod_ref):
-    top = jnp.maximum(jnp.max(x, axis=0, keepdims=True), FLOOR)
-    p = jnp.exp2(x - top)
-    p_ref[...] = p
-    prod_ref[...] = prod
+def sums_of(top, p, prod):
     return top, jnp.sum(p, axis=0, keepdims=True), jnp.sum(p * prod, axis=0, keepdims=True)
 
 
@@ -150,31 +152,43 @@
     table_ref[TABLE:] = jnp.where(past, NEG, jnp.concatenate(tail, axis=0))
     for h in range(HEADS):
         q, k, v, g = (ref[:, cols(h)] for ref in (q_ref, k_ref, v_ref, g_ref))
-        stats_ref[h] = rows_of(held_of(own_score(k, q, table_ref), nt(v, g), p_ref.at[h], prod_ref.at[h]))
+        top, p = own_exps(nt(k, q), table_ref)
+        prod = nt(v, g)
+        p_ref[h], prod_ref[h] = p, prod
+        stats_ref[h] = rows_of(sums_of(top, p, prod))
 
 
 def first_kernel(q_ref, g_ref, x_ref, table_ref, stats_ref, p_ref, prod_ref):
     for h in range(SPLIT):
         q, g = q_ref[:, cols(h)], g_ref[:, cols(h)]
-        x = biased(nt(x_ref[0, :, cols(h)], q), table_ref, 8)
-        stats_ref[h] = rows_of(held_of(x, nt(x_ref[1, :, cols(h)], g), p_ref.at[h], prod_ref.at[h]))
+        top, p = exps_of(nt(x_ref[0, :, cols(h)], q), table_ref, 8)
+        prod = nt(x_ref[1, :, cols(h)], g)
+        p_ref[h], prod_ref[h] = p, prod
+        stats_ref[h] = rows_of(sums_of(top, p, prod))
 
 
 def rim_kernel(first, q_ref, g_ref, x_ref, i_ref, table_ref, stats_ref, *refs):
-    gx_ref, final_ref, dq_ref, pi_ref, prodi_ref = refs[-5:]
-    for at in range(x_ref.shape[2] // DEPTH):
+    gx_ref, final_ref, ds_ref, pi_ref, prodi_ref = refs[-5:]
+    heads = range(x_ref.shape[2] // DEPTH)
+    parts = []
+    for at in heads:
         h = first + at
         q, g = q_ref[:, cols(h)], g_ref[:, cols(h)]
-        x = biased(nt(i_ref[0, :, cols(h)], q), table_ref, 8 + RB)
-        part_i = held_of(x, nt(i_ref[1, :, cols(h)], g), pi_ref.at[at], prodi_ref.at[at])
+        top, p = exps_of(nt(i_ref[0, :, cols(h)], q), table_ref, 8 + RB)
+        prod = nt(i_ref[1, :, cols(h)], g)
+        pi_ref[at], prodi_ref[at] = p, prod
+        part_i = sums_of(top, p, prod)
         if first:
-            score, prod = biased(nt(x_ref[0, :, cols(at)], q), table_ref, 8), nt(x_ref[1, :, cols(at)], g)
-            top = jnp.maximum(jnp.max(score, axis=0, keepdims=True), FLOOR)
-            p = jnp.exp2(score - top)
-            part_x = top, jnp.sum(p, axis=0, keepdims=True), jnp.sum(p * prod, axis=0, keepdims=True)
+            top, p = exps_of(nt(x_ref[0, :, cols(at)], q), table_ref, 8)
+            prod = nt(x_ref[1, :, cols(at)], g)
+            part_x = sums_of(top, p, prod)
         else:
             stats_x_ref, px_ref, prodx_ref = refs[:3]
             part_x, p, prod = known(stats_x_ref.at[h]), px_ref[h], prodx_ref[h]
+        parts.append((part_i, part_x, p, prod))
+    for at, (part_i, part_x, p, prod) in zip(heads, parts):
+        h = first + at
+        q, g = q_ref[:, cols(h)], g_ref[:, cols(h)]
         own = known(stats_ref.at[h])
         top, total, raw = merged(merged(own, part_i), part_x)
         inv = jnp.where(total > 0.0, 1.0 / jnp.where(total > 0.0, total, 1.0), 0.0)
@@ -182,35 +196,36 @@
         w, ds = grads_of(p, prod, jnp.exp2(part_x[0] - top) * inv, delta)
         gx_ref[0, :, cols(at)] = nn(ds, q).astype(jnp.bfloat16)
         gx_ref[1, :, cols(at)] = nn(w, g).astype(jnp.bfloat16)
-        dq_ref[at] = tn(x_ref[0, :, cols(at)], ds)
+        ds_ref[at] = ds
         final_ref[at] = rows_of((jnp.exp2(own[0] - top) * inv, jnp.exp2(part_i[0] - top) * inv, delta))
 
 
-def inside_kernel(q_ref, g_ref, i_ref, *refs):
-    gi_ref, dq_ref = refs[-2:]
+def inside_kernel(q_ref, g_ref, *refs):
+    gi_ref, ds_ref = refs[-2:]
     for h in range(HEADS):
-        final_ref, rim_dq_ref, pi_ref, prodi_ref = refs[:4] if h < SPLIT else refs[4:8]
+        final_ref, pi_ref, prodi_ref = refs[:3] if h < SPLIT else refs[3:6]
         at = h if h < SPLIT else h - SPLIT
         q, g = q_ref[:, cols(h)], g_ref[:, cols(h)]
         w, ds = grads_of(pi_ref[at], prodi_ref[at], final_ref[at, 1:2], final_ref[at, 2:3])
         gi_ref[0, :, cols(h)] = nn(ds, q).astype(jnp.bfloat16)
         gi_ref[1, :, cols(h)] = nn(w, g).astype(jnp.bfloat16)
-        dq_ref[h] = rim_dq_ref[at] + tn(i_ref[0, :, cols(h)], ds)
-
-
-def rest_of(first, at, q_ref, k_ref, g_ref, p_ref, prod_ref, final_ref, rim_dq_ref):
+        ds_ref[h] = ds
+
+
+def rest_of(first, at, q_ref, k_ref, g_ref, p_ref, prod_ref, final_ref, x_ref, dsx_ref, i_ref, dsi_ref):
     h = first + at
     q, k, g = (ref[:, cols(h)] for ref in (q_ref, k_ref, g_ref))
     w, ds = grads_of(p_ref[h], prod_ref[h], final_ref[at, 0:1], final_ref[at, 2:3])
-    dq = rim_dq_ref[h] + tn(k, ds)
+    frame_k = jnp.concatenate([k, x_ref[0, :, cols(at)], i_ref[0, :, cols(h)]], axis=0)
+    dq = tn(frame_k, jnp.concatenate([ds, dsx_ref[at], dsi_ref[h]], axis=0))
     return dq.T.astype(jnp.bfloat16), nn(ds, q), nn(w, g)
 
 
 def held_kernel(first, *refs):
-    _, dq_ref, pk_ref, pv_ref, dq_buf, sems = refs[7:]
+    _, dq_ref, pk_ref, pv_ref, dq_buf, sems = refs[10:]
     copies = []
     for at in range(pk_ref.shape[1] // DEPTH):
-        dq, pk_ref[:, cols(at)], pv_ref[:, cols(at)] = rest_of(first, at, *refs[:7])
+        dq, pk_ref[:, cols(at)], pv_ref[:, cols(at)] = rest_of(first, at, *refs[:10])
         dq_buf[:, cols(at)] = dq
         copies.append(pltpu.make_async_copy(dq_buf.at[:, cols(at)], dq_ref.at[:, cols(first + at)], sems.at[at]))
         copies[-1].start()
@@ -219,10 +234,10 @@
 
 
 def done_kernel(first, *refs):
-    gx_ref, gi_ref, _, dq_ref, dk_ref, dv_ref, dq_buf, dk_buf, dv_buf, sems = refs[7:]
+    gx_ref, gi_ref, _, dq_ref, dk_ref, dv_ref, dq_buf, dk_buf, dv_buf, sems = refs[10:]
     copies = []
     for at in range(dq_buf.shape[1] // DEPTH):
-        dq, dk, dv = rest_of(first, at, *refs[:7])
+        dq, dk, dv = rest_of(first, at, *refs[:10])
         dq_buf[:, cols(at)] = dq
         for slot, buf, part in ((0, dk_buf, dk), (1, dv_buf, dv)):
             lead = gx_ref[slot, :, cols(at)].astype(jnp.float32) + gi_ref[slot, :, cols(first + at)].astype(jnp.float32)
@@ -313,43 +328,43 @@
             functools.partial(rim_kernel, first),
             "rim_grads",
             [VMEM] * (6 + len(more)),
-            [shape(*x.shape), f32(heads, 8, tok), f32(heads, DEPTH, tok), f32(heads, RIM, tok), f32(heads, RIM, tok)],
+            [shape(*x.shape), f32(heads, 8, tok), shape(heads, RIM, tok), f32(heads, RIM, tok), f32(heads, RIM, tok)],
             [VMEM] * 5,
             (q, g, x, i, table, stats) + more,
         )
 
-    gx_a, *rest_a = rim(0, x_a, stats_x, px, prodx)
+    gx_a, final_a, dsx_a, *inside_a = rim(0, x_a, stats_x, px, prodx)
     gx_a = swap_across(gx_a)
-    gx_b, *rest_b = rim(SPLIT, x_b)
+    gx_b, final_b, dsx_b, *inside_b = rim(SPLIT, x_b)
     gx_b = swap_across(gx_b)
-    gi, dq_rim = call(
+    gi, ds_i = call(
         inside_kernel,
         "inside_grads",
-        [VMEM] * 11,
-        [shape(2, RIM, width), f32(HEADS, DEPTH, tok)],
+        [VMEM] * 8,
+        [shape(2, RIM, width), shape(HEADS, RIM, tok)],
         [VMEM] * 2,
-        (q, g, i, *rest_a, *rest_b),
+        (q, g, final_a, *inside_a, final_b, *inside_b),
     )
     gi = swap_inside(gi)
 
     dq, pk, pv = call(
         functools.partial(held_kernel, SPLIT),
         "held_grads",
-        [VMEM] * 7 + [ANY],
+        [VMEM] * 10 + [ANY],
         [shape(tok, width), f32(tok, part * DEPTH), f32(tok, part * DEPTH)],
         [ANY, VMEM, VMEM],
-        (q, k, g, p, prod, rest_b[0], dq_rim, gx_a),
+        (q, k, g, p, prod, final_b, x_b, dsx_b, i, ds_i, gx_a),
         [pltpu.VMEM((tok, part * DEPTH), jnp.bfloat16), pltpu.SemaphoreType.DMA((part,))],
     )
     dq, dk, dv = call(
         functools.partial(done_kernel, 0),
         "done_grads",
-        [VMEM] * 9 + [ANY],
+        [VMEM] * 12 + [ANY],
         [shape(tok, width)] * 3,
         [ANY] * 3,
-        (q, k, g, p, prod, rest_a[0], dq_rim, gx_a, gi, dq),
+        (q, k, g, p, prod, final_a, x_a, dsx_a, i, ds_i, gx_a, gi, dq),
         [pltpu.VMEM((tok, SPLIT * DEPTH), jnp.bfloat16)] * 3 + [pltpu.SemaphoreType.DMA((3, SPLIT))],
-        {9: 0},
+        {12: 0},
     )
     dk, dv = call(
         functools.partial(add_kernel, SPLIT),

time: 34.6 us -> 33.6 us (0.971)
  Pallas kernels: 10.4 us -> 9.53 us
    pallas_call x10, Pallas kernels: 10.4 us -> 9.53 us  [call(): pl.pallas_call(body, in_specs=ins, out_specs=out_specs, out_shape=outs, s...]
  transfers between devices with their start and end apart: 6 -> 6, of which waited for: 2 -> 2; matrix products, arithmetic and copies ran while one was open for 0% -> 0% of each run, Pallas kernels for 24% -> 22%
where the time goes in v4:
time: 33.6 us; the launch traced here: 33.3 us
  starting transfers between devices  19.3 us (57%)
  Pallas kernels  9.53 us (28%)
  waiting for transfers between devices  2.96 us (9%)
  between operations  1.52 us (5%)
    ppermute x4, starting transfers between devices, swap_across(): return lax.ppermute(x, 'band', pairs + [(b, a) for a, b in pairs])  15.5 us
    pallas_call x10, Pallas kernels, call(): pl.pallas_call(body, in_specs=ins, out_specs=out_specs, out_shape=outs, s...  9.53 us
    ppermute x2, starting transfers between devices, swap_inside(): lax.ppermute(x, 'band', [(at, at ^ 1) for at in range(lax.axis_size('band...  3.84 us
    ppermute x4, waiting for transfers between devices, swap_across(): return lax.ppermute(x, 'band', pairs + [(b, a) for a, b in pairs])  2.05 us
    ppermute x2, waiting for transfers between devices, swap_inside(): lax.ppermute(x, 'band', [(at, at ^ 1) for at in range(lax.axis_size('band...  0.9 us
  transfers between devices with their start and end apart: 6, of which 2 were waited for; matrix products, arithmetic and copies ran while one was open for 0% of the time, Pallas kernels for 22%

profile of v4, /device:TPU:454, one launch (start us, length us, event | category | flops | bytes accessed | tf_op | source)
XLA Modules:
  0.0 33.3 jit_solution(481806289782513841)
XLA Ops:
  0.6 0.0 copy-start.3
  0.6 0.0 copy-start.2
  0.7 0.0 copy-start.5
  0.7 0.0 copy-start.4
  0.7 1.3 %load_bands.1 = (bf16[2,192,512]{2,1,0:T(8,128)(2,1)S(1)}, bf16[2,192,512]{2,1,0:T(8,128)(2,1)S(1)}) custom-call(bf16[256,1024]{1,0:T(8,128)(2,1)} %refs_1_.3, bf16[256,1024]{1,0:T(8,128)(2,1)} %v_ref.5), custom_call_target="tpu_custom_call" | custom-call | flops 5500000256 | bytes 1000 | tf_op jit(solution)/shard_map/load_bands/pallas_call | solution.py:272
  2.0 0.0 copy-start
  2.0 0.0 copy-start.1
  2.0 4.9 %collective-permute-start = (bf16[2,192,512]{2,1,0:T(8,128)(2,1)S(1)}, bf16[2,192,512]{2,1,0:T(8,128)(2,1)S(1)}, u32[]{:S(2)}, u32[]{:S(2)}) collective-permute-start(bf16[2,192,512]{2,1,0:T(8,128)(2,1)S(1)} %get-tuple-element.34), channel_id=1, source_target_pairs={{1,2},{3,4},{5,6},{7,8},{9,10},{11,12},{13,14},{15,16},{17,18},{19... | collective-permute-start | bytes 1179656 | tf_op jit(solution)/shard_map/ppermute | solution.py:111
  7.0 2.9 %collective-permute-start.2 = (bf16[2,192,512]{2,1,0:T(8,128)(2,1)S(1)}, bf16[2,192,512]{2,1,0:T(8,128)(2,1)S(1)}, u32[]{:S(2)}, u32[]{:S(2)}) collective-permute-start(bf16[2,192,512]{2,1,0:T(8,128)(2,1)S(1)} %get-tuple-element.44), channel_id=1, source_target_pairs={{1,2},{3,4},{5,6},{7,8},{9,10},{11,12},{13,14},{15,16},{17,18},{19... | collective-permute-start | bytes 1179656 | tf_op jit(solution)/shard_map/ppermute | solution.py:111
  9.8 0.0 copy-done.3
  9.9 0.0 copy-done.2
  9.9 0.1 pack_leads.1
  9.9 1.9 %collective-permute-start.1 = (bf16[2,192,1024]{2,1,0:T(8,128)(2,1)S(1)}, bf16[2,192,1024]{2,1,0:T(8,128)(2,1)S(1)}, u32[]{:S(2)}, u32[]{:S(2)}) collective-permute-start(bf16[2,192,1024]{2,1,0:T(8,128)(2,1)S(1)} %pack_leads.1), channel_id=1, source_target_pairs={{0,1},{1,0},{2,3},{3,2},{4,5},{5,4},{6,7},{7,6},{8,9},{9,8},{10,11... | collective-permute-start | bytes 2359304 | tf_op jit(solution)/shard_map/ppermute | solution.py:115
  12.5 0.0 copy-done.5
  12.5 0.0 copy-done.4
  12.5 0.0 copy-done
  12.5 0.0 copy-done.1
  12.5 1.1 %own_stats.1 = (f32[96,256]{1,0:T(8,128)S(1)}, f32[8,8,256]{2,1,0:T(8,128)S(1)}, f32[8,256,256]{2,1,0:T(8,128)S(1)}, f32[8,256,256]{2,1,0:T(8,128)S(1)}) custom-call(s32[1,1]{1,0:T(1,128)} %bitcast.2.count_ref, s32[1,8]{1,0:T(1,128)S(1)} %bitcast.3, s32[8,14]{1,0:T(8,128)S(1)} %copy-done.4, bf16[256,1024]{1,0:T(8,128)(2,1)S(1)} %copy-done, ...), custom_call_target="tpu_custom_call" | custom-call | flops 1000000 | bytes 1000 | tf_op jit(solution)/shard_map/own_stats/pallas_call | solution.py:272
  13.7 0.0 collective-permute-done.x_ref.refs_6_
  13.7 0.5 %first_stats.1 = (f32[4,8,256]{2,1,0:T(8,128)S(1)}, f32[4,192,256]{2,1,0:T(8,128)S(1)}, f32[4,192,256]{2,1,0:T(8,128)S(1)}) custom-call(bf16[256,1024]{1,0:T(8,128)(2,1)S(1)} %copy-done, bf16[256,1024]{1,0:T(8,128)(2,1)S(1)} %copy-done.1, bf16[2,192,512]{2,1,0:T(8,128)(2,1)S(1)} %collective-permute-done.x_ref.refs_6_, f32[96,256]{1,0:T(8,128)S(1)} %get-tuple-element.35.table_ref), custom_call_target="tpu_custom_call" | custom-call | flops 11000000512 | bytes 1000 | tf_op jit(solution)/shard_map/first_stats/pallas_call | solution.py:272
  14.2 0.0 collective-permute-done.1.i_ref.refs_8_
  14.2 0.9 %rim_grads.2 = (bf16[2,192,512]{2,1,0:T(8,128)(2,1)S(1)}, f32[4,8,256]{2,1,0:T(8,128)S(1)}, bf16[4,192,256]{2,1,0:T(8,128)(2,1)S(1)}, f32[4,192,256]{2,1,0:T(8,128)S(1)}, f32[4,192,256]{2,1,0:T(8,128)S(1)}) custom-call(bf16[256,1024]{1,0:T(8,128)(2,1)S(1)} %copy-done, bf16[256,1024]{1,0:T(8,128)(2,1)S(1)} %copy-done.1, ...), custom_call_target="tpu_custom_call" | custom-call | flops 1000000 | bytes 1000 | tf_op jit(solution)/shard_map/rim_grads/pallas_call | solution.py:272
  15.1 4.8 %collective-permute-start.3 = (bf16[2,192,512]{2,1,0:T(8,128)(2,1)S(1)}, bf16[2,192,512]{2,1,0:T(8,128)(2,1)S(1)}, u32[]{:S(2)}, u32[]{:S(2)}) collective-permute-start(bf16[2,192,512]{2,1,0:T(8,128)(2,1)S(1)} %get-tuple-element.49), channel_id=1, source_target_pairs={{1,2},{3,4},{5,6},{7,8},{9,10},{11,12},{13,14},{15,16},{17,18},{19... | collective-permute-start | bytes 1179656 | tf_op jit(solution)/shard_map/ppermute | solution.py:111
  19.9 0.0 collective-permute-done.2.x_ref.refs_6_
  19.9 1.4 %rim_grads.3 = (bf16[2,192,512]{2,1,0:T(8,128)(2,1)S(1)}, f32[4,8,256]{2,1,0:T(8,128)S(1)}, bf16[4,192,256]{2,1,0:T(8,128)(2,1)S(1)}, f32[4,192,256]{2,1,0:T(8,128)S(1)}, f32[4,192,256]{2,1,0:T(8,128)S(1)}) custom-call(bf16[256,1024]{1,0:T(8,128)(2,1)S(1)} %copy-done, bf16[256,1024]{1,0:T(8,128)(2,1)S(1)} %copy-done.1, ...), custom_call_target="tpu_custom_call" | custom-call | flops 1000000 | bytes 1000 | tf_op jit(solution)/shard_map/rim_grads/pallas_call | solution.py:272
  21.2 2.9 %collective-permute-start.5 = (bf16[2,192,512]{2,1,0:T(8,128)(2,1)S(1)}, bf16[2,192,512]{2,1,0:T(8,128)(2,1)S(1)}, u32[]{:S(2)}, u32[]{:S(2)}) collective-permute-start(bf16[2,192,512]{2,1,0:T(8,128)(2,1)S(1)} %get-tuple-element.56), channel_id=1, source_target_pairs={{1,2},{3,4},{5,6},{7,8},{9,10},{11,12},{13,14},{15,16},{17,18},{19... | collective-permute-start | bytes 1179656 | tf_op jit(solution)/shard_map/ppermute | solution.py:111
  24.1 0.6 %inside_grads.1 = (bf16[2,192,1024]{2,1,0:T(8,128)(2,1)S(1)}, bf16[8,192,256]{2,1,0:T(8,128)(2,1)S(1)}) custom-call(bf16[256,1024]{1,0:T(8,128)(2,1)S(1)} %copy-done, bf16[256,1024]{1,0:T(8,128)(2,1)S(1)} %copy-done.1, f32[4,8,256]{2,1,0:T(8,128)S(1)} %get-tuple-element.40.refs_0_.refs_5_, f32[4,192,256]{2,1,0:T(8,128)S(1)} %get-tuple-element.42.refs_1_, ...), custom_call_target="tpu_custom_call" | custom-call | flops 1000000 | bytes 1000 | tf_op jit(solution)/shard_map/inside_grads/pallas_call | solution.py:272
  24.8 1.9 %collective-permute-start.4 = (bf16[2,192,1024]{2,1,0:T(8,128)(2,1)S(1)}, bf16[2,192,1024]{2,1,0:T(8,128)(2,1)S(1)}, u32[]{:S(2)}, u32[]{:S(2)}) collective-permute-start(bf16[2,192,1024]{2,1,0:T(8,128)(2,1)S(1)} %get-tuple-element.50), channel_id=1, source_target_pairs={{0,1},{1,0},{2,3},{3,2},{4,5},{5,4},{6,7},{7,6},{8,9},{9,8},{10,11... | collective-permute-start | bytes 2359304 | tf_op jit(solution)/shard_map/ppermute | solution.py:115
  26.7 0.0 collective-permute-done.3.refs_10_
  26.7 1.3 %held_grads.1 = (bf16[256,1024]{1,0:T(8,128)(2,1)}, f32[256,512]{1,0:T(8,128)S(1)}, f32[256,512]{1,0:T(8,128)S(1)}) custom-call(bf16[256,1024]{1,0:T(8,128)(2,1)S(1)} %copy-done, bf16[256,1024]{1,0:T(8,128)(2,1)S(1)} %copy-done.3, bf16[256,1024]{1,0:T(8,128)(2,1)S(1)} %copy-done.1, f32[8,256,256]{2,1,0:T(8,128)S(1)} %get-tuple-element.32.refs_3_, ...), custom_call_target="tpu_custom_call" | custom-call | flops 11000000512 | bytes 1000 | tf_op jit(solution)/shard_map/held_grads/pallas_call | solution.py:272
  28.0 0.9 %collective-permute-done.4.refs_11_.gi_ref = bf16[2,192,1024]{2,1,0:T(8,128)(2,1)S(1)} collective-permute-done((bf16[2,192,1024]{2,1,0:T(8,128)(2,1)S(1)}, bf16[2,192,1024]{2,1,0:T(8,128)(2,1)S(1)}, u32[]{:S(2)}, u32[]{:S(2)}) %collective-permute-start.4) | collective-permute-done | bytes 786464 | tf_op jit(solution)/shard_map/ppermute | solution.py:115
  29.0 1.5 %done_grads.1 = (bf16[256,1024]{1,0:T(8,128)(2,1)}, bf16[256,1024]{1,0:T(8,128)(2,1)}, bf16[256,1024]{1,0:T(8,128)(2,1)}) custom-call(bf16[256,1024]{1,0:T(8,128)(2,1)S(1)} %copy-done, bf16[256,1024]{1,0:T(8,128)(2,1)S(1)} %copy-done.3, bf16[256,1024]{1,0:T(8,128)(2,1)S(1)} %copy-done.1, ...), custom_call_target="tpu_custom_call", output_to_operand_aliasing={{0}: (12, {})} | custom-call | flops 11000000512 | bytes 1000 | tf_op jit(solution)/shard_map/done_grads/pallas_call | solution.py:272
  30.4 2.0 %collective-permute-done.5.gx_ref = bf16[2,192,512]{2,1,0:T(8,128)(2,1)S(1)} collective-permute-done((bf16[2,192,512]{2,1,0:T(8,128)(2,1)S(1)}, bf16[2,192,512]{2,1,0:T(8,128)(2,1)S(1)}, u32[]{:S(2)}, u32[]{:S(2)}) %collective-permute-start.5) | collective-permute-done | bytes 393248 | tf_op jit(solution)/shard_map/ppermute | solution.py:111
  32.5 0.9 %add_rims.1 = (bf16[256,1024]{1,0:T(8,128)(2,1)}, bf16[256,1024]{1,0:T(8,128)(2,1)}) custom-call(f32[256,512]{1,0:T(8,128)S(1)} %get-tuple-element.54.pk_ref, f32[256,512]{1,0:T(8,128)S(1)} %get-tuple-element.55.pv_ref, bf16[2,192,512]{2,1,0:T(8,128)(2,1)S(1)} %collective-permute-done.5.gx_ref, ...), custom_call_target="tpu_custom_call", output_to_operand_aliasing={{0}: (4, {}), {1}: (5, {})} | custom-call | flops 1000000 | bytes 1000 | tf_op jit(solution)/shard_map/add_rims/pallas_call | solution.py:272
Async XLA Ops:
  0.6 9.2 %copy-start.3 = (bf16[256,1024]{1,0:T(8,128)(2,1)S(1)}, bf16[256,1024]{1,0:T(8,128)(2,1)}, u32[]{:S(2)}) copy-start(bf16[256,1024]{1,0:T(8,128)(2,1)} %refs_1_.3) | copy-start | bytes 1572868
  0.6 9.2 %copy-start.2 = (bf16[256,1024]{1,0:T(8,128)(2,1)S(1)}, bf16[256,1024]{1,0:T(8,128)(2,1)}, u32[]{:S(2)}) copy-start(bf16[256,1024]{1,0:T(8,128)(2,1)} %v_ref.5) | copy-start | bytes 1572868
  0.7 11.9 %copy-start.5 = (s32[8]{0:T(128)S(1)}, s32[8]{0:T(128)}, u32[]{:S(2)}) copy-start(s32[8]{0:T(128)} %param.13) | copy-start | bytes 100
  0.7 11.9 %copy-start.4 = (s32[8,14]{1,0:T(8,128)S(1)}, s32[8,14]{1,0:T(8,128)}, u32[]{:S(2)}) copy-start(s32[8,14]{1,0:T(8,128)} %lists_ref.1) | copy-start | bytes 1348
  2.0 10.5 %copy-start = (bf16[256,1024]{1,0:T(8,128)(2,1)S(1)}, bf16[256,1024]{1,0:T(8,128)(2,1)}, u32[]{:S(2)}) copy-start(bf16[256,1024]{1,0:T(8,128)(2,1)} %refs_0_.3) | copy-start | bytes 1572868
  2.0 10.5 %copy-start.1 = (bf16[256,1024]{1,0:T(8,128)(2,1)S(1)}, bf16[256,1024]{1,0:T(8,128)(2,1)}, u32[]{:S(2)}) copy-start(bf16[256,1024]{1,0:T(8,128)(2,1)} %refs_2_.3) | copy-start | bytes 1572868
  2.0 11.6 %collective-permute-start = (bf16[2,192,512]{2,1,0:T(8,128)(2,1)S(1)}, bf16[2,192,512]{2,1,0:T(8,128)(2,1)S(1)}, u32[]{:S(2)}, u32[]{:S(2)}) collective-permute-start(bf16[2,192,512]{2,1,0:T(8,128)(2,1)S(1)} %get-tuple-element.34), channel_id=1, source_target_pairs={{1,2},{3,4},{5,6},{7,8},{9,10},{11,12},{13,14},{15,16},{17,18},{19... | collective-permute-start | bytes 1179656 | tf_op jit(solution)/shard_map/ppermute | solution.py:111
  7.0 12.9 %collective-permute-start.2 = (bf16[2,192,512]{2,1,0:T(8,128)(2,1)S(1)}, bf16[2,192,512]{2,1,0:T(8,128)(2,1)S(1)}, u32[]{:S(2)}, u32[]{:S(2)}) collective-permute-start(bf16[2,192,512]{2,1,0:T(8,128)(2,1)S(1)} %get-tuple-element.44), channel_id=1, source_target_pairs={{1,2},{3,4},{5,6},{7,8},{9,10},{11,12},{13,14},{15,16},{17,18},{19... | collective-permute-start | bytes 1179656 | tf_op jit(solution)/shard_map/ppermute | solution.py:111
  9.9 4.3 %collective-permute-start.1 = (bf16[2,192,1024]{2,1,0:T(8,128)(2,1)S(1)}, bf16[2,192,1024]{2,1,0:T(8,128)(2,1)S(1)}, u32[]{:S(2)}, u32[]{:S(2)}) collective-permute-start(bf16[2,192,1024]{2,1,0:T(8,128)(2,1)S(1)} %pack_leads.1), channel_id=1, source_target_pairs={{0,1},{1,0},{2,3},{3,2},{4,5},{5,4},{6,7},{7,6},{8,9},{9,8},{10,11... | collective-permute-start | bytes 2359304 | tf_op jit(solution)/shard_map/ppermute | solution.py:115
  15.1 11.6 %collective-permute-start.3 = (bf16[2,192,512]{2,1,0:T(8,128)(2,1)S(1)}, bf16[2,192,512]{2,1,0:T(8,128)(2,1)S(1)}, u32[]{:S(2)}, u32[]{:S(2)}) collective-permute-start(bf16[2,192,512]{2,1,0:T(8,128)(2,1)S(1)} %get-tuple-element.49), channel_id=1, source_target_pairs={{1,2},{3,4},{5,6},{7,8},{9,10},{11,12},{13,14},{15,16},{17,18},{19... | collective-permute-start | bytes 1179656 | tf_op jit(solution)/shard_map/ppermute | solution.py:111
  21.2 11.2 %collective-permute-start.5 = (bf16[2,192,512]{2,1,0:T(8,128)(2,1)S(1)}, bf16[2,192,512]{2,1,0:T(8,128)(2,1)S(1)}, u32[]{:S(2)}, u32[]{:S(2)}) collective-permute-start(bf16[2,192,512]{2,1,0:T(8,128)(2,1)S(1)} %get-tuple-element.56), channel_id=1, source_target_pairs={{1,2},{3,4},{5,6},{7,8},{9,10},{11,12},{13,14},{15,16},{17,18},{19... | collective-permute-start | bytes 1179656 | tf_op jit(solution)/shard_map/ppermute | solution.py:111
  24.8 4.2 %collective-permute-start.4 = (bf16[2,192,1024]{2,1,0:T(8,128)(2,1)S(1)}, bf16[2,192,1024]{2,1,0:T(8,128)(2,1)S(1)}, u32[]{:S(2)}, u32[]{:S(2)}) collective-permute-start(bf16[2,192,1024]{2,1,0:T(8,128)(2,1)S(1)} %get-tuple-element.50), channel_id=1, source_target_pairs={{0,1},{1,0},{2,3},{3,2},{4,5},{5,4},{6,7},{7,6},{8,9},{9,8},{10,11... | collective-permute-start | bytes 2359304 | tf_op jit(solution)/shard_map/ppermute | solution.py:115

commit v5 on v4

--- a/solution.py
+++ b/solution.py
@@ -16,17 +16,21 @@
 NEG = -1e30
 FLOOR = -1e20
 MIB = 1024 * 1024
-LOAD_LIMIT = 53.14
+LOAD_LIMIT = 53.5
 SPLIT = 4
+SENT = 1
+PIECES = 2 // SENT
+STATS = 32
 MEGA = 10**6
 WEIGHT = {
     "load_bands": 5500,
     "pack_leads": 1,
+    "pack_inside": 1,
     "own_stats": 1,
     "first_stats": 11000,
     "rim_grads": 1,
     "inside_grads": 1,
-    "held_grads": 11000,
+    "rest_grads": 11000,
     "done_grads": 11000,
     "add_rims": 1,
 }
@@ -99,6 +103,20 @@
     return ref[0:1], ref[1:2], ref[2:3]
 
 
+def thirds_of(rows):
+    high = rows.astype(jnp.bfloat16)
+    left = rows - high.astype(jnp.float32)
+    middle = left.astype(jnp.bfloat16)
+    low = (left - middle.astype(jnp.float32)).astype(jnp.bfloat16)
+    parts = [part.astype(jnp.float32) for part in (high, middle, low)]
+    return jnp.concatenate(parts + [jnp.zeros_like(rows)], axis=0).astype(jnp.bfloat16)
+
+
+def whole_of(parts):
+    high, middle, low = (parts[at * 8 : (at + 1) * 8] for at in range(3))
+    return high + (middle + low)
+
+
 def grads_of(p, prod, factor, delta):
     w = (p * factor).astype(jnp.bfloat16)
     ds = (p * (factor * (DEPTH ** -0.5)) * (prod - delta)).astype(jnp.bfloat16)
@@ -115,19 +133,36 @@
     return lax.ppermute(x, "band", [(at, at ^ 1) for at in range(lax.axis_size("band"))])
 
 
-def load_kernel(k_ref, v_ref, lead_a_ref, lead_b_ref, sems):
-    moves = []
-    for lead, first in ((lead_a_ref, 0), (lead_b_ref, k_ref.shape[1] - lead_b_ref.shape[2])):
-        for at, src in enumerate((k_ref, v_ref)):
-            moves.append((src.at[pl.ds(0, RIM), pl.ds(first, lead.shape[2])], lead.at[at]))
-    copies = [pltpu.make_async_copy(src, dst, sems.at[at]) for at, (src, dst) in enumerate(moves)]
+def load_kernel(k_ref, v_ref, lead_ref, sems):
+    copies = [
+        pltpu.make_async_copy(
+            src.at[pl.ds(0, RIM), pl.ds(0, SPLIT * DEPTH)], lead_ref.at[pl.ds(at * RIM, RIM), :], sems.at[at]
+        )
+        for at, src in enumerate((k_ref, v_ref))
+    ]
     for copy in copies:
         copy.start()
     for copy in copies:
         copy.wait()
 
 
-def pack_kernel(k_ref, v_ref, lead_ref):
+def pack_kernel(k_ref, v_ref, q_ref, g_ref, lead_ref):
+    for at, ref in enumerate((k_ref, v_ref)):
+        lead_ref[at * RIM : (at + 1) * RIM, :] = ref[:RIM, SPLIT * DEPTH :]
+    rows = q_ref.shape[0] // PIECES
+    for at, ref in enumerate((q_ref, g_ref)):
+        for n in range(SENT):
+            for piece in range(PIECES):
+                part = ref[piece * rows : (piece + 1) * rows, cols(HEADS - SENT + n)]
+                lead_ref[2 * RIM :, cols(2 * at + n * PIECES + piece)] = part
+
+
+def sent_of(x_ref, at, n):
+    parts = [x_ref[2 * RIM :, cols(2 * at + n * PIECES + piece)] for piece in range(PIECES)]
+    return jnp.concatenate(parts, axis=0)
+
+
+def inside_pack_kernel(k_ref, v_ref, _, lead_ref):
     for at, ref in enumerate((k_ref, v_ref)):
         lead_ref[at] = ref[:RIM, :]
 
@@ -161,15 +196,16 @@
 def first_kernel(q_ref, g_ref, x_ref, table_ref, stats_ref, p_ref, prod_ref):
     for h in range(SPLIT):
         q, g = q_ref[:, cols(h)], g_ref[:, cols(h)]
-        top, p = exps_of(nt(x_ref[0, :, cols(h)], q), table_ref, 8)
-        prod = nt(x_ref[1, :, cols(h)], g)
+        top, p = exps_of(nt(x_ref[:RIM, cols(h)], q), table_ref, 8)
+        prod = nt(x_ref[RIM : 2 * RIM, cols(h)], g)
         p_ref[h], prod_ref[h] = p, prod
         stats_ref[h] = rows_of(sums_of(top, p, prod))
 
 
 def rim_kernel(first, q_ref, g_ref, x_ref, i_ref, table_ref, stats_ref, *refs):
     gx_ref, final_ref, ds_ref, pi_ref, prodi_ref = refs[-5:]
-    heads = range(x_ref.shape[2] // DEPTH)
+    heads = range(x_ref.shape[1] // DEPTH)
+    returned = len(heads) - (SENT if first else 0)
     parts = []
     for at in heads:
         h = first + at
@@ -179,8 +215,8 @@
         pi_ref[at], prodi_ref[at] = p, prod
         part_i = sums_of(top, p, prod)
         if first:
-            top, p = exps_of(nt(x_ref[0, :, cols(at)], q), table_ref, 8)
-            prod = nt(x_ref[1, :, cols(at)], g)
+            top, p = exps_of(nt(x_ref[:RIM, cols(at)], q), table_ref, 8)
+            prod = nt(x_ref[RIM : 2 * RIM, cols(at)], g)
             part_x = sums_of(top, p, prod)
         else:
             stats_x_ref, px_ref, prodx_ref = refs[:3]
@@ -194,8 +230,13 @@
         inv = jnp.where(total > 0.0, 1.0 / jnp.where(total > 0.0, total, 1.0), 0.0)
         delta = raw * inv
         w, ds = grads_of(p, prod, jnp.exp2(part_x[0] - top) * inv, delta)
-        gx_ref[0, :, cols(at)] = nn(ds, q).astype(jnp.bfloat16)
-        gx_ref[1, :, cols(at)] = nn(w, g).astype(jnp.bfloat16)
+        if at < returned:
+            gx_ref[:RIM, cols(at)] = nn(ds, q).astype(jnp.bfloat16)
+            gx_ref[RIM : 2 * RIM, cols(at)] = nn(w, g).astype(jnp.bfloat16)
+        else:
+            rows = jnp.concatenate([table_ref[8 : 8 + RB] - top, inv, delta], axis=0)
+            begin = 2 * RIM + (at - returned) * STATS
+            gx_ref[begin : begin + STATS, : rows.shape[1]] = thirds_of(rows)
         ds_ref[at] = ds
         final_ref[at] = rows_of((jnp.exp2(own[0] - top) * inv, jnp.exp2(part_i[0] - top) * inv, delta))
 
@@ -212,53 +253,70 @@
         ds_ref[h] = ds
 
 
-def rest_of(first, at, q_ref, k_ref, g_ref, p_ref, prod_ref, final_ref, x_ref, dsx_ref, i_ref, dsi_ref):
-    h = first + at
-    q, k, g = (ref[:, cols(h)] for ref in (q_ref, k_ref, g_ref))
-    w, ds = grads_of(p_ref[h], prod_ref[h], final_ref[at, 0:1], final_ref[at, 2:3])
-    frame_k = jnp.concatenate([k, x_ref[0, :, cols(at)], i_ref[0, :, cols(h)]], axis=0)
-    dq = tn(frame_k, jnp.concatenate([ds, dsx_ref[at], dsi_ref[h]], axis=0))
-    return dq.T.astype(jnp.bfloat16), nn(ds, q), nn(w, g)
-
-
-def held_kernel(first, *refs):
-    _, dq_ref, pk_ref, pv_ref, dq_buf, sems = refs[10:]
-    copies = []
-    for at in range(pk_ref.shape[1] // DEPTH):
-        dq, pk_ref[:, cols(at)], pv_ref[:, cols(at)] = rest_of(first, at, *refs[:10])
-        dq_buf[:, cols(at)] = dq
-        copies.append(pltpu.make_async_copy(dq_buf.at[:, cols(at)], dq_ref.at[:, cols(first + at)], sems.at[at]))
-        copies[-1].start()
+def rest_kernel(q_ref, k_ref, v_ref, g_ref, p_ref, prod_ref, i_ref, dsi_ref, *refs):
+    parts, (_, dq_ref, pk_ref, pv_ref, score_ref, products_ref) = (refs[:3], refs[3:6]), refs[6:]
+    x_ref = parts[1][1]
+    for n in range(SENT):
+        h = HEADS - SENT + n
+        score_ref[n] = nt(k_ref[:RIM, cols(h)], sent_of(x_ref, 0, n))
+        products_ref[n] = nt(v_ref[:RIM, cols(h)], sent_of(x_ref, 1, n))
+    for h in range(HEADS):
+        at = h if h < SPLIT else h - SPLIT
+        final_ref, x_ref, dsx_ref = parts[0] if h < SPLIT else parts[1]
+        q, k, g = (ref[:, cols(h)] for ref in (q_ref, k_ref, g_ref))
+        w, ds = grads_of(p_ref[h], prod_ref[h], final_ref[at, 0:1], final_ref[at, 2:3])
+        pk_ref[:, cols(h)] = nn(ds, q)
+        pv_ref[:, cols(h)] = nn(w, g)
+        frame_k = jnp.concatenate([k, x_ref[:RIM, cols(at)], i_ref[0, :, cols(h)]], axis=0)
+        dq = tn(frame_k, jnp.concatenate([ds, dsx_ref[at], dsi_ref[h]], axis=0))
+        dq_ref[:, cols(h)] = dq.T.astype(jnp.bfloat16)
+
+
+def summed(own_ref, lead, gi_ref, slot, h):
+    lead = own_ref[:RIM, cols(h)] + (lead + gi_ref[slot, :, cols(h)].astype(jnp.float32))
+    return jnp.concatenate([lead, own_ref[RIM:, cols(h)]], axis=0).astype(jnp.bfloat16)
+
+
+def done_kernel(dq_in, pk_ref, pv_ref, gx_ref, gi_ref, dq_ref, dk_ref, dv_ref, dk_buf, dv_buf, sems):
+    span = pl.ds(0, dk_buf.shape[1])
+    copies = [
+        pltpu.make_async_copy(dq_in, dq_ref, sems.at[0]),
+        pltpu.make_async_copy(dk_buf, dk_ref.at[:, span], sems.at[1]),
+        pltpu.make_async_copy(dv_buf, dv_ref.at[:, span], sems.at[2]),
+    ]
+    copies[0].start()
+    for slot, (own, buf) in enumerate(((pk_ref, dk_buf), (pv_ref, dv_buf))):
+        for h in range(SPLIT):
+            lead = gx_ref[slot * RIM : (slot + 1) * RIM, cols(h)].astype(jnp.float32)
+            buf[:, cols(h)] = summed(own, lead, gi_ref, slot, h)
+        copies[1 + slot].start()
     for copy in copies:
         copy.wait()
 
 
-def done_kernel(first, *refs):
-    gx_ref, gi_ref, _, dq_ref, dk_ref, dv_ref, dq_buf, dk_buf, dv_buf, sems = refs[10:]
-    copies = []
-    for at in range(dq_buf.shape[1] // DEPTH):
-        dq, dk, dv = rest_of(first, at, *refs[:10])
-        dq_buf[:, cols(at)] = dq
-        for slot, buf, part in ((0, dk_buf, dk), (1, dv_buf, dv)):
-            lead = gx_ref[slot, :, cols(at)].astype(jnp.float32) + gi_ref[slot, :, cols(first + at)].astype(jnp.float32)
-            buf[:RIM, cols(at)] = (part[:RIM] + lead).astype(jnp.bfloat16)
-            buf[RIM:, cols(at)] = part[RIM:].astype(jnp.bfloat16)
-        for n, (buf, out) in enumerate(((dq_buf, dq_ref), (dk_buf, dk_ref), (dv_buf, dv_ref))):
-            copies.append(pltpu.make_async_copy(buf.at[:, cols(at)], out.at[:, cols(first + at)], sems.at[n, at]))
-            copies[-1].start()
-    for copy in copies:
-        copy.wait()
-
-
-def add_kernel(first, pk_ref, pv_ref, gx_ref, gi_ref, _k, _v, dk_ref, dv_ref, dk_buf, dv_buf, sems):
-    copies = []
-    for at in range(pk_ref.shape[1] // DEPTH):
-        for slot, (own, buf, out) in enumerate(((pk_ref, dk_buf, dk_ref), (pv_ref, dv_buf, dv_ref))):
-            lead = gx_ref[slot, :, cols(at)].astype(jnp.float32) + gi_ref[slot, :, cols(first + at)].astype(jnp.float32)
-            buf[:RIM, cols(at)] = (own[:RIM, cols(at)] + lead).astype(jnp.bfloat16)
-            buf[RIM:, cols(at)] = own[RIM:, cols(at)].astype(jnp.bfloat16)
-            copies.append(pltpu.make_async_copy(buf.at[:, cols(at)], out.at[:, cols(first + at)], sems.at[slot, at]))
-            copies[-1].start()
+def add_kernel(pk_ref, pv_ref, gx_ref, gi_ref, x_ref, score_ref, prod_ref, _k, _v, dk_ref, dv_ref, dk_buf, dv_buf, sems):
+    heads = HEADS - SPLIT
+    returned = heads - SENT
+    leads = {}
+    for n in range(SENT):
+        begin = 2 * RIM + n * STATS
+        rows = whole_of(gx_ref[begin : begin + STATS, : score_ref.shape[2]].astype(jnp.float32))
+        blocks = [jnp.exp2(score_ref[n, e * BLK : (e + 1) * BLK] * SCALE + rows[e : e + 1]) for e in range(RB)]
+        w, ds = grads_of(jnp.concatenate(blocks, axis=0), prod_ref[n], rows[RB : RB + 1], rows[RB + 1 : RB + 2])
+        leads[returned + n] = nn(ds, sent_of(x_ref, 0, n)), nn(w, sent_of(x_ref, 1, n))
+    span = pl.ds(SPLIT * DEPTH, heads * DEPTH)
+    copies = [
+        pltpu.make_async_copy(buf, out.at[:, span], sems.at[slot])
+        for slot, (buf, out) in enumerate(((dk_buf, dk_ref), (dv_buf, dv_ref)))
+    ]
+    for slot, (own, buf) in enumerate(((pk_ref, dk_buf), (pv_ref, dv_buf))):
+        for at in range(heads):
+            if at in leads:
+                lead = leads[at][slot]
+            else:
+                lead = gx_ref[slot * RIM : (slot + 1) * RIM, cols(at)].astype(jnp.float32)
+            buf[:, cols(at)] = summed(own, lead, gi_ref, slot, SPLIT + at)
+        copies[slot].start()
     for copy in copies:
         copy.wait()
 
@@ -292,18 +350,19 @@
     cuts = ((0, SPLIT), (SPLIT, HEADS))
     part = HEADS - SPLIT
     q, k, v, g = queries, keys, values, out_grad
-    lead_a, lead_b = call(
+    lead_a = call(
         load_kernel,
         "load_bands",
         [HBM] * 2,
-        [shape(2, RIM, SPLIT * DEPTH), shape(2, RIM, part * DEPTH)],
-        [VMEM] * 2,
-        (keys, values),
-        [pltpu.SemaphoreType.DMA((4,))],
+        shape(2 * RIM, SPLIT * DEPTH),
+        VMEM,
+        (k, v),
+        [pltpu.SemaphoreType.DMA((2,))],
         limit=LOAD_LIMIT,
     )
+    lead_b = call(pack_kernel, "pack_leads", [VMEM] * 4, shape(2 * RIM + tok // PIECES, part * DEPTH), VMEM, (k, v, q, g))
     x_a, x_b = swap_across(lead_a), swap_across(lead_b)
-    lead_i = call(pack_kernel, "pack_leads", [VMEM] * 2, shape(2, RIM, width), VMEM, (k, v))
+    lead_i = call(inside_pack_kernel, "pack_inside", [VMEM] * 2 + [ANY], shape(2, RIM, width), VMEM, (k, v, lead_b))
     i = swap_inside(lead_i)
     table, stats, p, prod = call(
         own_kernel,
@@ -323,12 +382,13 @@
     )
 
     def rim(first, x, *more):
-        heads = x.shape[2] // DEPTH
+        heads = x.shape[1] // DEPTH
+        gx = (2 * RIM + SENT * STATS, (heads - SENT) * DEPTH) if first else x.shape
         return call(
             functools.partial(rim_kernel, first),
             "rim_grads",
             [VMEM] * (6 + len(more)),
-            [shape(*x.shape), f32(heads, 8, tok), shape(heads, RIM, tok), f32(heads, RIM, tok), f32(heads, RIM, tok)],
+            [shape(*gx), f32(heads, 8, tok), shape(heads, RIM, tok), f32(heads, RIM, tok), f32(heads, RIM, tok)],
             [VMEM] * 5,
             (q, g, x, i, table, stats) + more,
         )
@@ -347,34 +407,32 @@
     )
     gi = swap_inside(gi)
 
-    dq, pk, pv = call(
-        functools.partial(held_kernel, SPLIT),
-        "held_grads",
-        [VMEM] * 10 + [ANY],
-        [shape(tok, width), f32(tok, part * DEPTH), f32(tok, part * DEPTH)],
-        [ANY, VMEM, VMEM],
-        (q, k, g, p, prod, final_b, x_b, dsx_b, i, ds_i, gx_a),
-        [pltpu.VMEM((tok, part * DEPTH), jnp.bfloat16), pltpu.SemaphoreType.DMA((part,))],
+    dq, pk, pv, score, products = call(
+        rest_kernel,
+        "rest_grads",
+        [VMEM] * 14 + [ANY],
+        [shape(tok, width), f32(tok, width), f32(tok, width), f32(SENT, RIM, tok), f32(SENT, RIM, tok)],
+        [VMEM] * 5,
+        (q, k, v, g, p, prod, i, ds_i, final_a, x_a, dsx_a, final_b, x_b, dsx_b, gx_a),
     )
     dq, dk, dv = call(
-        functools.partial(done_kernel, 0),
+        done_kernel,
         "done_grads",
-        [VMEM] * 12 + [ANY],
+        [VMEM] * 5,
         [shape(tok, width)] * 3,
         [ANY] * 3,
-        (q, k, g, p, prod, final_a, x_a, dsx_a, i, ds_i, gx_a, gi, dq),
-        [pltpu.VMEM((tok, SPLIT * DEPTH), jnp.bfloat16)] * 3 + [pltpu.SemaphoreType.DMA((3, SPLIT))],
-        {12: 0},
+        (dq, pk, pv, gx_a, gi),
+        [pltpu.VMEM((tok, SPLIT * DEPTH), jnp.bfloat16)] * 2 + [pltpu.SemaphoreType.DMA((3,))],
     )
     dk, dv = call(
-        functools.partial(add_kernel, SPLIT),
+        add_kernel,
         "add_rims",
-        [VMEM] * 4 + [ANY] * 2,
+        [VMEM] * 7 + [ANY] * 2,
         [shape(tok, width)] * 2,
         [ANY] * 2,
-        (pk, pv, gx_b, gi, dk, dv),
-        [pltpu.VMEM((tok, part * DEPTH), jnp.bfloat16)] * 2 + [pltpu.SemaphoreType.DMA((2, part))],
-        {4: 0, 5: 1},
+        (pk, pv, gx_b, gi, x_b, score, products, dk, dv),
+        [pltpu.VMEM((tok, part * DEPTH), jnp.bfloat16)] * 2 + [pltpu.SemaphoreType.DMA((2,))],
+        {7: 0, 8: 1},
     )
     return dq, dk, dv
 

time: 33.6 us -> 32.8 us (0.976)
  waiting for transfers between devices: 2.96 us -> 1.6 us
  starting transfers between devices: 19.3 us -> 20.1 us
    ppermute x4, waiting for transfers between devices: 2.05 us -> 0.77 us  [swap_across(): return lax.ppermute(x, 'band', pairs + [(b, a) for a, b in pairs])]
    ppermute x4, starting transfers between devices: 15.5 us -> 16.3 us  [swap_across(): return lax.ppermute(x, 'band', pairs + [(b, a) for a, b in pairs])]
    pallas_call x10 -> x11, Pallas kernels: 9.53 us -> 9.21 us  [call(): pl.pallas_call(body, in_specs=ins, out_specs=out_specs, out_shape=outs, s...]
  transfers between devices with their start and end apart: 6 -> 6, of which waited for: 2 -> 2; matrix products, arithmetic and copies ran while one was open for 0% -> 0% of each run, Pallas kernels for 22% -> 21%
where the time goes in v5:
time: 32.8 us; the launch traced here: 32.5 us
  starting transfers between devices  20.1 us (61%)
  Pallas kernels  9.21 us (28%)
  waiting for transfers between devices  1.6 us (5%)
  between operations  1.53 us (5%)
    ppermute x4, starting transfers between devices, swap_across(): return lax.ppermute(x, 'band', pairs + [(b, a) for a, b in pairs])  16.3 us
    pallas_call x11, Pallas kernels, call(): pl.pallas_call(body, in_specs=ins, out_specs=out_specs, out_shape=outs, s...  9.21 us
    ppermute x2, starting transfers between devices, swap_inside(): lax.ppermute(x, 'band', [(at, at ^ 1) for at in range(lax.axis_size('band...  3.84 us
    ppermute x2, waiting for transfers between devices, swap_inside(): lax.ppermute(x, 'band', [(at, at ^ 1) for at in range(lax.axis_size('band...  0.83 us
    ppermute x4, waiting for transfers between devices, swap_across(): return lax.ppermute(x, 'band', pairs + [(b, a) for a, b in pairs])  0.77 us
  transfers between devices with their start and end apart: 6, of which 2 were waited for; matrix products, arithmetic and copies ran while one was open for 0% of the time, Pallas kernels for 21%

profile of v5, /device:TPU:454, one launch (start us, length us, event | category | flops | bytes accessed | tf_op | source)
XLA Modules:
  0.0 32.5 jit_solution(3969220191171472543)
XLA Ops:
  0.6 0.0 copy-start.3
  0.6 0.0 copy-start.2
  0.7 0.0 copy-start.1
  0.7 0.0 copy-start
  0.7 1.2 %load_bands.1 = bf16[384,512]{1,0:T(8,128)(2,1)S(1)} custom-call(bf16[256,1024]{1,0:T(8,128)(2,1)} %k_ref.9, bf16[256,1024]{1,0:T(8,128)(2,1)} %v_ref.9), custom_call_target="tpu_custom_call" | custom-call | flops 5500000256 | bytes 1000 | tf_op jit(solution)/shard_map/load_bands/pallas_call | solution.py:330
  1.9 0.0 copy-start.4
  1.9 0.0 copy-start.5
  1.9 4.8 %collective-permute-start.1 = (bf16[384,512]{1,0:T(8,128)(2,1)S(1)}, bf16[384,512]{1,0:T(8,128)(2,1)S(1)}, u32[]{:S(2)}, u32[]{:S(2)}) collective-permute-start(bf16[384,512]{1,0:T(8,128)(2,1)S(1)} %load_bands.1), channel_id=1, source_target_pairs={{1,2},{3,4},{5,6},{7,8},{9,10},{11,12},{13,14},{15,16},{17,18},{19... | collective-permute-start | bytes 1179656 | tf_op jit(solution)/shard_map/ppermute | solution.py:129
  6.7 0.0 copy-done.3
  6.7 0.0 copy-done.2
  6.7 0.0 copy-done.1
  6.7 0.0 copy-done
  6.7 0.1 pack_leads.1._
  6.8 2.9 %collective-permute-start.2 = (bf16[512,512]{1,0:T(8,128)(2,1)S(1)}, bf16[512,512]{1,0:T(8,128)(2,1)S(1)}, u32[]{:S(2)}, u32[]{:S(2)}) collective-permute-start(bf16[512,512]{1,0:T(8,128)(2,1)S(1)} %pack_leads.1._), channel_id=1, source_target_pairs={{1,2},{3,4},{5,6},{7,8},{9,10},{11,12},{13,14},{15,16},{17,18},{19... | collective-permute-start | bytes 1572872 | tf_op jit(solution)/shard_map/ppermute | solution.py:129
  9.7 0.1 pack_inside.1
  9.7 1.9 %collective-permute-start = (bf16[2,192,1024]{2,1,0:T(8,128)(2,1)S(1)}, bf16[2,192,1024]{2,1,0:T(8,128)(2,1)S(1)}, u32[]{:S(2)}, u32[]{:S(2)}) collective-permute-start(bf16[2,192,1024]{2,1,0:T(8,128)(2,1)S(1)} %pack_inside.1), channel_id=1, source_target_pairs={{0,1},{1,0},{2,3},{3,2},{4,5},{5,4},{6,7},{7,6},{8,9},{9,8},{10,11... | collective-permute-start | bytes 2359304 | tf_op jit(solution)/shard_map/ppermute | solution.py:133
  12.3 0.0 copy-done.4
  12.3 0.0 copy-done.5
  12.3 1.1 %own_stats.1 = (f32[96,256]{1,0:T(8,128)S(1)}, f32[8,8,256]{2,1,0:T(8,128)S(1)}, f32[8,256,256]{2,1,0:T(8,128)S(1)}, f32[8,256,256]{2,1,0:T(8,128)S(1)}) custom-call(s32[1,1]{1,0:T(1,128)} %bitcast.2.count_ref, s32[1,8]{1,0:T(1,128)S(1)} %bitcast.3, s32[8,14]{1,0:T(8,128)S(1)} %copy-done.4, bf16[256,1024]{1,0:T(8,128)(2,1)S(1)} %copy-done, ...), custom_call_target="tpu_custom_call" | custom-call | flops 1000000 | bytes 1000 | tf_op jit(solution)/shard_map/own_stats/pallas_call | solution.py:330
  13.5 0.0 collective-permute-done.1.x_ref.refs_1_
  13.5 0.5 %first_stats.1 = (f32[4,8,256]{2,1,0:T(8,128)S(1)}, f32[4,192,256]{2,1,0:T(8,128)S(1)}, f32[4,192,256]{2,1,0:T(8,128)S(1)}) custom-call(bf16[256,1024]{1,0:T(8,128)(2,1)S(1)} %copy-done, bf16[256,1024]{1,0:T(8,128)(2,1)S(1)} %copy-done.1, bf16[384,512]{1,0:T(8,128)(2,1)S(1)} %collective-permute-done.1.x_ref.refs_1_, f32[96,256]{1,0:T(8,128)S(1)} %get-tuple-element.34.table_ref), custom_call_target="tpu_custom_call" | custom-call | flops 11000000512 | bytes 1000 | tf_op jit(solution)/shard_map/first_stats/pallas_call | solution.py:330
  14.0 0.0 collective-permute-done.i_ref
  14.0 0.9 %rim_grads.2 = (bf16[384,512]{1,0:T(8,128)(2,1)S(1)}, f32[4,8,256]{2,1,0:T(8,128)S(1)}, bf16[4,192,256]{2,1,0:T(8,128)(2,1)S(1)}, f32[4,192,256]{2,1,0:T(8,128)S(1)}, f32[4,192,256]{2,1,0:T(8,128)S(1)}) custom-call(bf16[256,1024]{1,0:T(8,128)(2,1)S(1)} %copy-done, bf16[256,1024]{1,0:T(8,128)(2,1)S(1)} %copy-done.1, ...), custom_call_target="tpu_custom_call" | custom-call | flops 1000000 | bytes 1000 | tf_op jit(solution)/shard_map/rim_grads/pallas_call | solution.py:330
  14.9 4.8 %collective-permute-start.3 = (bf16[384,512]{1,0:T(8,128)(2,1)S(1)}, bf16[384,512]{1,0:T(8,128)(2,1)S(1)}, u32[]{:S(2)}, u32[]{:S(2)}) collective-permute-start(bf16[384,512]{1,0:T(8,128)(2,1)S(1)} %get-tuple-element.48), channel_id=1, source_target_pairs={{1,2},{3,4},{5,6},{7,8},{9,10},{11,12},{13,14},{15,16},{17,18},{19... | collective-permute-start | bytes 1179656 | tf_op jit(solution)/shard_map/ppermute | solution.py:129
  19.7 0.0 collective-permute-done.2.x_ref.refs_4_
  19.7 1.3 %rim_grads.3 = (bf16[416,384]{1,0:T(8,128)(2,1)S(1)}, f32[4,8,256]{2,1,0:T(8,128)S(1)}, bf16[4,192,256]{2,1,0:T(8,128)(2,1)S(1)}, f32[4,192,256]{2,1,0:T(8,128)S(1)}, f32[4,192,256]{2,1,0:T(8,128)S(1)}) custom-call(bf16[256,1024]{1,0:T(8,128)(2,1)S(1)} %copy-done, bf16[256,1024]{1,0:T(8,128)(2,1)S(1)} %copy-done.1, ...), custom_call_target="tpu_custom_call" | custom-call | flops 1000000 | bytes 1000 | tf_op jit(solution)/shard_map/rim_grads/pallas_call | solution.py:330
  21.0 3.8 %collective-permute-start.5 = (bf16[416,384]{1,0:T(8,128)(2,1)S(1)}, bf16[416,384]{1,0:T(8,128)(2,1)S(1)}, u32[]{:S(2)}, u32[]{:S(2)}) collective-permute-start(bf16[416,384]{1,0:T(8,128)(2,1)S(1)} %get-tuple-element.54), channel_id=1, source_target_pairs={{1,2},{3,4},{5,6},{7,8},{9,10},{11,12},{13,14},{15,16},{17,18},{19... | collective-permute-start | bytes 958472 | tf_op jit(solution)/shard_map/ppermute | solution.py:129
  24.8 0.7 %inside_grads.1 = (bf16[2,192,1024]{2,1,0:T(8,128)(2,1)S(1)}, bf16[8,192,256]{2,1,0:T(8,128)(2,1)S(1)}) custom-call(bf16[256,1024]{1,0:T(8,128)(2,1)S(1)} %copy-done, bf16[256,1024]{1,0:T(8,128)(2,1)S(1)} %copy-done.1, f32[4,8,256]{2,1,0:T(8,128)S(1)} %get-tuple-element.39.refs_0_, f32[4,192,256]{2,1,0:T(8,128)S(1)} %get-tuple-element.40.refs_1_, ...), custom_call_target="tpu_custom_call" | custom-call | flops 1000000 | bytes 1000 | tf_op jit(solution)/shard_map/inside_grads/pallas_call | solution.py:330
  25.5 1.9 %collective-permute-start.4 = (bf16[2,192,1024]{2,1,0:T(8,128)(2,1)S(1)}, bf16[2,192,1024]{2,1,0:T(8,128)(2,1)S(1)}, u32[]{:S(2)}, u32[]{:S(2)}) collective-permute-start(bf16[2,192,1024]{2,1,0:T(8,128)(2,1)S(1)} %get-tuple-element.52), channel_id=1, source_target_pairs={{0,1},{1,0},{2,3},{3,2},{4,5},{5,4},{6,7},{7,6},{8,9},{9,8},{10,11... | collective-permute-start | bytes 2359304 | tf_op jit(solution)/shard_map/ppermute | solution.py:133
  27.4 0.0 collective-permute-done.3.refs_6_.gx_ref
  27.4 1.4 %rest_grads.1 = (bf16[256,1024]{1,0:T(8,128)(2,1)S(1)}, f32[256,1024]{1,0:T(8,128)S(1)}, f32[256,1024]{1,0:T(8,128)S(1)}, f32[1,192,256]{2,1,0:T(8,128)S(1)}, f32[1,192,256]{2,1,0:T(8,128)S(1)}) custom-call(bf16[256,1024]{1,0:T(8,128)(2,1)S(1)} %copy-done, bf16[256,1024]{1,0:T(8,128)(2,1)S(1)} %copy-done.2, bf16[256,1024]{1,0:T(8,128)(2,1)S(1)} %copy-done.3, ...), custom_call_target="tpu_custom_call" | custom-call | flops 11000000512 | bytes 1000 | tf_op jit(solution)/shard_map/rest_grads/pallas_call | solution.py:330
  28.9 0.8 %collective-permute-done.4.gi_ref = bf16[2,192,1024]{2,1,0:T(8,128)(2,1)S(1)} collective-permute-done((bf16[2,192,1024]{2,1,0:T(8,128)(2,1)S(1)}, bf16[2,192,1024]{2,1,0:T(8,128)(2,1)S(1)}, u32[]{:S(2)}, u32[]{:S(2)}) %collective-permute-start.4) | collective-permute-done | bytes 786464 | tf_op jit(solution)/shard_map/ppermute | solution.py:133
  29.7 1.0 %done_grads.1 = (bf16[256,1024]{1,0:T(8,128)(2,1)}, bf16[256,1024]{1,0:T(8,128)(2,1)}, bf16[256,1024]{1,0:T(8,128)(2,1)}) custom-call(bf16[256,1024]{1,0:T(8,128)(2,1)S(1)} %get-tuple-element.49.dq_in, f32[256,1024]{1,0:T(8,128)S(1)} %get-tuple-element.50.pk_ref, f32[256,1024]{1,0:T(8,128)S(1)} %get-tuple-element.51.pv_ref, ...), custom_call_target="tpu_custom_call" | custom-call | flops 11000000512 | bytes 1000 | tf_op jit(solution)/shard_map/done_grads/pallas_call | solution.py:330
  30.7 0.8 %collective-permute-done.5.gx_ref = bf16[416,384]{1,0:T(8,128)(2,1)S(1)} collective-permute-done((bf16[416,384]{1,0:T(8,128)(2,1)S(1)}, bf16[416,384]{1,0:T(8,128)(2,1)S(1)}, u32[]{:S(2)}, u32[]{:S(2)}) %collective-permute-start.5) | collective-permute-done | bytes 319520 | tf_op jit(solution)/shard_map/ppermute | solution.py:129
  31.4 1.0 %add_rims.1 = (bf16[256,1024]{1,0:T(8,128)(2,1)}, bf16[256,1024]{1,0:T(8,128)(2,1)}) custom-call(f32[256,1024]{1,0:T(8,128)S(1)} %get-tuple-element.50.pk_ref, f32[256,1024]{1,0:T(8,128)S(1)} %get-tuple-element.51.pv_ref, bf16[416,384]{1,0:T(8,128)(2,1)S(1)} %collective-permute-done.5.gx_ref, ...), custom_call_target="tpu_custom_call", output_to_operand_aliasing={{0}: (7, {}), {1}: (8, {})} | custom-call | flops 1000000 | bytes 1000 | tf_op jit(solution)/shard_map/add_rims/pallas_call | solution.py:330
Async XLA Ops:
  0.6 6.1 %copy-start.3 = (bf16[256,1024]{1,0:T(8,128)(2,1)S(1)}, bf16[256,1024]{1,0:T(8,128)(2,1)}, u32[]{:S(2)}) copy-start(bf16[256,1024]{1,0:T(8,128)(2,1)} %v_ref.9) | copy-start | bytes 1572868
  0.6 6.1 %copy-start.2 = (bf16[256,1024]{1,0:T(8,128)(2,1)S(1)}, bf16[256,1024]{1,0:T(8,128)(2,1)}, u32[]{:S(2)}) copy-start(bf16[256,1024]{1,0:T(8,128)(2,1)} %k_ref.9) | copy-start | bytes 1572868
  0.7 6.1 %copy-start.1 = (bf16[256,1024]{1,0:T(8,128)(2,1)S(1)}, bf16[256,1024]{1,0:T(8,128)(2,1)}, u32[]{:S(2)}) copy-start(bf16[256,1024]{1,0:T(8,128)(2,1)} %g_ref.13) | copy-start | bytes 1572868
  0.7 6.1 %copy-start = (bf16[256,1024]{1,0:T(8,128)(2,1)S(1)}, bf16[256,1024]{1,0:T(8,128)(2,1)}, u32[]{:S(2)}) copy-start(bf16[256,1024]{1,0:T(8,128)(2,1)} %q_ref.13) | copy-start | bytes 1572868
  1.9 10.5 %copy-start.4 = (s32[8,14]{1,0:T(8,128)S(1)}, s32[8,14]{1,0:T(8,128)}, u32[]{:S(2)}) copy-start(s32[8,14]{1,0:T(8,128)} %lists_ref.1) | copy-start | bytes 1348
  1.9 10.5 %copy-start.5 = (s32[8]{0:T(128)S(1)}, s32[8]{0:T(128)}, u32[]{:S(2)}) copy-start(s32[8]{0:T(128)} %param.13) | copy-start | bytes 100
  1.9 11.6 %collective-permute-start.1 = (bf16[384,512]{1,0:T(8,128)(2,1)S(1)}, bf16[384,512]{1,0:T(8,128)(2,1)S(1)}, u32[]{:S(2)}, u32[]{:S(2)}) collective-permute-start(bf16[384,512]{1,0:T(8,128)(2,1)S(1)} %load_bands.1), channel_id=1, source_target_pairs={{1,2},{3,4},{5,6},{7,8},{9,10},{11,12},{13,14},{15,16},{17,18},{19... | collective-permute-start | bytes 1179656 | tf_op jit(solution)/shard_map/ppermute | solution.py:129
  6.8 12.9 %collective-permute-start.2 = (bf16[512,512]{1,0:T(8,128)(2,1)S(1)}, bf16[512,512]{1,0:T(8,128)(2,1)S(1)}, u32[]{:S(2)}, u32[]{:S(2)}) collective-permute-start(bf16[512,512]{1,0:T(8,128)(2,1)S(1)} %pack_leads.1._), channel_id=1, source_target_pairs={{1,2},{3,4},{5,6},{7,8},{9,10},{11,12},{13,14},{15,16},{17,18},{19... | collective-permute-start | bytes 1572872 | tf_op jit(solution)/shard_map/ppermute | solution.py:129
  9.7 4.3 %collective-permute-start = (bf16[2,192,1024]{2,1,0:T(8,128)(2,1)S(1)}, bf16[2,192,1024]{2,1,0:T(8,128)(2,1)S(1)}, u32[]{:S(2)}, u32[]{:S(2)}) collective-permute-start(bf16[2,192,1024]{2,1,0:T(8,128)(2,1)S(1)} %pack_inside.1), channel_id=1, source_target_pairs={{0,1},{1,0},{2,3},{3,2},{4,5},{5,4},{6,7},{7,6},{8,9},{9,8},{10,11... | collective-permute-start | bytes 2359304 | tf_op jit(solution)/shard_map/ppermute | solution.py:133
  14.9 12.5 %collective-permute-start.3 = (bf16[384,512]{1,0:T(8,128)(2,1)S(1)}, bf16[384,512]{1,0:T(8,128)(2,1)S(1)}, u32[]{:S(2)}, u32[]{:S(2)}) collective-permute-start(bf16[384,512]{1,0:T(8,128)(2,1)S(1)} %get-tuple-element.48), channel_id=1, source_target_pairs={{1,2},{3,4},{5,6},{7,8},{9,10},{11,12},{13,14},{15,16},{17,18},{19... | collective-permute-start | bytes 1179656 | tf_op jit(solution)/shard_map/ppermute | solution.py:129
  21.0 10.4 %collective-permute-start.5 = (bf16[416,384]{1,0:T(8,128)(2,1)S(1)}, bf16[416,384]{1,0:T(8,128)(2,1)S(1)}, u32[]{:S(2)}, u32[]{:S(2)}) collective-permute-start(bf16[416,384]{1,0:T(8,128)(2,1)S(1)} %get-tuple-element.54), channel_id=1, source_target_pairs={{1,2},{3,4},{5,6},{7,8},{9,10},{11,12},{13,14},{15,16},{17,18},{19... | collective-permute-start | bytes 958472 | tf_op jit(solution)/shard_map/ppermute | solution.py:129
  25.5 4.2 %collective-permute-start.4 = (bf16[2,192,1024]{2,1,0:T(8,128)(2,1)S(1)}, bf16[2,192,1024]{2,1,0:T(8,128)(2,1)S(1)}, u32[]{:S(2)}, u32[]{:S(2)}) collective-permute-start(bf16[2,192,1024]{2,1,0:T(8,128)(2,1)S(1)} %get-tuple-element.52), channel_id=1, source_target_pairs={{0,1},{1,0},{2,3},{3,2},{4,5},{5,4},{6,7},{7,6},{8,9},{9,8},{10,11... | collective-permute-start | bytes 2359304 | tf_op jit(solution)/shard_map/ppermute | solution.py:133

commit v6 on v5

--- a/solution.py
+++ b/solution.py
@@ -18,8 +18,8 @@
 MIB = 1024 * 1024
 LOAD_LIMIT = 53.5
 SPLIT = 4
-SENT = 1
-PIECES = 2 // SENT
+SENT = 2
+PIECES = 2
 STATS = 32
 MEGA = 10**6
 WEIGHT = {
@@ -149,17 +149,18 @@
 def pack_kernel(k_ref, v_ref, q_ref, g_ref, lead_ref):
     for at, ref in enumerate((k_ref, v_ref)):
         lead_ref[at * RIM : (at + 1) * RIM, :] = ref[:RIM, SPLIT * DEPTH :]
+    pack_head(q_ref, g_ref, HEADS - 1, lead_ref)
+
+
+def pack_head(q_ref, g_ref, h, to_ref):
     rows = q_ref.shape[0] // PIECES
     for at, ref in enumerate((q_ref, g_ref)):
-        for n in range(SENT):
-            for piece in range(PIECES):
-                part = ref[piece * rows : (piece + 1) * rows, cols(HEADS - SENT + n)]
-                lead_ref[2 * RIM :, cols(2 * at + n * PIECES + piece)] = part
-
-
-def sent_of(x_ref, at, n):
-    parts = [x_ref[2 * RIM :, cols(2 * at + n * PIECES + piece)] for piece in range(PIECES)]
-    return jnp.concatenate(parts, axis=0)
+        for piece in range(PIECES):
+            to_ref[2 * RIM :, cols(at * PIECES + piece)] = ref[piece * rows : (piece + 1) * rows, cols(h)]
+
+
+def sent_of(ref, at):
+    return jnp.concatenate([ref[2 * RIM :, cols(at * PIECES + piece)] for piece in range(PIECES)], axis=0)
 
 
 def inside_pack_kernel(k_ref, v_ref, _, lead_ref):
@@ -204,6 +205,8 @@
 
 def rim_kernel(first, q_ref, g_ref, x_ref, i_ref, table_ref, stats_ref, *refs):
     gx_ref, final_ref, ds_ref, pi_ref, prodi_ref = refs[-5:]
+    if not first:
+        pack_head(q_ref, g_ref, HEADS - SENT, gx_ref)
     heads = range(x_ref.shape[1] // DEPTH)
     returned = len(heads) - (SENT if first else 0)
     parts = []
@@ -256,10 +259,8 @@
 def rest_kernel(q_ref, k_ref, v_ref, g_ref, p_ref, prod_ref, i_ref, dsi_ref, *refs):
     parts, (_, dq_ref, pk_ref, pv_ref, score_ref, products_ref) = (refs[:3], refs[3:6]), refs[6:]
     x_ref = parts[1][1]
-    for n in range(SENT):
-        h = HEADS - SENT + n
-        score_ref[n] = nt(k_ref[:RIM, cols(h)], sent_of(x_ref, 0, n))
-        products_ref[n] = nt(v_ref[:RIM, cols(h)], sent_of(x_ref, 1, n))
+    score_ref[...] = nt(k_ref[:RIM, cols(HEADS - 1)], sent_of(x_ref, 0))
+    products_ref[...] = nt(v_ref[:RIM, cols(HEADS - 1)], sent_of(x_ref, 1))
     for h in range(HEADS):
         at = h if h < SPLIT else h - SPLIT
         final_ref, x_ref, dsx_ref = parts[0] if h < SPLIT else parts[1]
@@ -277,7 +278,9 @@
     return jnp.concatenate([lead, own_ref[RIM:, cols(h)]], axis=0).astype(jnp.bfloat16)
 
 
-def done_kernel(dq_in, pk_ref, pv_ref, gx_ref, gi_ref, dq_ref, dk_ref, dv_ref, dk_buf, dv_buf, sems):
+def done_kernel(
+    k_ref, v_ref, dq_in, pk_ref, pv_ref, gx_ref, gi_ref, dq_ref, dk_ref, dv_ref, score_ref, products_ref, dk_buf, dv_buf, sems
+):
     span = pl.ds(0, dk_buf.shape[1])
     copies = [
         pltpu.make_async_copy(dq_in, dq_ref, sems.at[0]),
@@ -290,20 +293,23 @@
             lead = gx_ref[slot * RIM : (slot + 1) * RIM, cols(h)].astype(jnp.float32)
             buf[:, cols(h)] = summed(own, lead, gi_ref, slot, h)
         copies[1 + slot].start()
+    score_ref[...] = nt(k_ref[:RIM, cols(HEADS - SENT)], sent_of(gx_ref, 0))
+    products_ref[...] = nt(v_ref[:RIM, cols(HEADS - SENT)], sent_of(gx_ref, 1))
     for copy in copies:
         copy.wait()
 
 
-def add_kernel(pk_ref, pv_ref, gx_ref, gi_ref, x_ref, score_ref, prod_ref, _k, _v, dk_ref, dv_ref, dk_buf, dv_buf, sems):
+def add_kernel(pk_ref, pv_ref, gx_ref, gi_ref, *refs):
+    sent, (_, _, dk_ref, dv_ref, dk_buf, dv_buf, sems) = (refs[:3], refs[3:6]), refs[6:]
     heads = HEADS - SPLIT
     returned = heads - SENT
     leads = {}
-    for n in range(SENT):
+    for n, (from_ref, score_ref, prod_ref) in enumerate(sent):
         begin = 2 * RIM + n * STATS
-        rows = whole_of(gx_ref[begin : begin + STATS, : score_ref.shape[2]].astype(jnp.float32))
-        blocks = [jnp.exp2(score_ref[n, e * BLK : (e + 1) * BLK] * SCALE + rows[e : e + 1]) for e in range(RB)]
-        w, ds = grads_of(jnp.concatenate(blocks, axis=0), prod_ref[n], rows[RB : RB + 1], rows[RB + 1 : RB + 2])
-        leads[returned + n] = nn(ds, sent_of(x_ref, 0, n)), nn(w, sent_of(x_ref, 1, n))
+        rows = whole_of(gx_ref[begin : begin + STATS, : score_ref.shape[1]].astype(jnp.float32))
+        blocks = [jnp.exp2(score_ref[e * BLK : (e + 1) * BLK] * SCALE + rows[e : e + 1]) for e in range(RB)]
+        w, ds = grads_of(jnp.concatenate(blocks, axis=0), prod_ref[...], rows[RB : RB + 1], rows[RB + 1 : RB + 2])
+        leads[returned + n] = nn(ds, sent_of(from_ref, 0)), nn(w, sent_of(from_ref, 1))
     span = pl.ds(SPLIT * DEPTH, heads * DEPTH)
     copies = [
         pltpu.make_async_copy(buf, out.at[:, span], sems.at[slot])
@@ -383,7 +389,7 @@
 
     def rim(first, x, *more):
         heads = x.shape[1] // DEPTH
-        gx = (2 * RIM + SENT * STATS, (heads - SENT) * DEPTH) if first else x.shape
+        gx = (2 * RIM + SENT * STATS, (heads - SENT) * DEPTH) if first else (x.shape[0] + tok // PIECES, x.shape[1])
         return call(
             functools.partial(rim_kernel, first),
             "rim_grads",
@@ -407,32 +413,32 @@
     )
     gi = swap_inside(gi)
 
-    dq, pk, pv, score, products = call(
+    dq, pk, pv, *last = call(
         rest_kernel,
         "rest_grads",
         [VMEM] * 14 + [ANY],
-        [shape(tok, width), f32(tok, width), f32(tok, width), f32(SENT, RIM, tok), f32(SENT, RIM, tok)],
+        [shape(tok, width), f32(tok, width), f32(tok, width), f32(RIM, tok), f32(RIM, tok)],
         [VMEM] * 5,
         (q, k, v, g, p, prod, i, ds_i, final_a, x_a, dsx_a, final_b, x_b, dsx_b, gx_a),
     )
-    dq, dk, dv = call(
+    dq, dk, dv, *other = call(
         done_kernel,
         "done_grads",
-        [VMEM] * 5,
-        [shape(tok, width)] * 3,
-        [ANY] * 3,
-        (dq, pk, pv, gx_a, gi),
+        [VMEM] * 7,
+        [shape(tok, width)] * 3 + [f32(RIM, tok)] * 2,
+        [ANY] * 3 + [VMEM] * 2,
+        (k, v, dq, pk, pv, gx_a, gi),
         [pltpu.VMEM((tok, SPLIT * DEPTH), jnp.bfloat16)] * 2 + [pltpu.SemaphoreType.DMA((3,))],
     )
     dk, dv = call(
         add_kernel,
         "add_rims",
-        [VMEM] * 7 + [ANY] * 2,
+        [VMEM] * 10 + [ANY] * 2,
         [shape(tok, width)] * 2,
         [ANY] * 2,
-        (pk, pv, gx_b, gi, x_b, score, products, dk, dv),
+        (pk, pv, gx_b, gi, gx_a, *other, x_b, *last, dk, dv),
         [pltpu.VMEM((tok, part * DEPTH), jnp.bfloat16)] * 2 + [pltpu.SemaphoreType.DMA((2,))],
-        {7: 0, 8: 1},
+        {10: 0, 11: 1},
     )
     return dq, dk, dv
 

time: 32.8 us -> 32.3 us (0.985)
  waiting for transfers between devices: 1.6 us -> 0.95 us
    ppermute x4, waiting for transfers between devices: 0.77 us -> 0.25 us  [swap_across(): return lax.ppermute(x, 'band', pairs + [(b, a) for a, b in pairs])]
where the time goes in v6:
time: 32.3 us; the launch traced here: 31.7 us
  starting transfers between devices  20.1 us (62%)
  Pallas kernels  9.1 us (28%)
  between operations  1.53 us (5%)
  waiting for transfers between devices  0.95 us (3%)
    ppermute x4, starting transfers between devices, swap_across(): return lax.ppermute(x, 'band', pairs + [(b, a) for a, b in pairs])  16.3 us
    pallas_call x11, Pallas kernels, call(): pl.pallas_call(body, in_specs=ins, out_specs=out_specs, out_shape=outs, s...  9.1 us
    ppermute x2, starting transfers between devices, swap_inside(): lax.ppermute(x, 'band', [(at, at ^ 1) for at in range(lax.axis_size('band...  3.84 us
    ppermute x2, waiting for transfers between devices, swap_inside(): lax.ppermute(x, 'band', [(at, at ^ 1) for at in range(lax.axis_size('band...  0.7 us
  transfers between devices with their start and end apart: 6, of which 2 were waited for; matrix products, arithmetic and copies ran while one was open for 0% of the time, Pallas kernels for 21%

profile of v6, /device:TPU:454, one launch (start us, length us, event | category | flops | bytes accessed | tf_op | source)
XLA Modules:
  0.0 31.7 jit_solution(14743355031681827653)
XLA Ops:
  0.6 0.0 copy-start.3
  0.6 0.0 copy-start.2
  0.7 0.0 copy-start.1
  0.7 0.0 copy-start
  0.7 1.2 %load_bands.1 = bf16[384,512]{1,0:T(8,128)(2,1)S(1)} custom-call(bf16[256,1024]{1,0:T(8,128)(2,1)} %k_ref.11, bf16[256,1024]{1,0:T(8,128)(2,1)} %v_ref.11), custom_call_target="tpu_custom_call" | custom-call | flops 5500000256 | bytes 1000 | tf_op jit(solution)/shard_map/load_bands/pallas_call | solution.py:336
  1.9 0.0 copy-start.4
  1.9 0.0 copy-start.5
  1.9 4.8 %collective-permute-start.1 = (bf16[384,512]{1,0:T(8,128)(2,1)S(1)}, bf16[384,512]{1,0:T(8,128)(2,1)S(1)}, u32[]{:S(2)}, u32[]{:S(2)}) collective-permute-start(bf16[384,512]{1,0:T(8,128)(2,1)S(1)} %load_bands.1), channel_id=1, source_target_pairs={{1,2},{3,4},{5,6},{7,8},{9,10},{11,12},{13,14},{15,16},{17,18},{19... | collective-permute-start | bytes 1179656 | tf_op jit(solution)/shard_map/ppermute | solution.py:129
  6.7 0.0 copy-done.3
  6.7 0.0 copy-done.2
  6.7 0.0 copy-done.1
  6.7 0.0 copy-done
  6.7 0.1 pack_leads.1._
  6.8 2.9 %collective-permute-start.2 = (bf16[512,512]{1,0:T(8,128)(2,1)S(1)}, bf16[512,512]{1,0:T(8,128)(2,1)S(1)}, u32[]{:S(2)}, u32[]{:S(2)}) collective-permute-start(bf16[512,512]{1,0:T(8,128)(2,1)S(1)} %pack_leads.1._), channel_id=1, source_target_pairs={{1,2},{3,4},{5,6},{7,8},{9,10},{11,12},{13,14},{15,16},{17,18},{19... | collective-permute-start | bytes 1572872 | tf_op jit(solution)/shard_map/ppermute | solution.py:129
  9.7 0.1 pack_inside.1
  9.7 1.9 %collective-permute-start = (bf16[2,192,1024]{2,1,0:T(8,128)(2,1)S(1)}, bf16[2,192,1024]{2,1,0:T(8,128)(2,1)S(1)}, u32[]{:S(2)}, u32[]{:S(2)}) collective-permute-start(bf16[2,192,1024]{2,1,0:T(8,128)(2,1)S(1)} %pack_inside.1), channel_id=1, source_target_pairs={{0,1},{1,0},{2,3},{3,2},{4,5},{5,4},{6,7},{7,6},{8,9},{9,8},{10,11... | collective-permute-start | bytes 2359304 | tf_op jit(solution)/shard_map/ppermute | solution.py:133
  12.3 0.0 copy-done.4
  12.3 0.0 copy-done.5
  12.3 1.1 %own_stats.1 = (f32[96,256]{1,0:T(8,128)S(1)}, f32[8,8,256]{2,1,0:T(8,128)S(1)}, f32[8,256,256]{2,1,0:T(8,128)S(1)}, f32[8,256,256]{2,1,0:T(8,128)S(1)}) custom-call(s32[1,1]{1,0:T(1,128)} %bitcast.2.count_ref, s32[1,8]{1,0:T(1,128)S(1)} %bitcast.3, s32[8,14]{1,0:T(8,128)S(1)} %copy-done.4, bf16[256,1024]{1,0:T(8,128)(2,1)S(1)} %copy-done, ...), custom_call_target="tpu_custom_call" | custom-call | flops 1000000 | bytes 1000 | tf_op jit(solution)/shard_map/own_stats/pallas_call | solution.py:336
  13.5 0.0 collective-permute-done.1.x_ref.refs_1_
  13.5 0.5 %first_stats.1 = (f32[4,8,256]{2,1,0:T(8,128)S(1)}, f32[4,192,256]{2,1,0:T(8,128)S(1)}, f32[4,192,256]{2,1,0:T(8,128)S(1)}) custom-call(bf16[256,1024]{1,0:T(8,128)(2,1)S(1)} %copy-done, bf16[256,1024]{1,0:T(8,128)(2,1)S(1)} %copy-done.1, bf16[384,512]{1,0:T(8,128)(2,1)S(1)} %collective-permute-done.1.x_ref.refs_1_, f32[96,256]{1,0:T(8,128)S(1)} %get-tuple-element.36.table_ref), custom_call_target="tpu_custom_call" | custom-call | flops 11000000512 | bytes 1000 | tf_op jit(solution)/shard_map/first_stats/pallas_call | solution.py:336
  14.0 0.0 collective-permute-done.i_ref
  14.0 0.9 %rim_grads.2 = (bf16[512,512]{1,0:T(8,128)(2,1)S(1)}, f32[4,8,256]{2,1,0:T(8,128)S(1)}, bf16[4,192,256]{2,1,0:T(8,128)(2,1)S(1)}, f32[4,192,256]{2,1,0:T(8,128)S(1)}, f32[4,192,256]{2,1,0:T(8,128)S(1)}) custom-call(bf16[256,1024]{1,0:T(8,128)(2,1)S(1)} %copy-done, bf16[256,1024]{1,0:T(8,128)(2,1)S(1)} %copy-done.1, ...), custom_call_target="tpu_custom_call" | custom-call | flops 1000000 | bytes 1000 | tf_op jit(solution)/shard_map/rim_grads/pallas_call | solution.py:336
  14.9 4.8 %collective-permute-start.3 = (bf16[512,512]{1,0:T(8,128)(2,1)S(1)}, bf16[512,512]{1,0:T(8,128)(2,1)S(1)}, u32[]{:S(2)}, u32[]{:S(2)}) collective-permute-start(bf16[512,512]{1,0:T(8,128)(2,1)S(1)} %get-tuple-element.50), channel_id=1, source_target_pairs={{1,2},{3,4},{5,6},{7,8},{9,10},{11,12},{13,14},{15,16},{17,18},{19... | collective-permute-start | bytes 1572872 | tf_op jit(solution)/shard_map/ppermute | solution.py:129
  19.7 0.0 collective-permute-done.2.x_ref.refs_4_.refs_3_
  19.7 1.2 %rim_grads.3 = (bf16[448,256]{1,0:T(8,128)(2,1)S(1)}, f32[4,8,256]{2,1,0:T(8,128)S(1)}, bf16[4,192,256]{2,1,0:T(8,128)(2,1)S(1)}, f32[4,192,256]{2,1,0:T(8,128)S(1)}, f32[4,192,256]{2,1,0:T(8,128)S(1)}) custom-call(bf16[256,1024]{1,0:T(8,128)(2,1)S(1)} %copy-done, bf16[256,1024]{1,0:T(8,128)(2,1)S(1)} %copy-done.1, ...), custom_call_target="tpu_custom_call" | custom-call | flops 1000000 | bytes 1000 | tf_op jit(solution)/shard_map/rim_grads/pallas_call | solution.py:336
  20.9 3.8 %collective-permute-start.5 = (bf16[448,256]{1,0:T(8,128)(2,1)S(1)}, bf16[448,256]{1,0:T(8,128)(2,1)S(1)}, u32[]{:S(2)}, u32[]{:S(2)}) collective-permute-start(bf16[448,256]{1,0:T(8,128)(2,1)S(1)} %get-tuple-element.56), channel_id=1, source_target_pairs={{1,2},{3,4},{5,6},{7,8},{9,10},{11,12},{13,14},{15,16},{17,18},{19... | collective-permute-start | bytes 688136 | tf_op jit(solution)/shard_map/ppermute | solution.py:129
  24.7 0.6 %inside_grads.1 = (bf16[2,192,1024]{2,1,0:T(8,128)(2,1)S(1)}, bf16[8,192,256]{2,1,0:T(8,128)(2,1)S(1)}) custom-call(bf16[256,1024]{1,0:T(8,128)(2,1)S(1)} %copy-done, bf16[256,1024]{1,0:T(8,128)(2,1)S(1)} %copy-done.1, f32[4,8,256]{2,1,0:T(8,128)S(1)} %get-tuple-element.41.refs_0_, f32[4,192,256]{2,1,0:T(8,128)S(1)} %get-tuple-element.42.refs_1_, ...), custom_call_target="tpu_custom_call" | custom-call | flops 1000000 | bytes 1000 | tf_op jit(solution)/shard_map/inside_grads/pallas_call | solution.py:336
  25.3 1.9 %collective-permute-start.4 = (bf16[2,192,1024]{2,1,0:T(8,128)(2,1)S(1)}, bf16[2,192,1024]{2,1,0:T(8,128)(2,1)S(1)}, u32[]{:S(2)}, u32[]{:S(2)}) collective-permute-start(bf16[2,192,1024]{2,1,0:T(8,128)(2,1)S(1)} %get-tuple-element.54), channel_id=1, source_target_pairs={{0,1},{1,0},{2,3},{3,2},{4,5},{5,4},{6,7},{7,6},{8,9},{9,8},{10,11... | collective-permute-start | bytes 2359304 | tf_op jit(solution)/shard_map/ppermute | solution.py:133
  27.3 0.2 collective-permute-done.3.refs_6_.gx_ref.refs_0_
  27.5 1.3 %rest_grads.1 = (bf16[256,1024]{1,0:T(8,128)(2,1)S(1)}, f32[256,1024]{1,0:T(8,128)S(1)}, f32[256,1024]{1,0:T(8,128)S(1)}, f32[192,256]{1,0:T(8,128)S(1)}, f32[192,256]{1,0:T(8,128)S(1)}) custom-call(bf16[256,1024]{1,0:T(8,128)(2,1)S(1)} %copy-done, bf16[256,1024]{1,0:T(8,128)(2,1)S(1)} %copy-done.2, bf16[256,1024]{1,0:T(8,128)(2,1)S(1)} %copy-done.3, ...), custom_call_target="tpu_custom_call" | custom-call | flops 11000000512 | bytes 1000 | tf_op jit(solution)/shard_map/rest_grads/pallas_call | solution.py:336
  28.8 0.7 %collective-permute-done.4.gi_ref = bf16[2,192,1024]{2,1,0:T(8,128)(2,1)S(1)} collective-permute-done((bf16[2,192,1024]{2,1,0:T(8,128)(2,1)S(1)}, bf16[2,192,1024]{2,1,0:T(8,128)(2,1)S(1)}, u32[]{:S(2)}, u32[]{:S(2)}) %collective-permute-start.4) | collective-permute-done | bytes 786464 | tf_op jit(solution)/shard_map/ppermute | solution.py:133
  29.5 1.1 %done_grads.1 = (bf16[256,1024]{1,0:T(8,128)(2,1)}, bf16[256,1024]{1,0:T(8,128)(2,1)}, bf16[256,1024]{1,0:T(8,128)(2,1)}, f32[192,256]{1,0:T(8,128)S(1)}, f32[192,256]{1,0:T(8,128)S(1)}) custom-call(bf16[256,1024]{1,0:T(8,128)(2,1)S(1)} %copy-done.2, bf16[256,1024]{1,0:T(8,128)(2,1)S(1)} %copy-done.3, bf16[256,1024]{1,0:T(8,128)(2,1)S(1)} %get-tuple-element.51.dq_in, ...), custom_call_target="tpu_custom_call" | custom-call | flops 11000000512 | bytes 1000 | tf_op jit(solution)/shard_map/done_grads/pallas_call | solution.py:336
  30.6 0.0 collective-permute-done.5.gx_ref
  30.6 1.1 %add_rims.1 = (bf16[256,1024]{1,0:T(8,128)(2,1)}, bf16[256,1024]{1,0:T(8,128)(2,1)}) custom-call(f32[256,1024]{1,0:T(8,128)S(1)} %get-tuple-element.52.pk_ref, f32[256,1024]{1,0:T(8,128)S(1)} %get-tuple-element.53.pv_ref, bf16[448,256]{1,0:T(8,128)(2,1)S(1)} %collective-permute-done.5.gx_ref, ...), custom_call_target="tpu_custom_call", output_to_operand_aliasing={{0}: (10, {}), {1}: (11, {})} | custom-call | flops 1000000 | bytes 1000 | tf_op jit(solution)/shard_map/add_rims/pallas_call | solution.py:336
Async XLA Ops:
  0.6 6.1 %copy-start.3 = (bf16[256,1024]{1,0:T(8,128)(2,1)S(1)}, bf16[256,1024]{1,0:T(8,128)(2,1)}, u32[]{:S(2)}) copy-start(bf16[256,1024]{1,0:T(8,128)(2,1)} %v_ref.11) | copy-start | bytes 1572868
  0.6 6.1 %copy-start.2 = (bf16[256,1024]{1,0:T(8,128)(2,1)S(1)}, bf16[256,1024]{1,0:T(8,128)(2,1)}, u32[]{:S(2)}) copy-start(bf16[256,1024]{1,0:T(8,128)(2,1)} %k_ref.11) | copy-start | bytes 1572868
  0.7 6.1 %copy-start.1 = (bf16[256,1024]{1,0:T(8,128)(2,1)S(1)}, bf16[256,1024]{1,0:T(8,128)(2,1)}, u32[]{:S(2)}) copy-start(bf16[256,1024]{1,0:T(8,128)(2,1)} %g_ref.13) | copy-start | bytes 1572868
  0.7 6.1 %copy-start = (bf16[256,1024]{1,0:T(8,128)(2,1)S(1)}, bf16[256,1024]{1,0:T(8,128)(2,1)}, u32[]{:S(2)}) copy-start(bf16[256,1024]{1,0:T(8,128)(2,1)} %q_ref.13) | copy-start | bytes 1572868
  1.9 10.5 %copy-start.4 = (s32[8,14]{1,0:T(8,128)S(1)}, s32[8,14]{1,0:T(8,128)}, u32[]{:S(2)}) copy-start(s32[8,14]{1,0:T(8,128)} %lists_ref.1) | copy-start | bytes 1348
  1.9 10.5 %copy-start.5 = (s32[8]{0:T(128)S(1)}, s32[8]{0:T(128)}, u32[]{:S(2)}) copy-start(s32[8]{0:T(128)} %param.13) | copy-start | bytes 100
  1.9 11.6 %collective-permute-start.1 = (bf16[384,512]{1,0:T(8,128)(2,1)S(1)}, bf16[384,512]{1,0:T(8,128)(2,1)S(1)}, u32[]{:S(2)}, u32[]{:S(2)}) collective-permute-start(bf16[384,512]{1,0:T(8,128)(2,1)S(1)} %load_bands.1), channel_id=1, source_target_pairs={{1,2},{3,4},{5,6},{7,8},{9,10},{11,12},{13,14},{15,16},{17,18},{19... | collective-permute-start | bytes 1179656 | tf_op jit(solution)/shard_map/ppermute | solution.py:129
  6.8 12.9 %collective-permute-start.2 = (bf16[512,512]{1,0:T(8,128)(2,1)S(1)}, bf16[512,512]{1,0:T(8,128)(2,1)S(1)}, u32[]{:S(2)}, u32[]{:S(2)}) collective-permute-start(bf16[512,512]{1,0:T(8,128)(2,1)S(1)} %pack_leads.1._), channel_id=1, source_target_pairs={{1,2},{3,4},{5,6},{7,8},{9,10},{11,12},{13,14},{15,16},{17,18},{19... | collective-permute-start | bytes 1572872 | tf_op jit(solution)/shard_map/ppermute | solution.py:129
  9.7 4.2 %collective-permute-start = (bf16[2,192,1024]{2,1,0:T(8,128)(2,1)S(1)}, bf16[2,192,1024]{2,1,0:T(8,128)(2,1)S(1)}, u32[]{:S(2)}, u32[]{:S(2)}) collective-permute-start(bf16[2,192,1024]{2,1,0:T(8,128)(2,1)S(1)} %pack_inside.1), channel_id=1, source_target_pairs={{0,1},{1,0},{2,3},{3,2},{4,5},{5,4},{6,7},{7,6},{8,9},{9,8},{10,11... | collective-permute-start | bytes 2359304 | tf_op jit(solution)/shard_map/ppermute | solution.py:133
  14.9 12.6 %collective-permute-start.3 = (bf16[512,512]{1,0:T(8,128)(2,1)S(1)}, bf16[512,512]{1,0:T(8,128)(2,1)S(1)}, u32[]{:S(2)}, u32[]{:S(2)}) collective-permute-start(bf16[512,512]{1,0:T(8,128)(2,1)S(1)} %get-tuple-element.50), channel_id=1, source_target_pairs={{1,2},{3,4},{5,6},{7,8},{9,10},{11,12},{13,14},{15,16},{17,18},{19... | collective-permute-start | bytes 1572872 | tf_op jit(solution)/shard_map/ppermute | solution.py:129
  20.9 9.7 %collective-permute-start.5 = (bf16[448,256]{1,0:T(8,128)(2,1)S(1)}, bf16[448,256]{1,0:T(8,128)(2,1)S(1)}, u32[]{:S(2)}, u32[]{:S(2)}) collective-permute-start(bf16[448,256]{1,0:T(8,128)(2,1)S(1)} %get-tuple-element.56), channel_id=1, source_target_pairs={{1,2},{3,4},{5,6},{7,8},{9,10},{11,12},{13,14},{15,16},{17,18},{19... | collective-permute-start | bytes 688136 | tf_op jit(solution)/shard_map/ppermute | solution.py:129
  25.3 4.2 %collective-permute-start.4 = (bf16[2,192,1024]{2,1,0:T(8,128)(2,1)S(1)}, bf16[2,192,1024]{2,1,0:T(8,128)(2,1)S(1)}, u32[]{:S(2)}, u32[]{:S(2)}) collective-permute-start(bf16[2,192,1024]{2,1,0:T(8,128)(2,1)S(1)} %get-tuple-element.54), channel_id=1, source_target_pairs={{0,1},{1,0},{2,3},{3,2},{4,5},{5,4},{6,7},{7,6},{8,9},{9,8},{10,11... | collective-permute-start | bytes 2359304 | tf_op jit(solution)/shard_map/ppermute | solution.py:133

commit v7 on v6

--- a/solution.py
+++ b/solution.py
@@ -32,7 +32,7 @@
     "inside_grads": 1,
     "rest_grads": 11000,
     "done_grads": 11000,
-    "add_rims": 1,
+    "final_sums": 1,
 }
 
 
@@ -257,10 +257,11 @@
 
 
 def rest_kernel(q_ref, k_ref, v_ref, g_ref, p_ref, prod_ref, i_ref, dsi_ref, *refs):
-    parts, (_, dq_ref, pk_ref, pv_ref, score_ref, products_ref) = (refs[:3], refs[3:6]), refs[6:]
+    parts, (_, dq_ref, pk_ref, pv_ref, score_ref, products_ref, dq_buf, sems) = (refs[:3], refs[3:6]), refs[6:]
     x_ref = parts[1][1]
     score_ref[...] = nt(k_ref[:RIM, cols(HEADS - 1)], sent_of(x_ref, 0))
     products_ref[...] = nt(v_ref[:RIM, cols(HEADS - 1)], sent_of(x_ref, 1))
+    copies = []
     for h in range(HEADS):
         at = h if h < SPLIT else h - SPLIT
         final_ref, x_ref, dsx_ref = parts[0] if h < SPLIT else parts[1]
@@ -270,7 +271,13 @@
         pv_ref[:, cols(h)] = nn(w, g)
         frame_k = jnp.concatenate([k, x_ref[:RIM, cols(at)], i_ref[0, :, cols(h)]], axis=0)
         dq = tn(frame_k, jnp.concatenate([ds, dsx_ref[at], dsi_ref[h]], axis=0))
-        dq_ref[:, cols(h)] = dq.T.astype(jnp.bfloat16)
+        dq_buf[:, cols(h)] = dq.T.astype(jnp.bfloat16)
+        if at == SPLIT - 1:
+            span = (slice(None), pl.ds((h + 1 - SPLIT) * DEPTH, SPLIT * DEPTH))
+            copies.append(pltpu.make_async_copy(dq_buf.at[span], dq_ref.at[span], sems.at[len(copies)]))
+            copies[-1].start()
+    for copy in copies:
+        copy.wait()
 
 
 def summed(own_ref, lead, gi_ref, slot, h):
@@ -278,30 +285,28 @@
     return jnp.concatenate([lead, own_ref[RIM:, cols(h)]], axis=0).astype(jnp.bfloat16)
 
 
-def done_kernel(
-    k_ref, v_ref, dq_in, pk_ref, pv_ref, gx_ref, gi_ref, dq_ref, dk_ref, dv_ref, score_ref, products_ref, dk_buf, dv_buf, sems
-):
-    span = pl.ds(0, dk_buf.shape[1])
-    copies = [
-        pltpu.make_async_copy(dq_in, dq_ref, sems.at[0]),
-        pltpu.make_async_copy(dk_buf, dk_ref.at[:, span], sems.at[1]),
-        pltpu.make_async_copy(dv_buf, dv_ref.at[:, span], sems.at[2]),
-    ]
-    copies[0].start()
-    for slot, (own, buf) in enumerate(((pk_ref, dk_buf), (pv_ref, dv_buf))):
+def done_kernel(k_ref, v_ref, pk_ref, pv_ref, gx_ref, gi_ref, dk_ref, dv_ref, score_ref, products_ref):
+    for slot, (own, out) in enumerate(((pk_ref, dk_ref), (pv_ref, dv_ref))):
         for h in range(SPLIT):
             lead = gx_ref[slot * RIM : (slot + 1) * RIM, cols(h)].astype(jnp.float32)
-            buf[:, cols(h)] = summed(own, lead, gi_ref, slot, h)
-        copies[1 + slot].start()
+            out[:, cols(h)] = summed(own, lead, gi_ref, slot, h)
     score_ref[...] = nt(k_ref[:RIM, cols(HEADS - SENT)], sent_of(gx_ref, 0))
     products_ref[...] = nt(v_ref[:RIM, cols(HEADS - SENT)], sent_of(gx_ref, 1))
-    for copy in copies:
-        copy.wait()
-
-
-def add_kernel(pk_ref, pv_ref, gx_ref, gi_ref, *refs):
-    sent, (_, _, dk_ref, dv_ref, dk_buf, dv_buf, sems) = (refs[:3], refs[3:6]), refs[6:]
+
+
+def final_kernel(dk_in, dv_in, pk_ref, pv_ref, gx_ref, gi_ref, *refs):
+    sent, (dk_ref, dv_ref, dk_buf, dv_buf, sems) = (refs[:3], refs[3:6]), refs[6:]
     heads = HEADS - SPLIT
+    early = pl.ds(0, SPLIT * DEPTH)
+    late = pl.ds(SPLIT * DEPTH, heads * DEPTH)
+    copies = [
+        pltpu.make_async_copy(dk_in, dk_ref.at[:, early], sems.at[0]),
+        pltpu.make_async_copy(dv_in, dv_ref.at[:, early], sems.at[1]),
+        pltpu.make_async_copy(dk_buf, dk_ref.at[:, late], sems.at[2]),
+        pltpu.make_async_copy(dv_buf, dv_ref.at[:, late], sems.at[3]),
+    ]
+    for copy in copies[:2]:
+        copy.start()
     returned = heads - SENT
     leads = {}
     for n, (from_ref, score_ref, prod_ref) in enumerate(sent):
@@ -310,11 +315,6 @@
         blocks = [jnp.exp2(score_ref[e * BLK : (e + 1) * BLK] * SCALE + rows[e : e + 1]) for e in range(RB)]
         w, ds = grads_of(jnp.concatenate(blocks, axis=0), prod_ref[...], rows[RB : RB + 1], rows[RB + 1 : RB + 2])
         leads[returned + n] = nn(ds, sent_of(from_ref, 0)), nn(w, sent_of(from_ref, 1))
-    span = pl.ds(SPLIT * DEPTH, heads * DEPTH)
-    copies = [
-        pltpu.make_async_copy(buf, out.at[:, span], sems.at[slot])
-        for slot, (buf, out) in enumerate(((dk_buf, dk_ref), (dv_buf, dv_ref)))
-    ]
     for slot, (own, buf) in enumerate(((pk_ref, dk_buf), (pv_ref, dv_buf))):
         for at in range(heads):
             if at in leads:
@@ -322,7 +322,7 @@
             else:
                 lead = gx_ref[slot * RIM : (slot + 1) * RIM, cols(at)].astype(jnp.float32)
             buf[:, cols(at)] = summed(own, lead, gi_ref, slot, SPLIT + at)
-        copies[slot].start()
+        copies[2 + slot].start()
     for copy in copies:
         copy.wait()
 
@@ -418,27 +418,26 @@
         "rest_grads",
         [VMEM] * 14 + [ANY],
         [shape(tok, width), f32(tok, width), f32(tok, width), f32(RIM, tok), f32(RIM, tok)],
-        [VMEM] * 5,
+        [ANY] + [VMEM] * 4,
         (q, k, v, g, p, prod, i, ds_i, final_a, x_a, dsx_a, final_b, x_b, dsx_b, gx_a),
-    )
-    dq, dk, dv, *other = call(
+        [pltpu.VMEM((tok, width), jnp.bfloat16), pltpu.SemaphoreType.DMA((2,))],
+    )
+    dk_a, dv_a, *other = call(
         done_kernel,
         "done_grads",
-        [VMEM] * 7,
-        [shape(tok, width)] * 3 + [f32(RIM, tok)] * 2,
-        [ANY] * 3 + [VMEM] * 2,
-        (k, v, dq, pk, pv, gx_a, gi),
-        [pltpu.VMEM((tok, SPLIT * DEPTH), jnp.bfloat16)] * 2 + [pltpu.SemaphoreType.DMA((3,))],
+        [VMEM] * 6,
+        [shape(tok, SPLIT * DEPTH)] * 2 + [f32(RIM, tok)] * 2,
+        [VMEM] * 4,
+        (k, v, pk, pv, gx_a, gi),
     )
     dk, dv = call(
-        add_kernel,
-        "add_rims",
-        [VMEM] * 10 + [ANY] * 2,
+        final_kernel,
+        "final_sums",
+        [VMEM] * 12,
         [shape(tok, width)] * 2,
         [ANY] * 2,
-        (pk, pv, gx_b, gi, gx_a, *other, x_b, *last, dk, dv),
-        [pltpu.VMEM((tok, part * DEPTH), jnp.bfloat16)] * 2 + [pltpu.SemaphoreType.DMA((2,))],
-        {10: 0, 11: 1},
+        (dk_a, dv_a, pk, pv, gx_b, gi, gx_a, *other, x_b, *last),
+        [pltpu.VMEM((tok, part * DEPTH), jnp.bfloat16)] * 2 + [pltpu.SemaphoreType.DMA((4,))],
     )
     return dq, dk, dv
 

time: 32.3 us -> 31.9 us (0.988)
    ppermute x2, waiting for transfers between devices: 0.7 us -> 0.01 us  [swap_inside(): lax.ppermute(x, 'band', [(at, at ^ 1) for at in range(lax.axis_size('band...]
    ppermute x4, waiting for transfers between devices: 0.25 us -> 0.63 us  [swap_across(): return lax.ppermute(x, 'band', pairs + [(b, a) for a, b in pairs])]
  transfers between devices with their start and end apart: 6 -> 6, of which waited for: 2 -> 2; matrix products, arithmetic and copies ran while one was open for 0% -> 0% of each run, Pallas kernels for 21% -> 22%
where the time goes in v7:
time: 31.9 us; the launch traced here: 31.5 us
  starting transfers between devices  20.1 us (63%)
  Pallas kernels  9.24 us (29%)
  between operations  1.53 us (5%)
  waiting for transfers between devices  0.63 us (2%)
    ppermute x4, starting transfers between devices, swap_across(): return lax.ppermute(x, 'band', pairs + [(b, a) for a, b in pairs])  16.2 us
    pallas_call x11, Pallas kernels, call(): pl.pallas_call(body, in_specs=ins, out_specs=out_specs, out_shape=outs, s...  9.24 us
    ppermute x2, starting transfers between devices, swap_inside(): lax.ppermute(x, 'band', [(at, at ^ 1) for at in range(lax.axis_size('band...  3.84 us
  transfers between devices with their start and end apart: 6, of which 2 were waited for; matrix products, arithmetic and copies ran while one was open for 0% of the time, Pallas kernels for 22%

profile of v7, /device:TPU:454, one launch (start us, length us, event | category | flops | bytes accessed | tf_op | source)
XLA Modules:
  0.0 31.5 jit_solution(630925716736631360)
XLA Ops:
  0.6 0.0 copy-start.3
  0.6 0.0 copy-start.2
  0.7 0.0 copy-start.1
  0.7 0.0 copy-start
  0.7 1.2 %load_bands.1 = bf16[384,512]{1,0:T(8,128)(2,1)S(1)} custom-call(bf16[256,1024]{1,0:T(8,128)(2,1)} %k_ref.11, bf16[256,1024]{1,0:T(8,128)(2,1)} %v_ref.11), custom_call_target="tpu_custom_call" | custom-call | flops 5500000256 | bytes 1000 | tf_op jit(solution)/shard_map/load_bands/pallas_call | solution.py:336
  1.9 0.0 copy-start.4
  1.9 0.0 copy-start.5
  1.9 4.8 %collective-permute-start.1 = (bf16[384,512]{1,0:T(8,128)(2,1)S(1)}, bf16[384,512]{1,0:T(8,128)(2,1)S(1)}, u32[]{:S(2)}, u32[]{:S(2)}) collective-permute-start(bf16[384,512]{1,0:T(8,128)(2,1)S(1)} %load_bands.1), channel_id=1, source_target_pairs={{1,2},{3,4},{5,6},{7,8},{9,10},{11,12},{13,14},{15,16},{17,18},{19... | collective-permute-start | bytes 1179656 | tf_op jit(solution)/shard_map/ppermute | solution.py:129
  6.7 0.0 copy-done.3
  6.7 0.0 copy-done.2
  6.7 0.0 copy-done.1
  6.7 0.0 copy-done
  6.7 0.1 pack_leads.1._
  6.8 2.9 %collective-permute-start.2 = (bf16[512,512]{1,0:T(8,128)(2,1)S(1)}, bf16[512,512]{1,0:T(8,128)(2,1)S(1)}, u32[]{:S(2)}, u32[]{:S(2)}) collective-permute-start(bf16[512,512]{1,0:T(8,128)(2,1)S(1)} %pack_leads.1._), channel_id=1, source_target_pairs={{1,2},{3,4},{5,6},{7,8},{9,10},{11,12},{13,14},{15,16},{17,18},{19... | collective-permute-start | bytes 1572872 | tf_op jit(solution)/shard_map/ppermute | solution.py:129
  9.7 0.1 pack_inside.1
  9.7 1.9 %collective-permute-start = (bf16[2,192,1024]{2,1,0:T(8,128)(2,1)S(1)}, bf16[2,192,1024]{2,1,0:T(8,128)(2,1)S(1)}, u32[]{:S(2)}, u32[]{:S(2)}) collective-permute-start(bf16[2,192,1024]{2,1,0:T(8,128)(2,1)S(1)} %pack_inside.1), channel_id=1, source_target_pairs={{0,1},{1,0},{2,3},{3,2},{4,5},{5,4},{6,7},{7,6},{8,9},{9,8},{10,11... | collective-permute-start | bytes 2359304 | tf_op jit(solution)/shard_map/ppermute | solution.py:133
  12.3 0.0 copy-done.4
  12.3 0.0 copy-done.5
  12.3 1.1 %own_stats.1 = (f32[96,256]{1,0:T(8,128)S(1)}, f32[8,8,256]{2,1,0:T(8,128)S(1)}, f32[8,256,256]{2,1,0:T(8,128)S(1)}, f32[8,256,256]{2,1,0:T(8,128)S(1)}) custom-call(s32[1,1]{1,0:T(1,128)} %bitcast.2.count_ref, s32[1,8]{1,0:T(1,128)S(1)} %bitcast.3, s32[8,14]{1,0:T(8,128)S(1)} %copy-done.4, bf16[256,1024]{1,0:T(8,128)(2,1)S(1)} %copy-done, ...), custom_call_target="tpu_custom_call" | custom-call | flops 1000000 | bytes 1000 | tf_op jit(solution)/shard_map/own_stats/pallas_call | solution.py:336
  13.5 0.0 collective-permute-done.1.x_ref.refs_1_
  13.5 0.5 %first_stats.1 = (f32[4,8,256]{2,1,0:T(8,128)S(1)}, f32[4,192,256]{2,1,0:T(8,128)S(1)}, f32[4,192,256]{2,1,0:T(8,128)S(1)}) custom-call(bf16[256,1024]{1,0:T(8,128)(2,1)S(1)} %copy-done, bf16[256,1024]{1,0:T(8,128)(2,1)S(1)} %copy-done.1, bf16[384,512]{1,0:T(8,128)(2,1)S(1)} %collective-permute-done.1.x_ref.refs_1_, f32[96,256]{1,0:T(8,128)S(1)} %get-tuple-element.35.table_ref), custom_call_target="tpu_custom_call" | custom-call | flops 11000000512 | bytes 1000 | tf_op jit(solution)/shard_map/first_stats/pallas_call | solution.py:336
  14.0 0.0 collective-permute-done.i_ref
  14.0 0.9 %rim_grads.2 = (bf16[512,512]{1,0:T(8,128)(2,1)S(1)}, f32[4,8,256]{2,1,0:T(8,128)S(1)}, bf16[4,192,256]{2,1,0:T(8,128)(2,1)S(1)}, f32[4,192,256]{2,1,0:T(8,128)S(1)}, f32[4,192,256]{2,1,0:T(8,128)S(1)}) custom-call(bf16[256,1024]{1,0:T(8,128)(2,1)S(1)} %copy-done, bf16[256,1024]{1,0:T(8,128)(2,1)S(1)} %copy-done.1, ...), custom_call_target="tpu_custom_call" | custom-call | flops 1000000 | bytes 1000 | tf_op jit(solution)/shard_map/rim_grads/pallas_call | solution.py:336
  14.9 4.8 %collective-permute-start.3 = (bf16[512,512]{1,0:T(8,128)(2,1)S(1)}, bf16[512,512]{1,0:T(8,128)(2,1)S(1)}, u32[]{:S(2)}, u32[]{:S(2)}) collective-permute-start(bf16[512,512]{1,0:T(8,128)(2,1)S(1)} %get-tuple-element.49), channel_id=1, source_target_pairs={{1,2},{3,4},{5,6},{7,8},{9,10},{11,12},{13,14},{15,16},{17,18},{19... | collective-permute-start | bytes 1572872 | tf_op jit(solution)/shard_map/ppermute | solution.py:129
  19.7 0.0 collective-permute-done.2.x_ref.refs_4_.refs_3_
  19.7 1.2 %rim_grads.3 = (bf16[448,256]{1,0:T(8,128)(2,1)S(1)}, f32[4,8,256]{2,1,0:T(8,128)S(1)}, bf16[4,192,256]{2,1,0:T(8,128)(2,1)S(1)}, f32[4,192,256]{2,1,0:T(8,128)S(1)}, f32[4,192,256]{2,1,0:T(8,128)S(1)}) custom-call(bf16[256,1024]{1,0:T(8,128)(2,1)S(1)} %copy-done, bf16[256,1024]{1,0:T(8,128)(2,1)S(1)} %copy-done.1, ...), custom_call_target="tpu_custom_call" | custom-call | flops 1000000 | bytes 1000 | tf_op jit(solution)/shard_map/rim_grads/pallas_call | solution.py:336
  20.9 3.8 %collective-permute-start.5 = (bf16[448,256]{1,0:T(8,128)(2,1)S(1)}, bf16[448,256]{1,0:T(8,128)(2,1)S(1)}, u32[]{:S(2)}, u32[]{:S(2)}) collective-permute-start(bf16[448,256]{1,0:T(8,128)(2,1)S(1)} %get-tuple-element.56), channel_id=1, source_target_pairs={{1,2},{3,4},{5,6},{7,8},{9,10},{11,12},{13,14},{15,16},{17,18},{19... | collective-permute-start | bytes 688136 | tf_op jit(solution)/shard_map/ppermute | solution.py:129
  24.7 0.6 %inside_grads.1 = (bf16[2,192,1024]{2,1,0:T(8,128)(2,1)S(1)}, bf16[8,192,256]{2,1,0:T(8,128)(2,1)S(1)}) custom-call(bf16[256,1024]{1,0:T(8,128)(2,1)S(1)} %copy-done, bf16[256,1024]{1,0:T(8,128)(2,1)S(1)} %copy-done.1, f32[4,8,256]{2,1,0:T(8,128)S(1)} %get-tuple-element.40.refs_0_, f32[4,192,256]{2,1,0:T(8,128)S(1)} %get-tuple-element.41.refs_1_, ...), custom_call_target="tpu_custom_call" | custom-call | flops 1000000 | bytes 1000 | tf_op jit(solution)/shard_map/inside_grads/pallas_call | solution.py:336
  25.4 1.9 %collective-permute-start.4 = (bf16[2,192,1024]{2,1,0:T(8,128)(2,1)S(1)}, bf16[2,192,1024]{2,1,0:T(8,128)(2,1)S(1)}, u32[]{:S(2)}, u32[]{:S(2)}) collective-permute-start(bf16[2,192,1024]{2,1,0:T(8,128)(2,1)S(1)} %get-tuple-element.53), channel_id=1, source_target_pairs={{0,1},{1,0},{2,3},{3,2},{4,5},{5,4},{6,7},{7,6},{8,9},{9,8},{10,11... | collective-permute-start | bytes 2359304 | tf_op jit(solution)/shard_map/ppermute | solution.py:133
  27.3 0.3 collective-permute-done.3.refs_6_.gx_ref.refs_0_
  27.5 2.0 %rest_grads.1 = (bf16[256,1024]{1,0:T(8,128)(2,1)}, f32[256,1024]{1,0:T(8,128)S(1)}, f32[256,1024]{1,0:T(8,128)S(1)}, f32[192,256]{1,0:T(8,128)S(1)}, f32[192,256]{1,0:T(8,128)S(1)}) custom-call(bf16[256,1024]{1,0:T(8,128)(2,1)S(1)} %copy-done, bf16[256,1024]{1,0:T(8,128)(2,1)S(1)} %copy-done.2, bf16[256,1024]{1,0:T(8,128)(2,1)S(1)} %copy-done.3, ...), custom_call_target="tpu_custom_call" | custom-call | flops 11000000512 | bytes 1000 | tf_op jit(solution)/shard_map/rest_grads/pallas_call | solution.py:336
  29.6 0.0 collective-permute-done.4.gi_ref
  29.6 0.4 %done_grads.1 = (bf16[256,512]{1,0:T(8,128)(2,1)S(1)}, bf16[256,512]{1,0:T(8,128)(2,1)S(1)}, f32[192,256]{1,0:T(8,128)S(1)}, f32[192,256]{1,0:T(8,128)S(1)}) custom-call(bf16[256,1024]{1,0:T(8,128)(2,1)S(1)} %copy-done.2, bf16[256,1024]{1,0:T(8,128)(2,1)S(1)} %copy-done.3, f32[256,1024]{1,0:T(8,128)S(1)} %get-tuple-element.51.pk_ref, ...), custom_call_target="tpu_custom_call" | custom-call | flops 11000000512 | bytes 1000 | tf_op jit(solution)/shard_map/done_grads/pallas_call | solution.py:336
  30.0 0.4 %collective-permute-done.5.gx_ref = bf16[448,256]{1,0:T(8,128)(2,1)S(1)} collective-permute-done((bf16[448,256]{1,0:T(8,128)(2,1)S(1)}, bf16[448,256]{1,0:T(8,128)(2,1)S(1)}, u32[]{:S(2)}, u32[]{:S(2)}) %collective-permute-start.5) | collective-permute-done | bytes 229408 | tf_op jit(solution)/shard_map/ppermute | solution.py:129
  30.4 1.1 %final_sums.1 = (bf16[256,1024]{1,0:T(8,128)(2,1)}, bf16[256,1024]{1,0:T(8,128)(2,1)}) custom-call(bf16[256,512]{1,0:T(8,128)(2,1)S(1)} %get-tuple-element.54.dk_in, bf16[256,512]{1,0:T(8,128)(2,1)S(1)} %get-tuple-element.55.dv_in, f32[256,1024]{1,0:T(8,128)S(1)} %get-tuple-element.51.pk_ref, f32[256,1024]{1,0:T(8,128)S(1)} %get-tuple-element.52.pv_ref, ...), custom_call_target="tpu_custom_call" | custom-call | flops 1000000 | bytes 1000 | tf_op jit(solution)/shard_map/final_sums/pallas_call | solution.py:336
Async XLA Ops:
  0.6 6.1 %copy-start.3 = (bf16[256,1024]{1,0:T(8,128)(2,1)S(1)}, bf16[256,1024]{1,0:T(8,128)(2,1)}, u32[]{:S(2)}) copy-start(bf16[256,1024]{1,0:T(8,128)(2,1)} %v_ref.11) | copy-start | bytes 1572868
  0.6 6.1 %copy-start.2 = (bf16[256,1024]{1,0:T(8,128)(2,1)S(1)}, bf16[256,1024]{1,0:T(8,128)(2,1)}, u32[]{:S(2)}) copy-start(bf16[256,1024]{1,0:T(8,128)(2,1)} %k_ref.11) | copy-start | bytes 1572868
  0.7 6.1 %copy-start.1 = (bf16[256,1024]{1,0:T(8,128)(2,1)S(1)}, bf16[256,1024]{1,0:T(8,128)(2,1)}, u32[]{:S(2)}) copy-start(bf16[256,1024]{1,0:T(8,128)(2,1)} %g_ref.13) | copy-start | bytes 1572868
  0.7 6.1 %copy-start = (bf16[256,1024]{1,0:T(8,128)(2,1)S(1)}, bf16[256,1024]{1,0:T(8,128)(2,1)}, u32[]{:S(2)}) copy-start(bf16[256,1024]{1,0:T(8,128)(2,1)} %q_ref.13) | copy-start | bytes 1572868
  1.9 10.5 %copy-start.4 = (s32[8,14]{1,0:T(8,128)S(1)}, s32[8,14]{1,0:T(8,128)}, u32[]{:S(2)}) copy-start(s32[8,14]{1,0:T(8,128)} %lists_ref.1) | copy-start | bytes 1348
  1.9 10.5 %copy-start.5 = (s32[8]{0:T(128)S(1)}, s32[8]{0:T(128)}, u32[]{:S(2)}) copy-start(s32[8]{0:T(128)} %param.13) | copy-start | bytes 100
  1.9 11.6 %collective-permute-start.1 = (bf16[384,512]{1,0:T(8,128)(2,1)S(1)}, bf16[384,512]{1,0:T(8,128)(2,1)S(1)}, u32[]{:S(2)}, u32[]{:S(2)}) collective-permute-start(bf16[384,512]{1,0:T(8,128)(2,1)S(1)} %load_bands.1), channel_id=1, source_target_pairs={{1,2},{3,4},{5,6},{7,8},{9,10},{11,12},{13,14},{15,16},{17,18},{19... | collective-permute-start | bytes 1179656 | tf_op jit(solution)/shard_map/ppermute | solution.py:129
  6.8 12.9 %collective-permute-start.2 = (bf16[512,512]{1,0:T(8,128)(2,1)S(1)}, bf16[512,512]{1,0:T(8,128)(2,1)S(1)}, u32[]{:S(2)}, u32[]{:S(2)}) collective-permute-start(bf16[512,512]{1,0:T(8,128)(2,1)S(1)} %pack_leads.1._), channel_id=1, source_target_pairs={{1,2},{3,4},{5,6},{7,8},{9,10},{11,12},{13,14},{15,16},{17,18},{19... | collective-permute-start | bytes 1572872 | tf_op jit(solution)/shard_map/ppermute | solution.py:129
  9.7 4.3 %collective-permute-start = (bf16[2,192,1024]{2,1,0:T(8,128)(2,1)S(1)}, bf16[2,192,1024]{2,1,0:T(8,128)(2,1)S(1)}, u32[]{:S(2)}, u32[]{:S(2)}) collective-permute-start(bf16[2,192,1024]{2,1,0:T(8,128)(2,1)S(1)} %pack_inside.1), channel_id=1, source_target_pairs={{0,1},{1,0},{2,3},{3,2},{4,5},{5,4},{6,7},{7,6},{8,9},{9,8},{10,11... | collective-permute-start | bytes 2359304 | tf_op jit(solution)/shard_map/ppermute | solution.py:133
  14.9 12.6 %collective-permute-start.3 = (bf16[512,512]{1,0:T(8,128)(2,1)S(1)}, bf16[512,512]{1,0:T(8,128)(2,1)S(1)}, u32[]{:S(2)}, u32[]{:S(2)}) collective-permute-start(bf16[512,512]{1,0:T(8,128)(2,1)S(1)} %get-tuple-element.49), channel_id=1, source_target_pairs={{1,2},{3,4},{5,6},{7,8},{9,10},{11,12},{13,14},{15,16},{17,18},{19... | collective-permute-start | bytes 1572872 | tf_op jit(solution)/shard_map/ppermute | solution.py:129
  20.9 9.4 %collective-permute-start.5 = (bf16[448,256]{1,0:T(8,128)(2,1)S(1)}, bf16[448,256]{1,0:T(8,128)(2,1)S(1)}, u32[]{:S(2)}, u32[]{:S(2)}) collective-permute-start(bf16[448,256]{1,0:T(8,128)(2,1)S(1)} %get-tuple-element.56), channel_id=1, source_target_pairs={{1,2},{3,4},{5,6},{7,8},{9,10},{11,12},{13,14},{15,16},{17,18},{19... | collective-permute-start | bytes 688136 | tf_op jit(solution)/shard_map/ppermute | solution.py:129
  25.4 4.2 %collective-permute-start.4 = (bf16[2,192,1024]{2,1,0:T(8,128)(2,1)S(1)}, bf16[2,192,1024]{2,1,0:T(8,128)(2,1)S(1)}, u32[]{:S(2)}, u32[]{:S(2)}) collective-permute-start(bf16[2,192,1024]{2,1,0:T(8,128)(2,1)S(1)} %get-tuple-element.53), channel_id=1, source_target_pairs={{0,1},{1,0},{2,3},{3,2},{4,5},{5,4},{6,7},{7,6},{8,9},{9,8},{10,11... | collective-permute-start | bytes 2359304 | tf_op jit(solution)/shard_map/ppermute | solution.py:133

commit v8 on v7

--- a/solution.py
+++ b/solution.py
@@ -186,7 +186,7 @@
     past = lax.broadcasted_iota(jnp.int32, (tok - RIM, tok), 0) + RIM >= count
     tail = [jnp.broadcast_to(table[at : at + 1], (BLK, tok)) for at in range(RB, tok // BLK)]
     table_ref[TABLE:] = jnp.where(past, NEG, jnp.concatenate(tail, axis=0))
-    for h in range(HEADS):
+    for h in range(SPLIT):
         q, k, v, g = (ref[:, cols(h)] for ref in (q_ref, k_ref, v_ref, g_ref))
         top, p = own_exps(nt(k, q), table_ref)
         prod = nt(v, g)
@@ -203,8 +203,11 @@
         stats_ref[h] = rows_of(sums_of(top, p, prod))
 
 
-def rim_kernel(first, q_ref, g_ref, x_ref, i_ref, table_ref, stats_ref, *refs):
-    gx_ref, final_ref, ds_ref, pi_ref, prodi_ref = refs[-5:]
+def rim_kernel(first, q_ref, g_ref, x_ref, i_ref, table_ref, *refs):
+    if first:
+        k_ref, v_ref, gx_ref, final_ref, ds_ref, pi_ref, prodi_ref, po_ref, prodo_ref = refs
+    else:
+        stats_ref, stats_x_ref, px_ref, prodx_ref, gx_ref, final_ref, ds_ref, pi_ref, prodi_ref = refs
     if not first:
         pack_head(q_ref, g_ref, HEADS - SENT, gx_ref)
     heads = range(x_ref.shape[1] // DEPTH)
@@ -221,14 +224,17 @@
             top, p = exps_of(nt(x_ref[:RIM, cols(at)], q), table_ref, 8)
             prod = nt(x_ref[RIM : 2 * RIM, cols(at)], g)
             part_x = sums_of(top, p, prod)
+            top, po = own_exps(nt(k_ref[:, cols(h)], q), table_ref)
+            prodo = nt(v_ref[:, cols(h)], g)
+            po_ref[at], prodo_ref[at] = po, prodo
+            own = sums_of(top, po, prodo)
         else:
-            stats_x_ref, px_ref, prodx_ref = refs[:3]
             part_x, p, prod = known(stats_x_ref.at[h]), px_ref[h], prodx_ref[h]
-        parts.append((part_i, part_x, p, prod))
-    for at, (part_i, part_x, p, prod) in zip(heads, parts):
+            own = known(stats_ref.at[h])
+        parts.append((own, part_i, part_x, p, prod))
+    for at, (own, part_i, part_x, p, prod) in zip(heads, parts):
         h = first + at
         q, g = q_ref[:, cols(h)], g_ref[:, cols(h)]
-        own = known(stats_ref.at[h])
         top, total, raw = merged(merged(own, part_i), part_x)
         inv = jnp.where(total > 0.0, 1.0 / jnp.where(total > 0.0, total, 1.0), 0.0)
         delta = raw * inv
@@ -256,17 +262,17 @@
         ds_ref[h] = ds
 
 
-def rest_kernel(q_ref, k_ref, v_ref, g_ref, p_ref, prod_ref, i_ref, dsi_ref, *refs):
-    parts, (_, dq_ref, pk_ref, pv_ref, score_ref, products_ref, dq_buf, sems) = (refs[:3], refs[3:6]), refs[6:]
+def rest_kernel(q_ref, k_ref, v_ref, g_ref, i_ref, dsi_ref, *refs):
+    parts, (_, dq_ref, pk_ref, pv_ref, score_ref, products_ref, dq_buf, sems) = (refs[:5], refs[5:10]), refs[10:]
     x_ref = parts[1][1]
     score_ref[...] = nt(k_ref[:RIM, cols(HEADS - 1)], sent_of(x_ref, 0))
     products_ref[...] = nt(v_ref[:RIM, cols(HEADS - 1)], sent_of(x_ref, 1))
     copies = []
     for h in range(HEADS):
         at = h if h < SPLIT else h - SPLIT
-        final_ref, x_ref, dsx_ref = parts[0] if h < SPLIT else parts[1]
+        final_ref, x_ref, dsx_ref, p_ref, prod_ref = parts[0] if h < SPLIT else parts[1]
         q, k, g = (ref[:, cols(h)] for ref in (q_ref, k_ref, g_ref))
-        w, ds = grads_of(p_ref[h], prod_ref[h], final_ref[at, 0:1], final_ref[at, 2:3])
+        w, ds = grads_of(p_ref[at], prod_ref[at], final_ref[at, 0:1], final_ref[at, 2:3])
         pk_ref[:, cols(h)] = nn(ds, q)
         pv_ref[:, cols(h)] = nn(w, g)
         frame_k = jnp.concatenate([k, x_ref[:RIM, cols(at)], i_ref[0, :, cols(h)]], axis=0)
@@ -374,7 +380,7 @@
         own_kernel,
         "own_stats",
         [VMEM] * 7,
-        [f32(TABLE + tok - RIM, tok), f32(HEADS, 8, tok), f32(HEADS, tok, tok), f32(HEADS, tok, tok)],
+        [f32(TABLE + tok - RIM, tok), f32(SPLIT, 8, tok), f32(SPLIT, tok, tok), f32(SPLIT, tok, tok)],
         [VMEM] * 4,
         (band_counts[:, None], slot_counts[None], block_lists, q, k, v, g),
     )
@@ -393,15 +399,16 @@
         return call(
             functools.partial(rim_kernel, first),
             "rim_grads",
-            [VMEM] * (6 + len(more)),
-            [shape(*gx), f32(heads, 8, tok), shape(heads, RIM, tok), f32(heads, RIM, tok), f32(heads, RIM, tok)],
-            [VMEM] * 5,
-            (q, g, x, i, table, stats) + more,
+            [VMEM] * (5 + len(more)),
+            [shape(*gx), f32(heads, 8, tok), shape(heads, RIM, tok), f32(heads, RIM, tok), f32(heads, RIM, tok)]
+            + ([f32(heads, tok, tok)] * 2 if first else []),
+            [VMEM] * (7 if first else 5),
+            (q, g, x, i, table) + more,
         )
 
-    gx_a, final_a, dsx_a, *inside_a = rim(0, x_a, stats_x, px, prodx)
+    gx_a, final_a, dsx_a, *inside_a = rim(0, x_a, stats, stats_x, px, prodx)
     gx_a = swap_across(gx_a)
-    gx_b, final_b, dsx_b, *inside_b = rim(SPLIT, x_b)
+    gx_b, final_b, dsx_b, *inside_b, p_b, prod_b = rim(SPLIT, x_b, k, v)
     gx_b = swap_across(gx_b)
     gi, ds_i = call(
         inside_kernel,
@@ -416,10 +423,10 @@
     dq, pk, pv, *last = call(
         rest_kernel,
         "rest_grads",
-        [VMEM] * 14 + [ANY],
+        [VMEM] * 16 + [ANY],
         [shape(tok, width), f32(tok, width), f32(tok, width), f32(RIM, tok), f32(RIM, tok)],
         [ANY] + [VMEM] * 4,
-        (q, k, v, g, p, prod, i, ds_i, final_a, x_a, dsx_a, final_b, x_b, dsx_b, gx_a),
+        (q, k, v, g, i, ds_i, final_a, x_a, dsx_a, p, prod, final_b, x_b, dsx_b, p_b, prod_b, gx_a),
         [pltpu.VMEM((tok, width), jnp.bfloat16), pltpu.SemaphoreType.DMA((2,))],
     )
     dk_a, dv_a, *other = call(

time: 31.9 us -> 32.4 us (1.016)
  local copies, waits for them, and re-layouts: 0.03 us -> 0.66 us
    unnamed x12, local copies, waits for them, and re-layouts: 0.03 us -> 0.66 us
  transfers between devices with their start and end apart: 6 -> 6, of which waited for: 2 -> 2; matrix products, arithmetic and copies ran while one was open for 0% -> 0% of each run, Pallas kernels for 22% -> 21%
where the time goes in v8:
time: 32.4 us; the launch traced here: 32.1 us
  starting transfers between devices  19.9 us (61%)
  Pallas kernels  9.16 us (28%)
  between operations  1.52 us (5%)
  waiting for transfers between devices  0.85 us (3%)
  local copies, waits for them, and re-layouts  0.66 us (2%)
    ppermute x4, starting transfers between devices, swap_across(): return lax.ppermute(x, 'band', pairs + [(b, a) for a, b in pairs])  16.1 us
    pallas_call x11, Pallas kernels, call(): pl.pallas_call(body, in_specs=ins, out_specs=out_specs, out_shape=outs, s...  9.16 us
    ppermute x2, starting transfers between devices, swap_inside(): lax.ppermute(x, 'band', [(at, at ^ 1) for at in range(lax.axis_size('band...  3.84 us
    unnamed x12, local copies, waits for them, and re-layouts  0.66 us
  transfers between devices with their start and end apart: 6, of which 2 were waited for; matrix products, arithmetic and copies ran while one was open for 0% of the time, Pallas kernels for 21%

profile of v8, /device:TPU:454, one launch (start us, length us, event | category | flops | bytes accessed | tf_op | source)
XLA Modules:
  0.0 32.1 jit_solution(3215993664935152648)
XLA Ops:
  0.6 0.0 copy-start.3
  0.6 0.0 copy-start.2
  0.7 0.0 copy-start.1
  0.7 0.0 copy-start
  0.7 1.2 %load_bands.1 = bf16[384,512]{1,0:T(8,128)(2,1)S(1)} custom-call(bf16[256,1024]{1,0:T(8,128)(2,1)} %k_ref.11, bf16[256,1024]{1,0:T(8,128)(2,1)} %v_ref.11), custom_call_target="tpu_custom_call" | custom-call | flops 5500000256 | bytes 1000 | tf_op jit(solution)/shard_map/load_bands/pallas_call | solution.py:342
  1.9 4.8 %collective-permute-start.1 = (bf16[384,512]{1,0:T(8,128)(2,1)S(1)}, bf16[384,512]{1,0:T(8,128)(2,1)S(1)}, u32[]{:S(2)}, u32[]{:S(2)}) collective-permute-start(bf16[384,512]{1,0:T(8,128)(2,1)S(1)} %load_bands.1), channel_id=1, source_target_pairs={{1,2},{3,4},{5,6},{7,8},{9,10},{11,12},{13,14},{15,16},{17,18},{19... | collective-permute-start | bytes 1179656 | tf_op jit(solution)/shard_map/ppermute | solution.py:129
  6.7 0.0 copy-done.3
  6.7 0.0 copy-done.2
  6.7 0.0 copy-done.1
  6.7 0.0 copy-done
  6.7 0.1 pack_leads.1._
  6.8 2.9 %collective-permute-start.2 = (bf16[512,512]{1,0:T(8,128)(2,1)S(1)}, bf16[512,512]{1,0:T(8,128)(2,1)S(1)}, u32[]{:S(2)}, u32[]{:S(2)}) collective-permute-start(bf16[512,512]{1,0:T(8,128)(2,1)S(1)} %pack_leads.1._), channel_id=1, source_target_pairs={{1,2},{3,4},{5,6},{7,8},{9,10},{11,12},{13,14},{15,16},{17,18},{19... | collective-permute-start | bytes 1572872 | tf_op jit(solution)/shard_map/ppermute | solution.py:129
  9.7 0.1 pack_inside.1
  9.7 0.0 copy-start.4
  9.7 1.9 %collective-permute-start = (bf16[2,192,1024]{2,1,0:T(8,128)(2,1)S(1)}, bf16[2,192,1024]{2,1,0:T(8,128)(2,1)S(1)}, u32[]{:S(2)}, u32[]{:S(2)}) collective-permute-start(bf16[2,192,1024]{2,1,0:T(8,128)(2,1)S(1)} %pack_inside.1), channel_id=1, source_target_pairs={{0,1},{1,0},{2,3},{3,2},{4,5},{5,4},{6,7},{7,6},{8,9},{9,8},{10,11... | collective-permute-start | bytes 2359304 | tf_op jit(solution)/shard_map/ppermute | solution.py:133
  12.3 0.0 copy-start.5
  12.3 0.0 copy-done.4
  12.3 0.6 %copy-done.5 = s32[8]{0:T(128)S(1)} copy-done((s32[8]{0:T(128)S(1)}, s32[8]{0:T(128)}, u32[]{:S(2)}) %copy-start.5) | copy-done | bytes 56
  13.0 0.7 %own_stats.1 = (f32[96,256]{1,0:T(8,128)S(1)}, f32[4,8,256]{2,1,0:T(8,128)S(1)}, f32[4,256,256]{2,1,0:T(8,128)S(1)}, f32[4,256,256]{2,1,0:T(8,128)S(1)}) custom-call(s32[1,1]{1,0:T(1,128)} %bitcast.2.count_ref, s32[1,8]{1,0:T(1,128)S(1)} %bitcast.3, s32[8,14]{1,0:T(8,128)S(1)} %copy-done.4, bf16[256,1024]{1,0:T(8,128)(2,1)S(1)} %copy-done, ...), custom_call_target="tpu_custom_call" | custom-call | flops 1000000 | bytes 1000 | tf_op jit(solution)/shard_map/own_stats/pallas_call | solution.py:342
  13.6 0.0 collective-permute-done.1.x_ref.refs_1_
  13.7 0.5 %first_stats.1 = (f32[4,8,256]{2,1,0:T(8,128)S(1)}, f32[4,192,256]{2,1,0:T(8,128)S(1)}, f32[4,192,256]{2,1,0:T(8,128)S(1)}) custom-call(bf16[256,1024]{1,0:T(8,128)(2,1)S(1)} %copy-done, bf16[256,1024]{1,0:T(8,128)(2,1)S(1)} %copy-done.1, bf16[384,512]{1,0:T(8,128)(2,1)S(1)} %collective-permute-done.1.x_ref.refs_1_, f32[96,256]{1,0:T(8,128)S(1)} %get-tuple-element.35.table_ref), custom_call_target="tpu_custom_call" | custom-call | flops 11000000512 | bytes 1000 | tf_op jit(solution)/shard_map/first_stats/pallas_call | solution.py:342
  14.2 0.0 collective-permute-done.i_ref
  14.2 0.9 %rim_grads.2 = (bf16[512,512]{1,0:T(8,128)(2,1)S(1)}, f32[4,8,256]{2,1,0:T(8,128)S(1)}, bf16[4,192,256]{2,1,0:T(8,128)(2,1)S(1)}, f32[4,192,256]{2,1,0:T(8,128)S(1)}, f32[4,192,256]{2,1,0:T(8,128)S(1)}) custom-call(bf16[256,1024]{1,0:T(8,128)(2,1)S(1)} %copy-done, bf16[256,1024]{1,0:T(8,128)(2,1)S(1)} %copy-done.1, ...), custom_call_target="tpu_custom_call" | custom-call | flops 1000000 | bytes 1000 | tf_op jit(solution)/shard_map/rim_grads/pallas_call | solution.py:342
  15.1 4.8 %collective-permute-start.3 = (bf16[512,512]{1,0:T(8,128)(2,1)S(1)}, bf16[512,512]{1,0:T(8,128)(2,1)S(1)}, u32[]{:S(2)}, u32[]{:S(2)}) collective-permute-start(bf16[512,512]{1,0:T(8,128)(2,1)S(1)} %get-tuple-element.53), channel_id=1, source_target_pairs={{1,2},{3,4},{5,6},{7,8},{9,10},{11,12},{13,14},{15,16},{17,18},{19... | collective-permute-start | bytes 1572872 | tf_op jit(solution)/shard_map/ppermute | solution.py:129
  19.9 0.0 collective-permute-done.2.x_ref.refs_6_.refs_3_
  19.9 1.6 %rim_grads.3 = (bf16[448,256]{1,0:T(8,128)(2,1)S(1)}, f32[4,8,256]{2,1,0:T(8,128)S(1)}, bf16[4,192,256]{2,1,0:T(8,128)(2,1)S(1)}, f32[4,192,256]{2,1,0:T(8,128)S...) custom-call(bf16[256,1024]{1,0:T(8,128)(2,1)S(1)} %copy-done, ...), custom_call_target="tpu_custom_call" | custom-call | flops 1000000 | bytes 1000 | tf_op jit(solution)/shard_map/rim_grads/pallas_call | solution.py:342
  21.5 3.6 %collective-permute-start.5 = (bf16[448,256]{1,0:T(8,128)(2,1)S(1)}, bf16[448,256]{1,0:T(8,128)(2,1)S(1)}, u32[]{:S(2)}, u32[]{:S(2)}) collective-permute-start(bf16[448,256]{1,0:T(8,128)(2,1)S(1)} %get-tuple-element.60), channel_id=1, source_target_pairs={{1,2},{3,4},{5,6},{7,8},{9,10},{11,12},{13,14},{15,16},{17,18},{19... | collective-permute-start | bytes 688136 | tf_op jit(solution)/shard_map/ppermute | solution.py:129
  25.1 0.6 %inside_grads.1 = (bf16[2,192,1024]{2,1,0:T(8,128)(2,1)S(1)}, bf16[8,192,256]{2,1,0:T(8,128)(2,1)S(1)}) custom-call(bf16[256,1024]{1,0:T(8,128)(2,1)S(1)} %copy-done, bf16[256,1024]{1,0:T(8,128)(2,1)S(1)} %copy-done.1, f32[4,8,256]{2,1,0:T(8,128)S(1)} %get-tuple-element.40.refs_0_, f32[4,192,256]{2,1,0:T(8,128)S(1)} %get-tuple-element.41.refs_1_, ...), custom_call_target="tpu_custom_call" | custom-call | flops 1000000 | bytes 1000 | tf_op jit(solution)/shard_map/inside_grads/pallas_call | solution.py:342
  25.8 1.9 %collective-permute-start.4 = (bf16[2,192,1024]{2,1,0:T(8,128)(2,1)S(1)}, bf16[2,192,1024]{2,1,0:T(8,128)(2,1)S(1)}, u32[]{:S(2)}, u32[]{:S(2)}) collective-permute-start(bf16[2,192,1024]{2,1,0:T(8,128)(2,1)S(1)} %get-tuple-element.57), channel_id=1, source_target_pairs={{0,1},{1,0},{2,3},{3,2},{4,5},{5,4},{6,7},{7,6},{8,9},{9,8},{10,11... | collective-permute-start | bytes 2359304 | tf_op jit(solution)/shard_map/ppermute | solution.py:133
  27.7 0.0 collective-permute-done.3.refs_10_.gx_ref.refs_0_
  27.7 2.0 %rest_grads.1 = (bf16[256,1024]{1,0:T(8,128)(2,1)}, f32[256,1024]{1,0:T(8,128)S(1)}, f32[256,1024]{1,0:T(8,128)S(1)}, f32[192,256]{1,0:T(8,128)S(1)}, f32[192,256]{1,0:T(8,128)S(1)}) custom-call(bf16[256,1024]{1,0:T(8,128)(2,1)S(1)} %copy-done, bf16[256,1024]{1,0:T(8,128)(2,1)S(1)} %copy-done.2, bf16[256,1024]{1,0:T(8,128)(2,1)S(1)} %copy-done.3, ...), custom_call_target="tpu_custom_call" | custom-call | flops 11000000512 | bytes 1000 | tf_op jit(solution)/shard_map/rest_grads/pallas_call | solution.py:342
  29.7 0.2 collective-permute-done.4.gi_ref
  29.9 0.4 %done_grads.1 = (bf16[256,512]{1,0:T(8,128)(2,1)S(1)}, bf16[256,512]{1,0:T(8,128)(2,1)S(1)}, f32[192,256]{1,0:T(8,128)S(1)}, f32[192,256]{1,0:T(8,128)S(1)}) custom-call(bf16[256,1024]{1,0:T(8,128)(2,1)S(1)} %copy-done.2, bf16[256,1024]{1,0:T(8,128)(2,1)S(1)} %copy-done.3, f32[256,1024]{1,0:T(8,128)S(1)} %get-tuple-element.55.pk_ref, ...), custom_call_target="tpu_custom_call" | custom-call | flops 11000000512 | bytes 1000 | tf_op jit(solution)/shard_map/done_grads/pallas_call | solution.py:342
  30.4 0.6 %collective-permute-done.5.gx_ref = bf16[448,256]{1,0:T(8,128)(2,1)S(1)} collective-permute-done((bf16[448,256]{1,0:T(8,128)(2,1)S(1)}, bf16[448,256]{1,0:T(8,128)(2,1)S(1)}, u32[]{:S(2)}, u32[]{:S(2)}) %collective-permute-start.5) | collective-permute-done | bytes 229408 | tf_op jit(solution)/shard_map/ppermute | solution.py:129
  31.0 1.1 %final_sums.1 = (bf16[256,1024]{1,0:T(8,128)(2,1)}, bf16[256,1024]{1,0:T(8,128)(2,1)}) custom-call(bf16[256,512]{1,0:T(8,128)(2,1)S(1)} %get-tuple-element.58.dk_in, bf16[256,512]{1,0:T(8,128)(2,1)S(1)} %get-tuple-element.59.dv_in, f32[256,1024]{1,0:T(8,128)S(1)} %get-tuple-element.55.pk_ref, f32[256,1024]{1,0:T(8,128)S(1)} %get-tuple-element.56.pv_ref, ...), custom_call_target="tpu_custom_call" | custom-call | flops 1000000 | bytes 1000 | tf_op jit(solution)/shard_map/final_sums/pallas_call | solution.py:342
Async XLA Ops:
  0.6 6.0 %copy-start.3 = (bf16[256,1024]{1,0:T(8,128)(2,1)S(1)}, bf16[256,1024]{1,0:T(8,128)(2,1)}, u32[]{:S(2)}) copy-start(bf16[256,1024]{1,0:T(8,128)(2,1)} %v_ref.11) | copy-start | bytes 1572868
  0.6 6.0 %copy-start.2 = (bf16[256,1024]{1,0:T(8,128)(2,1)S(1)}, bf16[256,1024]{1,0:T(8,128)(2,1)}, u32[]{:S(2)}) copy-start(bf16[256,1024]{1,0:T(8,128)(2,1)} %k_ref.11) | copy-start | bytes 1572868
  0.7 6.0 %copy-start.1 = (bf16[256,1024]{1,0:T(8,128)(2,1)S(1)}, bf16[256,1024]{1,0:T(8,128)(2,1)}, u32[]{:S(2)}) copy-start(bf16[256,1024]{1,0:T(8,128)(2,1)} %g_ref.13) | copy-start | bytes 1572868
  0.7 6.0 %copy-start = (bf16[256,1024]{1,0:T(8,128)(2,1)S(1)}, bf16[256,1024]{1,0:T(8,128)(2,1)}, u32[]{:S(2)}) copy-start(bf16[256,1024]{1,0:T(8,128)(2,1)} %q_ref.13) | copy-start | bytes 1572868
  1.9 11.8 %collective-permute-start.1 = (bf16[384,512]{1,0:T(8,128)(2,1)S(1)}, bf16[384,512]{1,0:T(8,128)(2,1)S(1)}, u32[]{:S(2)}, u32[]{:S(2)}) collective-permute-start(bf16[384,512]{1,0:T(8,128)(2,1)S(1)} %load_bands.1), channel_id=1, source_target_pairs={{1,2},{3,4},{5,6},{7,8},{9,10},{11,12},{13,14},{15,16},{17,18},{19... | collective-permute-start | bytes 1179656 | tf_op jit(solution)/shard_map/ppermute | solution.py:129
  6.8 13.1 %collective-permute-start.2 = (bf16[512,512]{1,0:T(8,128)(2,1)S(1)}, bf16[512,512]{1,0:T(8,128)(2,1)S(1)}, u32[]{:S(2)}, u32[]{:S(2)}) collective-permute-start(bf16[512,512]{1,0:T(8,128)(2,1)S(1)} %pack_leads.1._), channel_id=1, source_target_pairs={{1,2},{3,4},{5,6},{7,8},{9,10},{11,12},{13,14},{15,16},{17,18},{19... | collective-permute-start | bytes 1572872 | tf_op jit(solution)/shard_map/ppermute | solution.py:129
  9.7 2.6 %copy-start.4 = (s32[8,14]{1,0:T(8,128)S(1)}, s32[8,14]{1,0:T(8,128)}, u32[]{:S(2)}) copy-start(s32[8,14]{1,0:T(8,128)} %lists_ref.1) | copy-start | bytes 1348
  9.7 4.4 %collective-permute-start = (bf16[2,192,1024]{2,1,0:T(8,128)(2,1)S(1)}, bf16[2,192,1024]{2,1,0:T(8,128)(2,1)S(1)}, u32[]{:S(2)}, u32[]{:S(2)}) collective-permute-start(bf16[2,192,1024]{2,1,0:T(8,128)(2,1)S(1)} %pack_inside.1), channel_id=1, source_target_pairs={{0,1},{1,0},{2,3},{3,2},{4,5},{5,4},{6,7},{7,6},{8,9},{9,8},{10,11... | collective-permute-start | bytes 2359304 | tf_op jit(solution)/shard_map/ppermute | solution.py:133
  12.3 0.7 %copy-start.5 = (s32[8]{0:T(128)S(1)}, s32[8]{0:T(128)}, u32[]{:S(2)}) copy-start(s32[8]{0:T(128)} %param.13) | copy-start | bytes 100
  15.1 12.6 %collective-permute-start.3 = (bf16[512,512]{1,0:T(8,128)(2,1)S(1)}, bf16[512,512]{1,0:T(8,128)(2,1)S(1)}, u32[]{:S(2)}, u32[]{:S(2)}) collective-permute-start(bf16[512,512]{1,0:T(8,128)(2,1)S(1)} %get-tuple-element.53), channel_id=1, source_target_pairs={{1,2},{3,4},{5,6},{7,8},{9,10},{11,12},{13,14},{15,16},{17,18},{19... | collective-permute-start | bytes 1572872 | tf_op jit(solution)/shard_map/ppermute | solution.py:129
  21.5 9.4 %collective-permute-start.5 = (bf16[448,256]{1,0:T(8,128)(2,1)S(1)}, bf16[448,256]{1,0:T(8,128)(2,1)S(1)}, u32[]{:S(2)}, u32[]{:S(2)}) collective-permute-start(bf16[448,256]{1,0:T(8,128)(2,1)S(1)} %get-tuple-element.60), channel_id=1, source_target_pairs={{1,2},{3,4},{5,6},{7,8},{9,10},{11,12},{13,14},{15,16},{17,18},{19... | collective-permute-start | bytes 688136 | tf_op jit(solution)/shard_map/ppermute | solution.py:129
  25.8 4.2 %collective-permute-start.4 = (bf16[2,192,1024]{2,1,0:T(8,128)(2,1)S(1)}, bf16[2,192,1024]{2,1,0:T(8,128)(2,1)S(1)}, u32[]{:S(2)}, u32[]{:S(2)}) collective-permute-start(bf16[2,192,1024]{2,1,0:T(8,128)(2,1)S(1)} %get-tuple-element.57), channel_id=1, source_target_pairs={{0,1},{1,0},{2,3},{3,2},{4,5},{5,4},{6,7},{7,6},{8,9},{9,8},{10,11... | collective-permute-start | bytes 2359304 | tf_op jit(solution)/shard_map/ppermute | solution.py:133
